TPU v7x, 256 devices: a whole 4x4x8 slice. The times are simulated.
256 devices in a mesh: wall: 4 (over y), tile: 64 (over x, z, core).
Axes of the slice: x: 4, y: 4, z: 8, core: 2. Of those that a mesh axis runs over, the one named last changes fastest.
Arguments:
- adjoint: float32 [10, 32, 512, 128], P(None, 'wall', 'tile'), may hold values from -6 to 6
- source: float32 [10, 32, 512, 128], P(None, 'wall', 'tile'), may hold values from -1.8 to 1.8
- radius: float32 [32, 512, 128], P('wall', 'tile'), may hold values from 0.1 to 0.6
- frequency: float32 [32, 512, 128], P('wall', 'tile'), may hold values from 0.1 to 1
- lower_coupling: float32 [10, 10, 32, 512, 128], P(None, None, 'wall', 'tile'), may hold values from -0.04 to 1
- diag_inverse: float32 [10, 10, 32, 512, 128], P(None, None, 'wall', 'tile'), may hold values from -0.03 to 0.2
- upper_coupling: float32 [10, 10, 32, 512, 128], P(None, None, 'wall', 'tile'), may hold values from -0.04 to 1
- wall_weight: float32 [32], P('wall'), may hold values from 0.01 to 0.1
- surface_weight: float32 [16384, 10, 8], P('tile'), may hold values from -0.625 to 0.625
- patch_owner: int32 [16384, 1], P('tile'), may hold values from 0 to 63; in each aligned block of 256 rows (0 to 255, 256 to 511, ...) at most 8 rows name the same one
- patch_row: int32 [16384], P('tile'), may hold values from 0 to 63
- surface_count: int32 [64], P('tile'), may hold values from 1 to 256, 14336 in all
Outputs:
- adjoint_next: float32 [10, 32, 512, 128], P(None, 'wall', 'tile')
- patch_load: float32 [4096, 128], P('tile')
Inputs may be any that keep to these rules, and one draw needn't show every extreme that they name: `patch_owner`: among the 256 blocks of one tile no owner is named more than 8 times. The live blocks of a tile are its first surface_count blocks.
All inputs are finite; a program needn't handle non-finite values.
Results may differ from a plain program's by a relative error of at most 0.0001.
Values sent between devices are 32-bit elements; how exact they have to be, the bound alone decides.
No kernel may reach another device: no remote copies, remote signals or barrier semaphores. Data moves between devices by JAX's collectives and lax.ppermute only.
A program may use at most 128 MiB of HBM per device.

v0:
```python
import jax
import jax.numpy as jnp
from jax import lax
from jax.sharding import PartitionSpec as P

PATCH_DEV = 64


highest = lax.Precision.HIGHEST


def shifted(block, axis, distance):
    devices = range(lax.axis_size(axis))
    route = [(i - distance, i) for i in devices if i - distance in devices]
    return lax.ppermute(block, axis, route)


def extended(cells, sides, width):
    for axis, dim in sides:
        count = lax.axis_size(axis)
        ends = count - 1
        head = lax.slice_in_dim(cells, 0, width, axis=dim)
        tail = lax.slice_in_dim(cells, cells.shape[dim] - width, cells.shape[dim], axis=dim)
        cells = jnp.concatenate(
            [
                lax.ppermute(tail, axis, [(i, (i + 1) % count) for i in range(ends)]),
                cells,
                lax.ppermute(head, axis, [((i + 1) % count, i) for i in range(ends)]),
            ],
            axis=dim,
        )
    return cells


def span_shift(values, shifter):
    return jnp.dot(values.reshape(-1, values.shape[-1]), shifter, precision=highest).reshape(
        values.shape
    )


def flux_apply(stacked_pad, radius, adjoint, frequency):
    chord_cells = adjoint.shape[2]
    neighbours = stacked_pad[:-1]
    radii = stacked_pad[-1]
    applied = jnp.zeros_like(adjoint)
    for offset, weight in ((-2, -0.125), (-1, 0.5), (1, 0.5), (2, -0.125)):
        first_cell = 2 + offset
        applied = (
            applied
            + weight
            * 0.5
            * (radius + radii[:, first_cell : first_cell + chord_cells])
            * neighbours[:, :, first_cell : first_cell + chord_cells]
        )
    span_cells = adjoint.shape[3]
    source_index = jnp.arange(span_cells)[:, None]
    target_index = jnp.arange(span_cells)[None, :]
    for step_offset in (-1, 1):
        shifter = (source_index == target_index + step_offset).astype(jnp.float32)
        span_state = span_shift(adjoint, shifter)
        span_radius = span_shift(radius, shifter)
        applied = applied + 0.5 * 0.5 * (radius + span_radius) * span_state
    half_count = adjoint.shape[0] // 2
    turned = jnp.concatenate([-adjoint[half_count:], adjoint[:half_count]], axis=0)
    return applied + frequency * turned


def block_times_block(left_block, right_block):
    running = None
    for column_index in range(left_block.shape[1]):
        product_term = left_block[:, column_index][:, None] * right_block[column_index][None]
        running = product_term if running is None else running + product_term
    return running


def block_times_vector(left_block, right_vector):
    running = None
    for column_index in range(left_block.shape[1]):
        product_term = left_block[:, column_index] * right_vector[column_index][None]
        running = product_term if running is None else running + product_term
    return running


def carry_up(seg_map, seg_val):
    incoming = jnp.zeros_like(seg_val)
    for rounds in range(lax.axis_size("wall") - 1):
        outgoing = block_times_vector(seg_map, incoming) + seg_val
        incoming = shifted(outgoing, "wall", 1)
    return incoming


def carry_down(seg_map, seg_val):
    incoming = jnp.zeros_like(seg_val)
    for rounds in range(lax.axis_size("wall") - 1):
        outgoing = block_times_vector(seg_map, incoming) + seg_val
        incoming = shifted(outgoing, "wall", -1)
    return incoming


def deliver(send_rows, send_tag):
    got_rows, got_tag = (
        lax.all_to_all(send_rows, "tile", split_axis=0, concat_axis=0, tiled=True),
        lax.all_to_all(send_tag, "tile", split_axis=0, concat_axis=0, tiled=True),
    )
    flat_tag = got_tag.reshape(-1)
    targets = (jnp.arange(PATCH_DEV) + 1).astype(jnp.float32)
    picker = (flat_tag[None, :] == targets[:, None]).astype(jnp.float32)
    return jnp.dot(picker, got_rows.reshape(-1, got_rows.shape[-1]), precision=highest)


def on_device(
    adjoint,
    source,
    radius,
    frequency,
    lower_coupling,
    diag_inverse,
    upper_coupling,
    wall_weight,
    surface_weight,
    patch_owner,
    patch_row,
    surface_count,
):
    stacked = jnp.concatenate([adjoint, radius[None]], axis=0)
    stacked_pad = extended(stacked, (("tile", 2),), 2)
    residual = source - flux_apply(stacked_pad, radius, adjoint, frequency)
    depth = residual.shape[1]
    seg_map = lower_coupling[:, :, 0]
    seg_val = residual[:, 0]
    for level in range(1, depth):
        step_block = lower_coupling[:, :, level]
        seg_map = block_times_block(step_block, seg_map)
        seg_val = block_times_vector(step_block, seg_val) + residual[:, level]
    incoming = carry_up(seg_map, seg_val)
    scaled_rows = []
    running = incoming
    for level in range(depth):
        running = block_times_vector(lower_coupling[:, :, level], running) + residual[:, level]
        scaled_rows.append(block_times_vector(diag_inverse[:, :, level], running))
    back_map = -upper_coupling[:, :, depth - 1]
    back_val = scaled_rows[depth - 1]
    for level in range(depth - 2, -1, -1):
        step_block = -upper_coupling[:, :, level]
        back_map = block_times_block(step_block, back_map)
        back_val = block_times_vector(step_block, back_val) + scaled_rows[level]
    incoming_back = carry_down(back_map, back_val)
    next_rows = [None] * depth
    running = incoming_back
    for level in range(depth - 1, -1, -1):
        running = scaled_rows[level] - block_times_vector(upper_coupling[:, :, level], running)
        next_rows[level] = running
    adjoint_next = jnp.stack(next_rows, axis=1)
    profile = jnp.einsum("ikcs,k->ics", adjoint_next, wall_weight, precision=highest)
    sens_rows = jnp.einsum("bic,ics->bs", surface_weight, profile, precision=highest)
    block_count = sens_rows.shape[0]
    live_mask = (jnp.arange(block_count) < surface_count[0]).astype(jnp.float32)
    tile_count = lax.axis_size("tile")
    capacity = max(4, 2 * block_count // tile_count)
    owner_ids = patch_owner[:, 0]
    owner_hits = (owner_ids[:, None] == jnp.arange(tile_count)[None, :]).astype(jnp.int32)
    slot_index = jnp.sum(jnp.cumsum(owner_hits, axis=0) * owner_hits, axis=1) - 1
    position = owner_ids * capacity + slot_index
    placement = (jnp.arange(tile_count * capacity)[:, None] == position[None, :]).astype(
        jnp.float32
    )
    send_rows = jnp.dot(placement, sens_rows * live_mask[:, None], precision=highest).reshape(
        tile_count, capacity, -1
    )
    send_tag = jnp.dot(
        placement, (patch_row + 1).astype(jnp.float32) * live_mask, precision=highest
    ).reshape(tile_count, capacity)
    patch_sums = lax.psum(deliver(send_rows, send_tag), "wall")
    return (adjoint_next, patch_sums)


def solution(mesh):
    in_specs = (
        P(None, "wall", "tile", None),
        P(None, "wall", "tile", None),
        P("wall", "tile", None),
        P("wall", "tile", None),
        P(None, None, "wall", "tile", None),
        P(None, None, "wall", "tile", None),
        P(None, None, "wall", "tile", None),
        P("wall"),
        P("tile", None, None),
        P("tile", None),
        P("tile"),
        P("tile"),
    )
    out_specs = (P(None, "wall", "tile", None), P("tile", None))
    return jax.shard_map(
        on_device, mesh=mesh, in_specs=in_specs, out_specs=out_specs, check_vma=False
    )
```

profile of v0, /device:TPU:6, one launch (start us, length us, event | category | flops | bytes accessed | tf_op | source)
XLA Modules:
  0.0 143.5 jit_solution(17548576484815693216)
XLA Ops:
  0.6 1.9 %pad_maximum_fusion.5 = (f32[11,8,2,128]{3,2,1,0:T(2,128)}, f32[11,8,2,128]{3,2,1,0:T(2,128)}) fusion(f32[1,8,8,128]{3,2,1,0:T(8,128)} %bitcast.3093, f32[10,8,8,128]{3,2,1,0:T(8,128)} %param.12), kind=kLoop, calls=%fused_computation.76 | loop fusion | flops 45056 | bytes 540672 | tf_op jit(solution)/shard_map/slice | solution.py:23
  2.5 1.9 %collective-permute-start = (f32[11,8,2,128]{3,2,1,0:T(2,128)}, f32[11,8,2,128]{3,2,1,0:T(2,128)}, u32[]{:S(2)}, u32[]{:S(2)}) collective-permute-start(f32[11,8,2,128]{3,2,1,0:T(2,128)} %get-tuple-element.326), channel_id=1, source_target_pairs={{0,1},{1,2},{2,3},{3,4},{4,5},{5,6},{6,7},{7,8},{8,9},{9,10},{10,1... | collective-permute-start | bytes 270344 | tf_op jit(solution)/shard_map/ppermute | solution.py:26
  4.4 7.5 %collective-permute-start.1 = (f32[11,8,2,128]{3,2,1,0:T(2,128)}, f32[11,8,2,128]{3,2,1,0:T(2,128)}, u32[]{:S(2)}, u32[]{:S(2)}) collective-permute-start(f32[11,8,2,128]{3,2,1,0:T(2,128)} %get-tuple-element.327), channel_id=1, source_target_pairs={{1,0},{2,1},{3,2},{4,3},{5,4},{6,5},{7,6},{8,7},{9,8},{10,9},{11,1... | collective-permute-start | bytes 270344 | tf_op jit(solution)/shard_map/ppermute | solution.py:28
  17.3 9.7 %all-to-all-start = ((f32[64,1,8]{2,1,0:T(1,128)}), f32[64,1,8]{2,1,0:T(1,128)}, u32[]{:S(2)}, u32[]{:S(2)}) async-start(f32[64,1,8]{2,1,0:T(1,128)} %bitcast.860), calls=%async_computation | async-start | bytes 65536 | tf_op jit(solution)/shard_map/all_to_all | solution.py:103
  27.1 1.7 %slice_negate_fusion = (f32[5,8,8,128]{3,2,1,0:T(8,128)S(1)}, f32[5,8,8,128]{3,2,1,0:T(8,128)}) fusion(f32[10,8,8,128]{3,2,1,0:T(8,128)} %param.12), kind=kLoop, calls=%fused_computation.73 | loop fusion | flops 40960 | bytes 655360 | tf_op jit(solution)/shard_map/neg | solution.py:64
  28.8 3.1 %fusion.235 = (f32[10,10,1,8,128]{4,3,2,1,0:T(8,128)S(1)}, f32[10,10,1,8,128]{4,3,2,1,0:T(8,128)S(1)}, f32[10,10,1,8,128]{4,3,2,1,0:T(8,128)S(1)}, f32[10,10,1,8...) fusion(f32[10,10,8,8,128]{4,3,2,1,0:T(8,128)} %param.16), kind=kLoop, calls=%fused_computation.1162 | loop fusion | bytes 6553600 | tf_op jit(solution)/shard_map/slice | solution.py:132
  33.2 1.1 copy_bitcast_fusion
  38.6 1.1 convolution_bitcast_fusion
  39.7 1.1 convolution_bitcast_fusion.1
  43.4 1.3 copy-done.38
  48.7 1.0 multiply_add_fusion.1
  49.8 1.1 multiply_add_fusion.7
  51.0 1.9 %copy.99 = f32[640,128]{1,0:T(8,128)} copy(f32[640,128]{0,1:T(8,128)} %convolution_bitcast_fusion.1) | data formatting | bytes 655360 | tf_op jit(solution)/shard_map/dot_general | solution.py:36
  52.9 1.9 %copy.100 = f32[640,128]{1,0:T(8,128)} copy(f32[640,128]{0,1:T(8,128)} %convolution_bitcast_fusion) | data formatting | bytes 655360 | tf_op jit(solution)/shard_map/dot_general | solution.py:36
  55.6 1.9 %fusion.11 = f32[10,8,8,128]{3,2,1,0:T(8,128)S(1)} fusion(f32[10,8,8,128]{3,2,1,0:T(8,128)} %param.13, f32[11,8,2,128]{3,2,1,0:T(2,128)} %collective-permute-done.1, f32[1,8,8,128]{3,2,1,0:T(8,128)S(1)} %bitcast.3095, f32[10,8,8,128]{3,2,1,0:T(8,128)S(1)} %copy-done.1, f32[11,8,2,128]{3,2,1,0:T(2,128)} %collective-permute-done, ...), kind=kLoop, calls=%fused_computation.57 | loop fusion | flops 1884160 | bytes 2408448 | tf_op jit(solution)/shard_map/sub | solution.py:127
  63.4 3.5 %collective-permute-start.2 = (f32[10,8,128]{2,1,0:T(8,128)S(1)}, f32[10,8,128]{2,1,0:T(8,128)S(1)}, u32[]{:S(2)}, u32[]{:S(2)}) collective-permute-start(f32[10,8,128]{2,1,0:T(8,128)S(1)} %get-tuple-element.20), channel_id=1, source_target_pairs={{0,64},{64,128},{128,192},{1,65},{65,129},{129,193},{2,66},{66,130... | collective-permute-start | bytes 122888 | tf_op jit(solution)/shard_map/ppermute | solution.py:15
  67.0 1.6 %collective-permute-done.2 = f32[10,8,128]{2,1,0:T(8,128)S(1)} collective-permute-done((f32[10,8,128]{2,1,0:T(8,128)S(1)}, f32[10,8,128]{2,1,0:T(8,128)S(1)}, u32[]{:S(2)}, u32[]{:S(2)}) %collective-permute-start.2) | collective-permute-done | bytes 40992 | tf_op jit(solution)/shard_map/ppermute | solution.py:15
  68.6 4.2 %collective-permute-start.3 = (f32[10,8,128]{2,1,0:T(8,128)S(1)}, f32[10,8,128]{2,1,0:T(8,128)S(1)}, u32[]{:S(2)}, u32[]{:S(2)}) collective-permute-start(f32[10,8,128]{2,1,0:T(8,128)S(1)} %add_add_fusion.16), channel_id=1, source_target_pairs={{0,64},{64,128},{128,192},{1,65},{65,129},{129,193},{2,66},{66,130... | collective-permute-start | bytes 122888 | tf_op jit(solution)/shard_map/ppermute | solution.py:15
  72.9 1.6 %collective-permute-done.3 = f32[10,8,128]{2,1,0:T(8,128)S(1)} collective-permute-done((f32[10,8,128]{2,1,0:T(8,128)S(1)}, f32[10,8,128]{2,1,0:T(8,128)S(1)}, u32[]{:S(2)}, u32[]{:S(2)}) %collective-permute-start.3) | collective-permute-done | bytes 40992 | tf_op jit(solution)/shard_map/ppermute | solution.py:15
  74.6 4.4 %collective-permute-start.4 = (f32[10,8,128]{2,1,0:T(8,128)S(1)}, f32[10,8,128]{2,1,0:T(8,128)S(1)}, u32[]{:S(2)}, u32[]{:S(2)}) collective-permute-start(f32[10,8,128]{2,1,0:T(8,128)S(1)} %add_add_fusion.15), channel_id=1, source_target_pairs={{0,64},{64,128},{128,192},{1,65},{65,129},{129,193},{2,66},{66,130... | collective-permute-start | bytes 122888 | tf_op jit(solution)/shard_map/ppermute | solution.py:15
  79.4 1.1 collective-permute-done.4
  83.0 1.4 collective-permute-start.5
  84.5 4.8 %collective-permute-done.5 = f32[10,8,128]{2,1,0:T(8,128)S(1)} collective-permute-done((f32[10,8,128]{2,1,0:T(8,128)S(1)}, f32[10,8,128]{2,1,0:T(8,128)S(1)}, u32[]{:S(2)}, u32[]{:S(2)}) %collective-permute-start.5) | collective-permute-done | bytes 40992 | tf_op jit(solution)/shard_map/ppermute | solution.py:15
  89.4 1.3 collective-permute-start.6
  90.7 4.6 %collective-permute-done.6 = f32[10,8,128]{2,1,0:T(8,128)S(1)} collective-permute-done((f32[10,8,128]{2,1,0:T(8,128)S(1)}, f32[10,8,128]{2,1,0:T(8,128)S(1)}, u32[]{:S(2)}, u32[]{:S(2)}) %collective-permute-start.6) | collective-permute-done | bytes 40992 | tf_op jit(solution)/shard_map/ppermute | solution.py:15
  95.4 1.3 collective-permute-start.7
  96.7 4.6 %collective-permute-done.7 = f32[10,8,128]{2,1,0:T(8,128)S(1)} collective-permute-done((f32[10,8,128]{2,1,0:T(8,128)S(1)}, f32[10,8,128]{2,1,0:T(8,128)S(1)}, u32[]{:S(2)}, u32[]{:S(2)}) %collective-permute-start.7) | collective-permute-done | bytes 40992 | tf_op jit(solution)/shard_map/ppermute | solution.py:15
  103.4 1.1 convolution_bitcast_fusion.2
  104.5 10.3 %all-to-all-start.1 = ((f32[64,8,128]{2,1,0:T(8,128)}), f32[64,8,128]{2,1,0:T(8,128)S(1)}, u32[]{:S(2)}, u32[]{:S(2)}) async-start(f32[64,8,128]{2,1,0:T(8,128)} %convolution_bitcast_fusion.2), calls=%async_computation.1 | async-start | bytes 524288 | tf_op jit(solution)/shard_map/all_to_all | solution.py:102
  115.3 1.5 %reduce.5 = f32[64,8]{1,0:T(8,128)S(1)} reduce(f32[64,1,8]{2,1,0:T(1,128)} %all-to-all-done, f32[]{:T(128)} %broadcast.251), dimensions={1}, to_apply=%all_to_all.10.reduce_sub_computation.3 | reduce | bytes 4100 | tf_op jit(solution)/shard_map/all_to_all | solution.py:103
  117.7 8.7 %all-to-all-done.1 = f32[64,8,128]{2,1,0:T(8,128)S(1)} async-done(((f32[64,8,128]{2,1,0:T(8,128)}), f32[64,8,128]{2,1,0:T(8,128)S(1)}, u32[]{:S(2)}, u32[]{:S(2)}) %all-to-all-start.1) | async-done | bytes 262176 | tf_op jit(solution)/shard_map/all_to_all | solution.py:102
  126.6 16.9 %psum.7 = f32[64,128]{1,0:T(8,128)} all-reduce(f32[64,128]{1,0:T(8,128)S(1)} %fusion.17), channel_id=1, replica_groups=mesh['wall'=4,'tile'=64] {'wall'}, use_global_device_ids=true, to_apply=%region_3.4 | all-reduce | flops 8192 | bytes 65536 | tf_op jit(solution)/shard_map/psum | solution.py:173
  (251 shorter events, 29.9 us)
Async XLA Ops:
  0.6 102.4 %copy-start = (f32[256,10,8]{0,2,1:T(8,128)S(1)}, f32[256,10,8]{0,2,1:T(8,128)}, u32[]{:S(2)}) copy-start(f32[256,10,8]{0,2,1:T(8,128)} %param.20) | copy-start | bytes 245764
  2.5 52.3 %collective-permute-start = (f32[11,8,2,128]{3,2,1,0:T(2,128)}, f32[11,8,2,128]{3,2,1,0:T(2,128)}, u32[]{:S(2)}, u32[]{:S(2)}) collective-permute-start(f32[11,8,2,128]{3,2,1,0:T(2,128)} %get-tuple-element.326), channel_id=1, source_target_pairs={{0,1},{1,2},{2,3},{3,4},{4,5},{5,6},{6,7},{7,8},{8,9},{9,10},{10,1... | collective-permute-start | bytes 270344 | tf_op jit(solution)/shard_map/ppermute | solution.py:26
  4.4 50.3 %collective-permute-start.1 = (f32[11,8,2,128]{3,2,1,0:T(2,128)}, f32[11,8,2,128]{3,2,1,0:T(2,128)}, u32[]{:S(2)}, u32[]{:S(2)}) collective-permute-start(f32[11,8,2,128]{3,2,1,0:T(2,128)} %get-tuple-element.327), channel_id=1, source_target_pairs={{1,0},{2,1},{3,2},{4,3},{5,4},{6,5},{7,6},{8,7},{9,8},{10,9},{11,1... | collective-permute-start | bytes 270344 | tf_op jit(solution)/shard_map/ppermute | solution.py:28
  17.3 87.2 %all-to-all-start = ((f32[64,1,8]{2,1,0:T(1,128)}), f32[64,1,8]{2,1,0:T(1,128)}, u32[]{:S(2)}, u32[]{:S(2)}) async-start(f32[64,1,8]{2,1,0:T(1,128)} %bitcast.860), calls=%async_computation | async-start | bytes 65536 | tf_op jit(solution)/shard_map/all_to_all | solution.py:103
  28.8 4.1 %copy-start.37 = (f32[10,10,8,8,128]{4,3,2,1,0:T(8,128)S(1)}, f32[10,10,8,8,128]{4,3,2,1,0:T(8,128)}, u32[]{:S(2)}) copy-start(f32[10,10,8,8,128]{4,3,2,1,0:T(8,128)} %param.18) | copy-start | bytes 9830404
  33.1 3.5 %copy-start.10 = (f32[10,10,1,8,128]{4,3,2,1,0:T(8,128)}, f32[10,10,1,8,128]{4,3,2,1,0:T(8,128)S(1)}, u32[]{:S(2)}) copy-start(f32[10,10,1,8,128]{4,3,2,1,0:T(8,128)S(1)} %get-tuple-element.26) | copy-start | bytes 1228804
  33.1 3.5 %copy-start.12 = (f32[10,10,1,8,128]{4,3,2,1,0:T(8,128)}, f32[10,10,1,8,128]{4,3,2,1,0:T(8,128)S(1)}, u32[]{:S(2)}) copy-start(f32[10,10,1,8,128]{4,3,2,1,0:T(8,128)S(1)} %get-tuple-element.27) | copy-start | bytes 1228804
  33.1 4.4 %copy-start.6 = (f32[10,10,1,8,128]{4,3,2,1,0:T(8,128)}, f32[10,10,1,8,128]{4,3,2,1,0:T(8,128)S(1)}, u32[]{:S(2)}) copy-start(f32[10,10,1,8,128]{4,3,2,1,0:T(8,128)S(1)} %get-tuple-element.28) | copy-start | bytes 1228804
  33.1 4.4 %copy-start.8 = (f32[10,10,1,8,128]{4,3,2,1,0:T(8,128)}, f32[10,10,1,8,128]{4,3,2,1,0:T(8,128)S(1)}, u32[]{:S(2)}) copy-start(f32[10,10,1,8,128]{4,3,2,1,0:T(8,128)S(1)} %get-tuple-element.29) | copy-start | bytes 1228804
  33.2 2.3 %copy-start.29 = (f32[10,10,8,128]{3,2,0,1:T(8,128)}, f32[10,10,8,128]{3,2,0,1:T(8,128)S(1)}, u32[]{:S(2)}) copy-start(f32[10,10,8,128]{3,2,0,1:T(8,128)S(1)} %get-tuple-element.698) | copy-start | bytes 1228804
  38.4 2.8 %copy-start.35 = (f32[10,10,8,128]{3,2,0,1:T(8,128)}, f32[10,10,8,128]{3,2,0,1:T(8,128)S(1)}, u32[]{:S(2)}) copy-start(f32[10,10,8,128]{3,2,0,1:T(8,128)S(1)} %get-tuple-element.693) | copy-start | bytes 1228804
  55.5 7.8 %copy-start.3 = (f32[10,10,1,8,128]{4,3,0,1,2:T(8,128)S(1)}, f32[10,10,1,8,128]{4,3,0,1,2:T(8,128)}, u32[]{:S(2)}) copy-start(f32[10,10,1,8,128]{4,3,0,1,2:T(8,128)} %copy-done.2) | copy-start | bytes 1228804
  55.5 7.8 %copy-start.4 = (f32[10,10,8,128]{3,2,0,1:T(8,128)S(1)}, f32[10,10,8,128]{3,2,0,1:T(8,128)}, u32[]{:S(2)}) copy-start(f32[10,10,8,128]{3,2,0,1:T(8,128)} %multiply_add_fusion.7) | copy-start | bytes 1228804
  55.6 11.3 %copy-start.42 = (f32[10,10,8,128]{3,2,1,0:T(8,128)S(1)}, f32[10,10,8,128]{3,2,1,0:T(8,128)}, u32[]{:S(2)}) copy-start(f32[10,10,8,128]{3,2,1,0:T(8,128)} %multiply_add_fusion.1) | copy-start | bytes 1228804
  57.4 15.4 %copy-start.19 = (f32[10,10,8,128]{3,2,0,1:T(8,128)S(1)}, f32[10,10,8,128]{3,2,0,1:T(8,128)}, u32[]{:S(2)}) copy-start(f32[10,10,8,128]{3,2,0,1:T(8,128)} %get-tuple-element.692) | copy-start | bytes 1228804
  59.0 4.4 %copy-start.40 = (f32[10,8,8,128]{3,2,1,0:T(8,128)S(1)}, f32[10,8,8,128]{3,2,1,0:T(8,128)}, u32[]{:S(2)}) copy-start(f32[10,8,8,128]{3,2,1,0:T(8,128)} %copy-done.39) | copy-start | bytes 983044
  61.6 17.7 %copy-start.41 = (f32[10,10,1,8,128]{4,3,2,1,0:T(8,128)S(1)}, f32[10,10,1,8,128]{4,3,2,1,0:T(8,128)}, u32[]{:S(2)}) copy-start(f32[10,10,1,8,128]{4,3,2,1,0:T(8,128)} %get-tuple-element.44) | copy-start | bytes 1228804
  63.4 5.1 %collective-permute-start.2 = (f32[10,8,128]{2,1,0:T(8,128)S(1)}, f32[10,8,128]{2,1,0:T(8,128)S(1)}, u32[]{:S(2)}, u32[]{:S(2)}) collective-permute-start(f32[10,8,128]{2,1,0:T(8,128)S(1)} %get-tuple-element.20), channel_id=1, source_target_pairs={{0,64},{64,128},{128,192},{1,65},{65,129},{129,193},{2,66},{66,130... | collective-permute-start | bytes 122888 | tf_op jit(solution)/shard_map/ppermute | solution.py:15
  68.6 5.9 %collective-permute-start.3 = (f32[10,8,128]{2,1,0:T(8,128)S(1)}, f32[10,8,128]{2,1,0:T(8,128)S(1)}, u32[]{:S(2)}, u32[]{:S(2)}) collective-permute-start(f32[10,8,128]{2,1,0:T(8,128)S(1)} %add_add_fusion.16), channel_id=1, source_target_pairs={{0,64},{64,128},{128,192},{1,65},{65,129},{129,193},{2,66},{66,130... | collective-permute-start | bytes 122888 | tf_op jit(solution)/shard_map/ppermute | solution.py:15
  74.6 5.9 %collective-permute-start.4 = (f32[10,8,128]{2,1,0:T(8,128)S(1)}, f32[10,8,128]{2,1,0:T(8,128)S(1)}, u32[]{:S(2)}, u32[]{:S(2)}) collective-permute-start(f32[10,8,128]{2,1,0:T(8,128)S(1)} %add_add_fusion.15), channel_id=1, source_target_pairs={{0,64},{64,128},{128,192},{1,65},{65,129},{129,193},{2,66},{66,130... | collective-permute-start | bytes 122888 | tf_op jit(solution)/shard_map/ppermute | solution.py:15
  81.6 2.8 %copy-start.11 = (f32[10,10,1,8,128]{4,3,2,1,0:T(8,128)S(1)}, f32[10,10,1,8,128]{4,3,2,1,0:T(8,128)}, u32[]{:S(2)}) copy-start(f32[10,10,1,8,128]{4,3,2,1,0:T(8,128)} %copy-done.10) | copy-start | bytes 1228804
  81.6 2.8 %copy-start.13 = (f32[10,10,1,8,128]{4,3,2,1,0:T(8,128)S(1)}, f32[10,10,1,8,128]{4,3,2,1,0:T(8,128)}, u32[]{:S(2)}) copy-start(f32[10,10,1,8,128]{4,3,2,1,0:T(8,128)} %copy-done.12) | copy-start | bytes 1228804
  82.1 8.5 %copy-start.7 = (f32[10,10,1,8,128]{4,3,2,1,0:T(8,128)S(1)}, f32[10,10,1,8,128]{4,3,2,1,0:T(8,128)}, u32[]{:S(2)}) copy-start(f32[10,10,1,8,128]{4,3,2,1,0:T(8,128)} %copy-done.6) | copy-start | bytes 1228804
  82.1 8.5 %copy-start.9 = (f32[10,10,1,8,128]{4,3,2,1,0:T(8,128)S(1)}, f32[10,10,1,8,128]{4,3,2,1,0:T(8,128)}, u32[]{:S(2)}) copy-start(f32[10,10,1,8,128]{4,3,2,1,0:T(8,128)} %copy-done.8) | copy-start | bytes 1228804
  82.8 18.5 %copy-start.5 = (f32[10,10,8,128]{3,2,0,1:T(8,128)S(1)}, f32[10,10,8,128]{3,2,0,1:T(8,128)}, u32[]{:S(2)}) copy-start(f32[10,10,8,128]{3,2,0,1:T(8,128)} %get-tuple-element.684) | copy-start | bytes 1228804
  82.8 18.5 %copy-start.14 = (f32[10,10,8,128]{3,2,0,1:T(8,128)S(1)}, f32[10,10,8,128]{3,2,0,1:T(8,128)}, u32[]{:S(2)}) copy-start(f32[10,10,8,128]{3,2,0,1:T(8,128)} %get-tuple-element.685) | copy-start | bytes 1228804
  82.9 18.5 %copy-start.15 = (f32[10,10,8,128]{3,2,0,1:T(8,128)S(1)}, f32[10,10,8,128]{3,2,0,1:T(8,128)}, u32[]{:S(2)}) copy-start(f32[10,10,8,128]{3,2,0,1:T(8,128)} %get-tuple-element.686) | copy-start | bytes 1228804
  83.0 18.6 %copy-start.16 = (f32[10,10,8,128]{3,2,0,1:T(8,128)S(1)}, f32[10,10,8,128]{3,2,0,1:T(8,128)}, u32[]{:S(2)}) copy-start(f32[10,10,8,128]{3,2,0,1:T(8,128)} %get-tuple-element.687) | copy-start | bytes 1228804
  83.0 6.3 %collective-permute-start.5 = (f32[10,8,128]{2,1,0:T(8,128)S(1)}, f32[10,8,128]{2,1,0:T(8,128)S(1)}, u32[]{:S(2)}, u32[]{:S(2)}) collective-permute-start(f32[10,8,128]{2,1,0:T(8,128)S(1)} %get-tuple-element.6), channel_id=1, source_target_pairs={{64,0},{128,64},{192,128},{65,1},{129,65},{193,129},{66,2},{130,66... | collective-permute-start | bytes 122888 | tf_op jit(solution)/shard_map/ppermute | solution.py:15
  89.4 6.0 %collective-permute-start.6 = (f32[10,8,128]{2,1,0:T(8,128)S(1)}, f32[10,8,128]{2,1,0:T(8,128)S(1)}, u32[]{:S(2)}, u32[]{:S(2)}) collective-permute-start(f32[10,8,128]{2,1,0:T(8,128)S(1)} %add_add_fusion.1), channel_id=1, source_target_pairs={{64,0},{128,64},{192,128},{65,1},{129,65},{193,129},{66,2},{130,66... | collective-permute-start | bytes 122888 | tf_op jit(solution)/shard_map/ppermute | solution.py:15
  95.4 5.9 %collective-permute-start.7 = (f32[10,8,128]{2,1,0:T(8,128)S(1)}, f32[10,8,128]{2,1,0:T(8,128)S(1)}, u32[]{:S(2)}, u32[]{:S(2)}) collective-permute-start(f32[10,8,128]{2,1,0:T(8,128)S(1)} %add_add_fusion), channel_id=1, source_target_pairs={{64,0},{128,64},{192,128},{65,1},{129,65},{193,129},{66,2},{130,66... | collective-permute-start | bytes 122888 | tf_op jit(solution)/shard_map/ppermute | solution.py:15
  104.5 21.9 %all-to-all-start.1 = ((f32[64,8,128]{2,1,0:T(8,128)}), f32[64,8,128]{2,1,0:T(8,128)S(1)}, u32[]{:S(2)}, u32[]{:S(2)}) async-start(f32[64,8,128]{2,1,0:T(8,128)} %convolution_bitcast_fusion.2), calls=%async_computation.1 | async-start | bytes 524288 | tf_op jit(solution)/shard_map/all_to_all | solution.py:102
  (23 other events, 33.8 us)
where the time goes:
time: 145 us; the launch traced here: 144 us
  starting transfers between devices  45.6 us (31%)
  waiting for transfers between devices  27 us (19%)
  other arithmetic  25.1 us (17%)
  local copies, waits for them, and re-layouts  21.2 us (15%)
  blocking collectives  16.9 us (12%)
  matrix products  4.99 us (3%)
  between operations  2.63 us (2%)
    ppermute x6, waiting for transfers between devices, shifted(): return lax.ppermute(block, axis, route)  18.3 us
    psum x1, blocking collectives, on_device(): patch_sums = lax.psum(deliver(send_rows, send_tag), 'wall')  16.9 us
    ppermute x6, starting transfers between devices, shifted(): return lax.ppermute(block, axis, route)  16.1 us
    all_to_all x1, starting transfers between devices, deliver(): lax.all_to_all(send_rows, 'tile', split_axis=0, concat_axis=0, tiled=True)  10.3 us
    all_to_all x1, starting transfers between devices, deliver(): lax.all_to_all(send_tag, 'tile', split_axis=0, concat_axis=0, tiled=True)  9.74 us
    all_to_all x1, waiting for transfers between devices, deliver(): lax.all_to_all(send_rows, 'tile', split_axis=0, concat_axis=0, tiled=True)  8.7 us
    ppermute x1, starting transfers between devices, extended(): lax.ppermute(head, axis, [((i + 1) % count, i) for i in range(ends)])  7.47 us
    add x14, other arithmetic, block_times_block(): running = product_term if running is None else running + product_term  5.76 us
  transfers between devices with their start and end apart: 10, of which 7 were waited for; matrix products, arithmetic and copies ran while one was open for 32% of the time, Pallas kernels for 0%

commit v1 on v0

v1 whole, which is shorter than its diff:
```python
import jax
import jax.numpy as jnp
from jax import lax
from jax.experimental import pallas as pl
from jax.experimental.pallas import tpu as pltpu
from jax.sharding import PartitionSpec as P

NV = 10
K = 8
H = 8
S = 128
PATCH_DEV = 64
SLOTS = 8
ROWS_PER_OWNER = SLOTS + 1
F32 = jnp.float32
highest = lax.Precision.HIGHEST

VM = pl.BlockSpec(memory_space=pltpu.VMEM)
SM = pl.BlockSpec(memory_space=pltpu.SMEM)


def f32(*shape):
    return jax.ShapeDtypeStruct(shape, F32)


def call(body, out_shape, n_in, smem=(), scratch=(), flops=0, nbytes=0):
    single = not isinstance(out_shape, (tuple, list))
    return pl.pallas_call(
        body,
        out_shape=out_shape,
        in_specs=[SM if i in smem else VM for i in range(n_in)],
        out_specs=VM if single else [VM] * len(out_shape),
        scratch_shapes=list(scratch),
        compiler_params=pltpu.CompilerParams(vmem_limit_bytes=40 * 1024 * 1024),
        cost_estimate=pl.CostEstimate(flops=flops, bytes_accessed=nbytes, transcendentals=0),
    )


def block_dot(m_ref, k, x):
    acc = None
    for j in range(NV):
        term = m_ref[:, j, k] * x[j][None]
        acc = term if acc is None else acc + term
    return acc


def forward_sweep(l_ref, d_ref, r_ref, s_ref, x):
    f = x
    for k in range(K):
        r = r_ref[:, k]
        f = r if f is None else r + block_dot(l_ref, k, f)
        s_ref[k] = block_dot(d_ref, k, f)
    return f


def backward_sweep(u_ref, s_ref, w_ref, y, emit=None):
    b, p = y, None
    for k in range(K - 1, -1, -1):
        s = s_ref[k]
        b = s if b is None else s - block_dot(u_ref, k, b)
        if w_ref is not None:
            p = b * w_ref[k] if p is None else p + b * w_ref[k]
        if emit is not None:
            emit(k, b)
    return b, p


def map_dot(m_ref, base, x):
    acc = None
    for j in range(NV):
        term = m_ref[base + j] * x[j][None]
        acc = term if acc is None else acc + term
    return acc


def pack_kernel(a_ref, rad_ref, lo_ref, hi_ref):
    for v in range(NV + 1):
        for k in range(K):
            cell = a_ref[v, k] if v < NV else rad_ref[k]
            at = 2 * (v * K + k)
            lo_ref[at : at + 2, :] = cell[0:2]
            hi_ref[at : at + 2, :] = cell[6:8]


def interior_kernel(a_ref, src_ref, rad_ref, frq_ref, out_ref):
    row = lax.broadcasted_iota(jnp.int32, (H, S), 0)
    lane = lax.broadcasted_iota(jnp.int32, (H, S), 1)
    for k in range(K):
        a = a_ref[:, k]
        rad = rad_ref[k]
        applied = None
        for d, w in ((-2, -0.0625), (-1, 0.25), (1, 0.25), (2, -0.0625)):
            inside = (row + d >= 0) & (row + d < H)
            coef = jnp.where(inside, w * (rad + pltpu.roll(rad, (-d) % H, 0)), 0.0)
            term = coef[None] * pltpu.roll(a, (-d) % H, 1)
            applied = term if applied is None else applied + term
        for d in (-1, 1):
            inside = (lane + d >= 0) & (lane + d < S)
            coef = jnp.where(inside, 0.25 * (rad + pltpu.roll(rad, (-d) % S, 1)), 0.0)
            applied = applied + coef[None] * pltpu.roll(a, (-d) % S, 2)
        frq = frq_ref[k][None]
        half = NV // 2
        src = src_ref[:, k] - applied
        out_ref[:half, k] = src[:half] + frq * a[half:]
        out_ref[half:, k] = src[half:] - frq * a[:half]


def maps_kernel(pos_ref, w_ref, l_ref, d_ref, u_ref, ab_ref, q_ref, s_ref):
    wall = pos_ref[0]

    def pair_dot(m_ref, k, xs):
        accs = [None] * len(xs)
        for j in range(NV):
            m = m_ref[:, j, k]
            for n, x in enumerate(xs):
                term = m * x[j][None]
                accs[n] = term if accs[n] is None else accs[n] + term
        return accs

    @pl.when(wall <= 1)
    def _():
        @pl.loop(0, NV // 2)
        def _(pair):
            cols = [2 * pair, 2 * pair + 1]
            bs = [-u_ref[:, c, K - 1] for c in cols]
            ps = [b * w_ref[K - 1] for b in bs]
            for k in range(K - 2, -1, -1):
                bs = [-b for b in pair_dot(u_ref, k, bs)]
                ps = [p + b * w_ref[k] for p, b in zip(ps, bs)]
            for c, b, p in zip(cols, bs, ps):
                ab_ref[c] = b
                ab_ref[NV + c] = p
                q_ref[c] = p

    @pl.when(wall == 3)
    def _():
        @pl.loop(0, NV // 2)
        def _(pair):
            cols = [2 * pair, 2 * pair + 1]
            gs = [l_ref[:, c, 0] for c in cols]
            for k in range(K):
                if k > 0:
                    gs = pair_dot(l_ref, k, gs)
                for n, s in enumerate(pair_dot(d_ref, k, gs)):
                    s_ref[k, n] = s
            cs = [s_ref[K - 1, n] for n in range(2)]
            ps = [c * w_ref[K - 1] for c in cs]
            for k in range(K - 2, -1, -1):
                cs = [s_ref[k, n] - c for n, c in enumerate(pair_dot(u_ref, k, cs))]
                ps = [p + c * w_ref[k] for p, c in zip(ps, cs)]
            for col, c, p in zip(cols, cs, ps):
                ab_ref[col] = c
                ab_ref[NV + col] = p


def residual_kernel(pos_ref, w_ref, r_ref, left_ref, right_ref, rad_ref, l_ref, d_ref, u_ref, out_ref, msg_ref, s_ref):
    wall, tile, last = pos_ref[0], pos_ref[1], pos_ref[2]
    row = lax.broadcasted_iota(jnp.int32, (H, S), 0)
    has_left = tile > 0
    has_right = tile < last

    def line(ref, v, k, c):
        at = 2 * (v * K + k) + c
        return jnp.broadcast_to(ref[at : at + 1, :], (H, S))

    for k in range(K):
        rad = rad_ref[k]
        l0, l1, r0, r1 = (line(ref, NV, k, c) for ref in (left_ref, right_ref) for c in (0, 1))
        zero = jnp.zeros((H, S), F32)
        f_l0 = jnp.where((row == 0) & has_left, -0.0625 * (rad + l0), zero)
        f_l1 = jnp.where(row == 0, 0.25 * (rad + l1), jnp.where(row == 1, -0.0625 * (rad + l1), zero))
        f_l1 = jnp.where(has_left, f_l1, zero)
        f_r0 = jnp.where(row == 7, 0.25 * (rad + r0), jnp.where(row == 6, -0.0625 * (rad + r0), zero))
        f_r0 = jnp.where(has_right, f_r0, zero)
        f_r1 = jnp.where((row == 7) & has_right, -0.0625 * (rad + r1), zero)
        for v in range(NV):
            applied = f_l0 * line(left_ref, v, k, 0) + f_l1 * line(left_ref, v, k, 1)
            applied = applied + (f_r0 * line(right_ref, v, k, 0) + f_r1 * line(right_ref, v, k, 1))
            out_ref[v, k] = r_ref[v, k] - applied

    @pl.when((wall == 0) | (wall == 3))
    def _():
        f = forward_sweep(l_ref, d_ref, out_ref, s_ref, None)
        b, p = backward_sweep(u_ref, s_ref, w_ref, None)
        msg_ref[:NV] = jnp.where(wall == 0, f, b)
        msg_ref[NV:] = p


def middle_kernel(pos_ref, w_ref, msg_ref, r_ref, l_ref, d_ref, u_ref, out_ref, s_ref):
    @pl.when(pos_ref[0] == 1)
    def _():
        x = msg_ref[:NV]
        out_ref[:NV] = forward_sweep(l_ref, d_ref, r_ref, s_ref, x)
        b, p = backward_sweep(u_ref, s_ref, w_ref, None)
        out_ref[NV : 2 * NV] = b
        out_ref[2 * NV :] = p + msg_ref[NV:]


def decide_kernel(
    pos_ref, w_ref, low_ref, high_ref, m1_ref, m3_ref, m0_ref, pw_ref, r_ref, l_ref, d_ref, u_ref,
    x3_ref, y2_ref, y1_ref, y0_ref, rows_ref, s_ref, prof_ref,
):
    @pl.when(pos_ref[0] == 2)
    def _():
        x3 = forward_sweep(l_ref, d_ref, r_ref, s_ref, low_ref[:NV])
        x3_ref[...] = x3
        y2 = high_ref[:NV] + map_dot(m3_ref, 0, x3)
        y2_ref[...] = y2
        total = low_ref[2 * NV :] + high_ref[NV:] + map_dot(m3_ref, NV, x3)
        y1, p2 = backward_sweep(u_ref, s_ref, w_ref, y2)
        y1_ref[...] = y1
        y0 = low_ref[NV : 2 * NV] + map_dot(m1_ref, 0, y1)
        y0_ref[...] = y0
        total = total + p2 + map_dot(m1_ref, NV, y1) + map_dot(m0_ref, 0, y0)
        for v in range(NV):
            prof_ref[v * H : (v + 1) * H, :] = total[v]
        row = lax.broadcasted_iota(jnp.int32, (SLOTS, S), 0)
        lane = lax.broadcasted_iota(jnp.int32, (SLOTS, S), 1)
        prof_ref[NV * H :, :] = (row == lane).astype(F32)
        rows_ref[...] = jnp.dot(pw_ref[...], prof_ref[...], precision=highest, preferred_element_type=F32)


def finish_kernel(pos_ref, low_ref, mid_ref, x3_ref, y2_ref, y1_ref, y0_ref, r_ref, l_ref, d_ref, u_ref, out_ref, s_ref, x_ref, y_ref):
    wall = pos_ref[0]
    zero = jnp.zeros((NV, H, S), F32)
    x = jnp.where(wall == 1, low_ref[:NV], zero)
    x = jnp.where(wall == 2, mid_ref[:NV], x)
    x_ref[...] = jnp.where(wall == 3, x3_ref[...], x)
    y = jnp.where(wall == 0, y0_ref[...], zero)
    y = jnp.where(wall == 1, y1_ref[...], y)
    y_ref[...] = jnp.where(wall == 2, y2_ref[...], y)
    forward_sweep(l_ref, d_ref, r_ref, s_ref, x_ref[...])

    def emit(k, b):
        out_ref[:, k] = b

    backward_sweep(u_ref, s_ref, None, y_ref[...], emit)


def place_kernel(count_ref, w_ref, owner_ref, tag_ref, out_ref):
    blocks = owner_ref.shape[0]
    owners = out_ref.shape[0] // ROWS_PER_OWNER
    owner = owner_ref[...]
    index = lax.broadcasted_iota(jnp.int32, (blocks, 1), 0)
    live = index < count_ref[0]
    hits = (owner == lax.broadcasted_iota(jnp.int32, (blocks, owners), 1)).astype(F32)
    earlier = lax.broadcasted_iota(jnp.int32, (blocks, blocks), 1) < lax.broadcasted_iota(jnp.int32, (blocks, blocks), 0)
    before = jnp.dot(earlier.astype(F32), hits, preferred_element_type=F32)
    slot = jnp.sum(before * hits, axis=1, keepdims=True).astype(jnp.int32)
    column = lax.broadcasted_iota(jnp.int32, (blocks, owners * ROWS_PER_OWNER), 1)
    placed = ((owner * ROWS_PER_OWNER + slot == column) & live).astype(F32)
    tagged = ((owner * ROWS_PER_OWNER + SLOTS == column) & live).astype(F32)
    width = NV * H
    lanes = lax.broadcasted_iota(jnp.int32, (blocks, SLOTS), 1)
    tags = jnp.where(lanes == slot, (tag_ref[...] + 1).astype(F32), 0.0)
    dims = (((0,), (0,)), ((), ()))
    out_ref[:, :width] = lax.dot_general(placed, w_ref[...], dims, precision=highest, preferred_element_type=F32)
    out_ref[:, width:] = lax.dot_general(tagged, tags, dims, precision=highest, preferred_element_type=F32)


def pick_kernel(got_ref, out_ref):
    rows = got_ref.shape[0]
    sources = rows // ROWS_PER_OWNER
    tag_rows = got_ref[pl.ds(SLOTS, sources, stride=ROWS_PER_OWNER), :]
    lane_of = (
        lax.broadcasted_iota(jnp.int32, (SLOTS, S), 0) == lax.broadcasted_iota(jnp.int32, (SLOTS, S), 1)
    ).astype(F32)
    tags = lax.dot_general(
        lane_of, tag_rows, (((1,), (1,)), ((), ())), precision=highest, preferred_element_type=F32
    )
    column = lax.broadcasted_iota(jnp.int32, (sources, rows), 1)
    first = lax.broadcasted_iota(jnp.int32, (sources, rows), 0) * ROWS_PER_OWNER
    spread = ((column >= first) & (column < first + ROWS_PER_OWNER)).astype(F32)
    wide = jnp.dot(tags, spread, precision=highest, preferred_element_type=F32)
    slot = lax.broadcasted_iota(jnp.int32, (SLOTS, rows), 1) % ROWS_PER_OWNER
    mine = slot == lax.broadcasted_iota(jnp.int32, (SLOTS, rows), 0)
    tag = jnp.sum(jnp.where(mine, wide, 0.0), axis=0, keepdims=True)
    target = (lax.broadcasted_iota(jnp.int32, (PATCH_DEV, rows), 0) + 1).astype(F32)
    picker = (tag == target).astype(F32)
    out_ref[...] = jnp.dot(picker, got_ref[...], precision=highest, preferred_element_type=F32)


def on_device(
    adjoint, source, radius, frequency, lower, diag, upper, wall_weight,
    surface_weight, patch_owner, patch_row, surface_count,
):
    tiles = lax.axis_size("tile")
    pos = jnp.stack([lax.axis_index("wall"), lax.axis_index("tile"), jnp.int32(tiles - 1)]).astype(jnp.int32)
    vm = lambda x: pltpu.with_memory_space_constraint(x, pltpu.VMEM)
    lower, diag, upper = vm(lower), vm(diag), vm(upper)
    vec = f32(NV, H, S)
    levels = pltpu.VMEM((K, NV, H, S), F32)

    lo, hi = call(pack_kernel, (f32(22 * K, S), f32(22 * K, S)), 2, nbytes=800_000)(adjoint, radius)
    left = lax.ppermute(hi, "tile", [(i, (i + 1) % tiles) for i in range(tiles)])
    right = lax.ppermute(lo, "tile", [((i + 1) % tiles, i) for i in range(tiles)])

    inner = call(interior_kernel, f32(NV, K, H, S), 4, flops=4_000_000, nbytes=1_200_000)(
        adjoint, source, radius, frequency
    )
    maps, q0 = call(
        maps_kernel, (f32(2 * NV, NV, H, S), f32(NV, NV, H, S)), 5, smem=(0, 1),
        scratch=(pltpu.VMEM((K, 2, NV, H, S), F32),), flops=44_000_000, nbytes=11_000_000,
    )(pos, wall_weight, lower, diag, upper)
    map1 = lax.ppermute(maps, "wall", [(1, 2)])
    map3 = lax.ppermute(maps, "wall", [(3, 2)])
    map0 = lax.ppermute(q0, "wall", [(0, 2)])

    resid, first = call(
        residual_kernel, (f32(NV, K, H, S), f32(2 * NV, H, S)), 9, smem=(0, 1), scratch=(levels,),
        flops=6_000_000, nbytes=2_000_000,
    )(pos, wall_weight, inner, left, right, radius, lower, diag, upper)
    low = lax.ppermute(first, "wall", [(0, 1), (3, 2)])
    second = call(
        middle_kernel, f32(3 * NV, H, S), 7, smem=(0, 1), scratch=(levels,), flops=5_000_000, nbytes=2_000_000
    )(pos, wall_weight, low, resid, lower, diag, upper)
    mid = lax.ppermute(second, "wall", [(1, 2)])

    placed = call(
        place_kernel, f32(tiles * ROWS_PER_OWNER, NV * H + SLOTS), 4, smem=(0,), flops=50_000_000, nbytes=1_000_000
    )(surface_count, surface_weight.reshape(-1, NV * H), patch_owner, patch_row.reshape(-1, 1))

    x3, y2, y1, y0, rows = call(
        decide_kernel, (vec, vec, vec, vec, f32(tiles * ROWS_PER_OWNER, S)), 12, smem=(0, 1),
        scratch=(levels, pltpu.VMEM((NV * H + SLOTS, S), F32)), flops=20_000_000, nbytes=3_000_000,
    )(pos, wall_weight, mid, low, map1, map3, map0, placed, resid, lower, diag, upper)
    x3 = lax.ppermute(x3, "wall", [(2, 3)])
    y1 = lax.ppermute(y1, "wall", [(2, 1)])
    y0 = lax.ppermute(y0, "wall", [(2, 0)])
    got = lax.all_to_all(rows, "tile", split_axis=0, concat_axis=0, tiled=True)
    adjoint_next = call(
        finish_kernel, f32(NV, K, H, S), 11, smem=(0,),
        scratch=(levels, pltpu.VMEM((NV, H, S), F32), pltpu.VMEM((NV, H, S), F32)), flops=5_000_000, nbytes=2_000_000,
    )(pos, low, mid, x3, y2, y1, y0, resid, lower, diag, upper)
    part = call(pick_kernel, f32(PATCH_DEV, S), 1, flops=20_000_000, nbytes=400_000)(got)
    part = jnp.where(lax.axis_index("wall") == 2, part, 0.0)
    patch = part
    for w in (0, 1, 3):
        patch = patch + lax.ppermute(part, "wall", [(2, w)])
    return adjoint_next, patch


def solution(mesh):
    in_specs = (
        P(None, "wall", "tile", None),
        P(None, "wall", "tile", None),
        P("wall", "tile", None),
        P("wall", "tile", None),
        P(None, None, "wall", "tile", None),
        P(None, None, "wall", "tile", None),
        P(None, None, "wall", "tile", None),
        P("wall"),
        P("tile", None, None),
        P("tile", None),
        P("tile"),
        P("tile"),
    )
    out_specs = (P(None, "wall", "tile", None), P("tile", None))
    return jax.shard_map(
        on_device, mesh=mesh, in_specs=in_specs, out_specs=out_specs, check_vma=False
    )
```

time: 145 us -> 112 us (0.77)
  the two profiles are of different devices: /device:TPU:6 before, /device:TPU:23 now
where the time goes in v1:
time: 112 us
  waiting for transfers between devices  38.4 us (34%)
  starting transfers between devices  32.4 us (29%)
  local copies, waits for them, and re-layouts  25.5 us (23%)
  Pallas kernels  13 us (12%)
  between operations  1.59 us (1%)
    ppermute x1, waiting for transfers between devices, on_device(): low = lax.ppermute(first, 'wall', [(0, 1), (3, 2)])  22.3 us
    unnamed x51, local copies, waits for them, and re-layouts  20.3 us
    all_to_all x1, starting transfers between devices, on_device(): got = lax.all_to_all(rows, 'tile', split_axis=0, concat_axis=0, tiled=True)  13.4 us
    all_to_all x1, waiting for transfers between devices, on_device(): got = lax.all_to_all(rows, 'tile', split_axis=0, concat_axis=0, tiled=True)  12 us
    ppermute x3, starting transfers between devices, on_device(): patch = patch + lax.ppermute(part, 'wall', [(2, w)])  5.08 us
    pallas_call x1, Pallas kernels, on_device(): call(decide_kernel, (vec, vec, vec, vec, f32(tiles * ROWS_PER_OWNER, S)),...  3.95 us
    all_to_all x2, local copies, waits for them, and re-layouts, on_device(): got = lax.all_to_all(rows, 'tile', split_axis=0, concat_axis=0, tiled=True)  3.61 us
    pallas_call x1, Pallas kernels, on_device(): call(finish_kernel, f32(NV, K, H, S), 11, smem=(0,), scratch=(levels, plt...  2.84 us
  transfers between devices with their start and end apart: 14, of which 4 were waited for; matrix products, arithmetic and copies ran while one was open for 2% of the time, Pallas kernels for 7%

profile of v1, /device:TPU:23, one launch (start us, length us, event | category | flops | bytes accessed | tf_op | source)
XLA Modules:
  0.0 111.6 jit_solution(72753875276526626)
XLA Ops:
  0.7 1.9 %copy-done = f32[10,10,8,8,128]{4,3,2,1,0:T(8,128)S(1)} copy-done((f32[10,10,8,8,128]{4,3,2,1,0:T(8,128)S(1)}, f32[10,10,8,8,128]{4,3,2,1,0:T(8,128)}, u32[]{:S(2)}) %copy-start) | copy-done | bytes 3276824
  2.6 1.9 %copy-done.2 = f32[10,10,8,8,128]{4,3,2,1,0:T(8,128)S(1)} copy-done((f32[10,10,8,8,128]{4,3,2,1,0:T(8,128)S(1)}, f32[10,10,8,8,128]{4,3,2,1,0:T(8,128)}, u32[]{:S(2)}) %copy-start.2) | copy-done | bytes 3276824
  4.6 1.9 %copy-done.5 = f32[10,10,8,8,128]{4,3,2,1,0:T(8,128)S(1)} copy-done((f32[10,10,8,8,128]{4,3,2,1,0:T(8,128)S(1)}, f32[10,10,8,8,128]{4,3,2,1,0:T(8,128)}, u32[]{:S(2)}) %copy-start.5) | copy-done | bytes 3276824
  7.2 1.6 %shard_map.135 = (f32[20,10,8,128]{3,2,1,0:T(8,128)}, f32[10,10,8,128]{3,2,1,0:T(8,128)}) custom-call(s32[3]{0:T(128)S(1)} %pad_add_fusion.pos_ref, f32[8]{0:T(128)S(1)} %copy-done.19, f32[10,10,8,8,128]{4,3,2,1,0:T(8,128)S(1)} %copy-done, f32[10,10,8,8,128]{4,3,2,1,0:T(8,128)S(1)} %copy-done.2, f32[10,10,8,8,128]{4,3,2,1,0:T(8,128)S(1)} %copy-done.5), custom_call_target="tpu_custom_call" | custom-call | flops 44000000 | bytes 11000000 | tf_op jit(solution)/shard_map/pallas_call | solution.py:301
  8.8 1.4 %collective-permute-start.4 = (f32[20,10,8,128]{3,2,1,0:T(8,128)}, f32[20,10,8,128]{3,2,1,0:T(8,128)}, u32[]{:S(2)}, u32[]{:S(2)}) collective-permute-start(f32[20,10,8,128]{3,2,1,0:T(8,128)} %get-tuple-element.17), channel_id=1, source_target_pairs={{64,128},{65,129},{66,130},{67,131},{68,132},{69,133},{70,134},{71... | collective-permute-start | bytes 2457608 | tf_op jit(solution)/shard_map/ppermute | solution.py:305
  10.2 1.3 %collective-permute-start.5 = (f32[20,10,8,128]{3,2,1,0:T(8,128)}, f32[20,10,8,128]{3,2,1,0:T(8,128)}, u32[]{:S(2)}, u32[]{:S(2)}) collective-permute-start(f32[20,10,8,128]{3,2,1,0:T(8,128)} %get-tuple-element.17), channel_id=1, source_target_pairs={{192,128},{193,129},{194,130},{195,131},{196,132},{197,133},{198,1... | collective-permute-start | bytes 2457608 | tf_op jit(solution)/shard_map/ppermute | solution.py:306
  11.5 1.3 %collective-permute-start.6 = (f32[10,10,8,128]{3,2,1,0:T(8,128)}, f32[10,10,8,128]{3,2,1,0:T(8,128)}, u32[]{:S(2)}, u32[]{:S(2)}) collective-permute-start(f32[10,10,8,128]{3,2,1,0:T(8,128)} %get-tuple-element.18), channel_id=1, source_target_pairs={{0,128},{1,129},{2,130},{3,131},{4,132},{5,133},{6,134},{7,135},{8... | collective-permute-start | bytes 1228808 | tf_op jit(solution)/shard_map/ppermute | solution.py:307
  12.9 2.3 %collective-permute-start = (f32[176,128]{1,0:T(8,128)S(1)}, f32[176,128]{1,0:T(8,128)S(1)}, u32[]{:S(2)}, u32[]{:S(2)}) collective-permute-start(f32[176,128]{1,0:T(8,128)S(1)} %get-tuple-element.13), channel_id=1, source_target_pairs={{0,1},{1,2},{2,3},{3,4},{4,5},{5,6},{6,7},{7,8},{8,9},{9,10},{10,1... | collective-permute-start | bytes 270344 | tf_op jit(solution)/shard_map/ppermute | solution.py:295
  15.4 1.3 %collective-permute-done.left_ref = f32[176,128]{1,0:T(8,128)S(1)} collective-permute-done((f32[176,128]{1,0:T(8,128)S(1)}, f32[176,128]{1,0:T(8,128)S(1)}, u32[]{:S(2)}, u32[]{:S(2)}) %collective-permute-start) | collective-permute-done | bytes 90144 | tf_op jit(solution)/shard_map/ppermute | solution.py:295
  16.7 2.8 %collective-permute-done.1.right_ref = f32[176,128]{1,0:T(8,128)S(1)} collective-permute-done((f32[176,128]{1,0:T(8,128)S(1)}, f32[176,128]{1,0:T(8,128)S(1)}, u32[]{:S(2)}, u32[]{:S(2)}) %collective-permute-start.1) | collective-permute-done | bytes 90144 | tf_op jit(solution)/shard_map/ppermute | solution.py:296
  20.2 1.3 %collective-permute-start.2 = (f32[20,8,128]{2,1,0:T(8,128)S(1)}, f32[20,8,128]{2,1,0:T(8,128)S(1)}, u32[]{:S(2)}, u32[]{:S(2)}) collective-permute-start(f32[20,8,128]{2,1,0:T(8,128)S(1)} %get-tuple-element.15), channel_id=1, source_target_pairs={{0,64},{192,128},{1,65},{193,129},{2,66},{194,130},{3,67},{195,131... | collective-permute-start | bytes 245768 | tf_op jit(solution)/shard_map/ppermute | solution.py:313
  21.5 22.3 %collective-permute-done.2.msg_ref.high_ref.low_ref = f32[20,8,128]{2,1,0:T(8,128)S(1)} collective-permute-done((f32[20,8,128]{2,1,0:T(8,128)S(1)}, f32[20,8,128]{2,1,0:T(8,128)S(1)}, u32[]{:S(2)}, u32[]{:S(2)}) %collective-permute-start.2) | collective-permute-done | bytes 81952 | tf_op jit(solution)/shard_map/ppermute | solution.py:313
  43.8 1.2 %shard_map.134 = f32[30,8,128]{2,1,0:T(8,128)} custom-call(s32[3]{0:T(128)S(1)} %pad_add_fusion.pos_ref, f32[8]{0:T(128)S(1)} %copy-done.19, f32[20,8,128]{2,1,0:T(8,128)S(1)} %collective-permute-done.2.msg_ref.high_ref.low_ref, f32[10,8,8,128]{3,2,1,0:T(8,128)S(1)} %get-tuple-element.16.r_ref, f32[10,10,8,8,128]{4,3,2,1,0:T(8,128)S(1)} %copy-done.1, ...), custom_call_target="tpu_custom_call" | custom-call | flops 5000000 | bytes 2000000 | tf_op jit(solution)/shard_map/pallas_call | solution.py:314
  45.0 1.3 %collective-permute-start.3 = (f32[30,8,128]{2,1,0:T(8,128)}, f32[30,8,128]{2,1,0:T(8,128)}, u32[]{:S(2)}, u32[]{:S(2)}) collective-permute-start(f32[30,8,128]{2,1,0:T(8,128)} %shard_map.134), channel_id=1, source_target_pairs={{64,128},{65,129},{66,130},{67,131},{68,132},{69,133},{70,134},{71... | collective-permute-start | bytes 368648 | tf_op jit(solution)/shard_map/ppermute | solution.py:317
  50.5 1.7 %shard_map.136.pw_ref = f32[576,88]{1,0:T(8,128)S(1)} custom-call(s32[1]{0:T(128)S(6)} %copy.19.count_ref, f32[256,80]{1,0:T(8,128)S(1)} %copy-done.14, s32[256,1]{1,0:T(8,128)S(1)} %copy.17.owner_ref, s32[256,1]{1,0:T(8,128)S(1)} %copy-done.13), custom_call_target="tpu_custom_call" | custom-call | flops 50000000 | bytes 1000000 | tf_op jit(solution)/shard_map/pallas_call | solution.py:319
  52.3 1.9 %copy-done.3 = f32[10,10,8,8,128]{4,3,2,1,0:T(8,128)S(1)} copy-done((f32[10,10,8,8,128]{4,3,2,1,0:T(8,128)S(1)}, f32[10,10,8,8,128]{4,3,2,1,0:T(8,128)}, u32[]{:S(2)}) %copy-start.3) | copy-done | bytes 3276824
  54.2 1.9 %copy-done.6 = f32[10,10,8,8,128]{4,3,2,1,0:T(8,128)S(1)} copy-done((f32[10,10,8,8,128]{4,3,2,1,0:T(8,128)S(1)}, f32[10,10,8,8,128]{4,3,2,1,0:T(8,128)}, u32[]{:S(2)}) %copy-start.6) | copy-done | bytes 3276824
  56.1 1.0 copy-done.9
  57.1 4.0 %shard_map.137 = (f32[10,8,128]{2,1,0:T(8,128)}, f32[10,8,128]{2,1,0:T(8,128)S(1)}, f32[10,8,128]{2,1,0:T(8,128)}, f32[10,8,128]{2,1,0:T(8,128)S(1)}, f32[576,128]{1,0:T(8,128)S(1)}) custom-call(s32[3]{0:T(128)S(1)} %pad_add_fusion.pos_ref, f32[8]{0:T(128)S(1)} %copy-done.20, f32[30,8,128]{2,1,0:T(8,128)} %collective-permute-done.3.low_ref.mid_ref, ...), custom_call_target="tpu_custom_call" | custom-call | flops 20000000 | bytes 3000000 | tf_op jit(solution)/shard_map/pallas_call | solution.py:323
  62.4 1.8 %all_to_all.7 = f32[64,9,128]{2,1,0:T(8,128)} reshape(f32[576,128]{1,0:T(8,128)} %copy-done.17) | data formatting | bytes 589824 | tf_op jit(solution)/shard_map/all_to_all | solution.py:330
  64.2 13.4 %all-to-all-start = ((f32[64,9,128]{2,1,0:T(8,128)}), f32[64,9,128]{2,1,0:T(8,128)}, u32[]{:S(2)}, u32[]{:S(2)}) async-start(f32[64,9,128]{2,1,0:T(8,128)} %all_to_all.7), calls=%async_computation | async-start | bytes 1048576 | tf_op jit(solution)/shard_map/all_to_all | solution.py:330
  77.6 1.3 %collective-permute-start.7 = (f32[10,8,128]{2,1,0:T(8,128)}, f32[10,8,128]{2,1,0:T(8,128)S(1)}, u32[]{:S(2)}, u32[]{:S(2)}) collective-permute-start(f32[10,8,128]{2,1,0:T(8,128)} %get-tuple-element.19), channel_id=1, source_target_pairs={{128,192},{129,193},{130,194},{131,195},{132,196},{133,197},{134,1... | collective-permute-start | bytes 122888 | tf_op jit(solution)/shard_map/ppermute | solution.py:327
  78.9 2.5 %collective-permute-start.8 = (f32[10,8,128]{2,1,0:T(8,128)}, f32[10,8,128]{2,1,0:T(8,128)S(1)}, u32[]{:S(2)}, u32[]{:S(2)}) collective-permute-start(f32[10,8,128]{2,1,0:T(8,128)} %get-tuple-element.21), channel_id=1, source_target_pairs={{128,64},{129,65},{130,66},{131,67},{132,68},{133,69},{134,70},{13... | collective-permute-start | bytes 122888 | tf_op jit(solution)/shard_map/ppermute | solution.py:328
  81.4 1.3 %collective-permute-start.9 = (f32[10,8,128]{2,1,0:T(8,128)}, f32[10,8,128]{2,1,0:T(8,128)S(1)}, u32[]{:S(2)}, u32[]{:S(2)}) collective-permute-start(f32[10,8,128]{2,1,0:T(8,128)} %copy-done.21), channel_id=1, source_target_pairs={{128,0},{129,1},{130,2},{131,3},{132,4},{133,5},{134,6},{135,7},{1... | collective-permute-start | bytes 122888 | tf_op jit(solution)/shard_map/ppermute | solution.py:329
  82.7 12.0 %all-to-all-done = f32[64,9,128]{2,1,0:T(8,128)} async-done(((f32[64,9,128]{2,1,0:T(8,128)}), f32[64,9,128]{2,1,0:T(8,128)}, u32[]{:S(2)}, u32[]{:S(2)}) %all-to-all-start) | async-done | bytes 294944 | tf_op jit(solution)/shard_map/all_to_all | solution.py:330
  94.7 1.8 %all_to_all.9.got_ref = f32[576,128]{1,0:T(8,128)} reshape(f32[64,9,128]{2,1,0:T(8,128)} %all-to-all-done) | data formatting | bytes 589824 | tf_op jit(solution)/shard_map/all_to_all | solution.py:330
  98.1 1.3 %collective-permute-start.10 = (f32[64,128]{1,0:T(8,128)S(1)}, f32[64,128]{1,0:T(8,128)S(1)}, u32[]{:S(2)}, u32[]{:S(2)}) collective-permute-start(f32[64,128]{1,0:T(8,128)S(1)} %broadcast_select_fusion), channel_id=1, source_target_pairs={{128,0},{129,1},{130,2},{131,3},{132,4},{133,5},{134,6},{135,7},{1... | collective-permute-start | bytes 98312 | tf_op jit(solution)/shard_map/ppermute | solution.py:339
  99.4 2.5 %collective-permute-start.11 = (f32[64,128]{1,0:T(8,128)S(1)}, f32[64,128]{1,0:T(8,128)S(1)}, u32[]{:S(2)}, u32[]{:S(2)}) collective-permute-start(f32[64,128]{1,0:T(8,128)S(1)} %broadcast_select_fusion), channel_id=1, source_target_pairs={{128,64},{129,65},{130,66},{131,67},{132,68},{133,69},{134,70},{13... | collective-permute-start | bytes 98312 | tf_op jit(solution)/shard_map/ppermute | solution.py:339
  102.0 1.3 %collective-permute-start.12 = (f32[64,128]{1,0:T(8,128)S(1)}, f32[64,128]{1,0:T(8,128)S(1)}, u32[]{:S(2)}, u32[]{:S(2)}) collective-permute-start(f32[64,128]{1,0:T(8,128)S(1)} %broadcast_select_fusion), channel_id=1, source_target_pairs={{128,192},{129,193},{130,194},{131,195},{132,196},{133,197},{134,1... | collective-permute-start | bytes 98312 | tf_op jit(solution)/shard_map/ppermute | solution.py:339
  103.3 1.9 %copy-done.4 = f32[10,10,8,8,128]{4,3,2,1,0:T(8,128)S(1)} copy-done((f32[10,10,8,8,128]{4,3,2,1,0:T(8,128)S(1)}, f32[10,10,8,8,128]{4,3,2,1,0:T(8,128)}, u32[]{:S(2)}) %copy-start.4) | copy-done | bytes 3276824
  105.2 1.9 %copy-done.7 = f32[10,10,8,8,128]{4,3,2,1,0:T(8,128)S(1)} copy-done((f32[10,10,8,8,128]{4,3,2,1,0:T(8,128)S(1)}, f32[10,10,8,8,128]{4,3,2,1,0:T(8,128)}, u32[]{:S(2)}) %copy-start.7) | copy-done | bytes 3276824
  108.1 2.8 %shard_map.138 = f32[10,8,8,128]{3,2,1,0:T(8,128)} custom-call(s32[3]{0:T(128)S(1)} %pad_add_fusion.pos_ref, f32[20,8,128]{2,1,0:T(8,128)S(1)} %collective-permute-done.2.msg_ref.high_ref.low_ref, f32[30,8,128]{2,1,0:T(8,128)} %collective-permute-done.3.low_ref.mid_ref, f32[10,8,128]{2,1,0:T(8,128)S(1)} %collective-permute-done.7.x3_ref, ...), custom_call_target="tpu_custom_call" | custom-call | flops 5000000 | bytes 2000000 | tf_op jit(solution)/shard_map/pallas_call | solution.py:331
  (63 shorter events, 9.9 us)
Async XLA Ops:
  0.7 1.9 %copy-start = (f32[10,10,8,8,128]{4,3,2,1,0:T(8,128)S(1)}, f32[10,10,8,8,128]{4,3,2,1,0:T(8,128)}, u32[]{:S(2)}) copy-start(f32[10,10,8,8,128]{4,3,2,1,0:T(8,128)} %l_ref.9) | copy-start | bytes 9830404
  2.6 1.9 %copy-start.2 = (f32[10,10,8,8,128]{4,3,2,1,0:T(8,128)S(1)}, f32[10,10,8,8,128]{4,3,2,1,0:T(8,128)}, u32[]{:S(2)}) copy-start(f32[10,10,8,8,128]{4,3,2,1,0:T(8,128)} %d_ref.9) | copy-start | bytes 9830404
  4.6 1.9 %copy-start.5 = (f32[10,10,8,8,128]{4,3,2,1,0:T(8,128)S(1)}, f32[10,10,8,8,128]{4,3,2,1,0:T(8,128)}, u32[]{:S(2)}) copy-start(f32[10,10,8,8,128]{4,3,2,1,0:T(8,128)} %u_ref.9) | copy-start | bytes 9830404
  7.1 5.6 %copy-start.11 = (f32[10,8,8,128]{3,2,1,0:T(8,128)S(1)}, f32[10,8,8,128]{3,2,1,0:T(8,128)}, u32[]{:S(2)}) copy-start(f32[10,8,8,128]{3,2,1,0:T(8,128)} %a_ref.3) | copy-start | bytes 983044
  7.2 5.6 %copy-start.16 = (f32[8,8,128]{2,1,0:T(8,128)S(1)}, f32[8,8,128]{2,1,0:T(8,128)}, u32[]{:S(2)}) copy-start(f32[8,8,128]{2,1,0:T(8,128)} %rad_ref.5) | copy-start | bytes 98308
  7.2 8.0 %copy-start.15 = (f32[10,8,8,128]{3,2,1,0:T(8,128)S(1)}, f32[10,8,8,128]{3,2,1,0:T(8,128)}, u32[]{:S(2)}) copy-start(f32[10,8,8,128]{3,2,1,0:T(8,128)} %src_ref.1) | copy-start | bytes 983044
  7.2 8.0 %copy-start.18 = (f32[8,8,128]{2,1,0:T(8,128)S(1)}, f32[8,8,128]{2,1,0:T(8,128)}, u32[]{:S(2)}) copy-start(f32[8,8,128]{2,1,0:T(8,128)} %frq_ref.1) | copy-start | bytes 98308
  7.2 12.3 %copy-start.1 = (f32[10,10,8,8,128]{4,3,2,1,0:T(8,128)S(1)}, f32[10,10,8,8,128]{4,3,2,1,0:T(8,128)}, u32[]{:S(2)}) copy-start(f32[10,10,8,8,128]{4,3,2,1,0:T(8,128)} %l_ref.9) | copy-start | bytes 9830404
  8.8 43.5 %collective-permute-start.4 = (f32[20,10,8,128]{3,2,1,0:T(8,128)}, f32[20,10,8,128]{3,2,1,0:T(8,128)}, u32[]{:S(2)}, u32[]{:S(2)}) collective-permute-start(f32[20,10,8,128]{3,2,1,0:T(8,128)} %get-tuple-element.17), channel_id=1, source_target_pairs={{64,128},{65,129},{66,130},{67,131},{68,132},{69,133},{70,134},{71... | collective-permute-start | bytes 2457608 | tf_op jit(solution)/shard_map/ppermute | solution.py:305
  10.2 42.1 %collective-permute-start.5 = (f32[20,10,8,128]{3,2,1,0:T(8,128)}, f32[20,10,8,128]{3,2,1,0:T(8,128)}, u32[]{:S(2)}, u32[]{:S(2)}) collective-permute-start(f32[20,10,8,128]{3,2,1,0:T(8,128)} %get-tuple-element.17), channel_id=1, source_target_pairs={{192,128},{193,129},{194,130},{195,131},{196,132},{197,133},{198,1... | collective-permute-start | bytes 2457608 | tf_op jit(solution)/shard_map/ppermute | solution.py:306
  11.5 40.8 %collective-permute-start.6 = (f32[10,10,8,128]{3,2,1,0:T(8,128)}, f32[10,10,8,128]{3,2,1,0:T(8,128)}, u32[]{:S(2)}, u32[]{:S(2)}) collective-permute-start(f32[10,10,8,128]{3,2,1,0:T(8,128)} %get-tuple-element.18), channel_id=1, source_target_pairs={{0,128},{1,129},{2,130},{3,131},{4,132},{5,133},{6,134},{7,135},{8... | collective-permute-start | bytes 1228808 | tf_op jit(solution)/shard_map/ppermute | solution.py:307
  12.9 3.8 %collective-permute-start = (f32[176,128]{1,0:T(8,128)S(1)}, f32[176,128]{1,0:T(8,128)S(1)}, u32[]{:S(2)}, u32[]{:S(2)}) collective-permute-start(f32[176,128]{1,0:T(8,128)S(1)} %get-tuple-element.13), channel_id=1, source_target_pairs={{0,1},{1,2},{2,3},{3,4},{4,5},{5,6},{6,7},{7,8},{8,9},{9,10},{10,1... | collective-permute-start | bytes 270344 | tf_op jit(solution)/shard_map/ppermute | solution.py:295
  15.1 4.4 %collective-permute-start.1 = (f32[176,128]{1,0:T(8,128)S(1)}, f32[176,128]{1,0:T(8,128)S(1)}, u32[]{:S(2)}, u32[]{:S(2)}) collective-permute-start(f32[176,128]{1,0:T(8,128)S(1)} %get-tuple-element.14), channel_id=1, source_target_pairs={{1,0},{2,1},{3,2},{4,3},{5,4},{6,5},{7,6},{8,7},{9,8},{10,9},{11,1... | collective-permute-start | bytes 270344 | tf_op jit(solution)/shard_map/ppermute | solution.py:296
  20.2 24.8 %copy-start.8 = (f32[10,8,8,128]{3,2,1,0:T(8,128)}, f32[10,8,8,128]{3,2,1,0:T(8,128)S(1)}, u32[]{:S(2)}) copy-start(f32[10,8,8,128]{3,2,1,0:T(8,128)S(1)} %get-tuple-element.16.r_ref) | copy-start | bytes 983044
  20.2 23.6 %collective-permute-start.2 = (f32[20,8,128]{2,1,0:T(8,128)S(1)}, f32[20,8,128]{2,1,0:T(8,128)S(1)}, u32[]{:S(2)}, u32[]{:S(2)}) collective-permute-start(f32[20,8,128]{2,1,0:T(8,128)S(1)} %get-tuple-element.15), channel_id=1, source_target_pairs={{0,64},{192,128},{1,65},{193,129},{2,66},{194,130},{3,67},{195,131... | collective-permute-start | bytes 245768 | tf_op jit(solution)/shard_map/ppermute | solution.py:313
  43.8 2.5 %copy-start.22 = (f32[256,10,8]{0,2,1:T(8,128)S(1)}, f32[256,10,8]{0,2,1:T(8,128)}, u32[]{:S(2)}) copy-start(f32[256,10,8]{0,2,1:T(8,128)} %param.20) | copy-start | bytes 245764
  43.8 3.3 %copy-start.23 = (s32[256,1]{0,1:T(1,128)S(1)}, s32[256,1]{0,1:T(1,128)}, u32[]{:S(2)}) copy-start(s32[256,1]{0,1:T(1,128)} %param.21) | copy-start | bytes 3076
  43.8 3.4 %copy-start.24 = (s32[256]{0:T(256)S(1)}, s32[256]{0:T(256)}, u32[]{:S(2)}) copy-start(s32[256]{0:T(256)} %param.22) | copy-start | bytes 3076
  43.8 8.5 %copy-start.20 = (f32[8]{0:T(128)S(1)}, f32[8]{0:T(128)}, u32[]{:S(2)}) copy-start(f32[8]{0:T(128)} %w_ref.7) | copy-start | bytes 100
  45.0 7.2 %collective-permute-start.3 = (f32[30,8,128]{2,1,0:T(8,128)}, f32[30,8,128]{2,1,0:T(8,128)}, u32[]{:S(2)}, u32[]{:S(2)}) collective-permute-start(f32[30,8,128]{2,1,0:T(8,128)} %shard_map.134), channel_id=1, source_target_pairs={{64,128},{65,129},{66,130},{67,131},{68,132},{69,133},{70,134},{71... | collective-permute-start | bytes 368648 | tf_op jit(solution)/shard_map/ppermute | solution.py:317
  52.3 1.9 %copy-start.3 = (f32[10,10,8,8,128]{4,3,2,1,0:T(8,128)S(1)}, f32[10,10,8,8,128]{4,3,2,1,0:T(8,128)}, u32[]{:S(2)}) copy-start(f32[10,10,8,8,128]{4,3,2,1,0:T(8,128)} %d_ref.9) | copy-start | bytes 9830404
  54.2 1.9 %copy-start.6 = (f32[10,10,8,8,128]{4,3,2,1,0:T(8,128)S(1)}, f32[10,10,8,8,128]{4,3,2,1,0:T(8,128)}, u32[]{:S(2)}) copy-start(f32[10,10,8,8,128]{4,3,2,1,0:T(8,128)} %u_ref.9) | copy-start | bytes 9830404
  56.1 1.0 copy-start.9
  64.2 30.5 %all-to-all-start = ((f32[64,9,128]{2,1,0:T(8,128)}), f32[64,9,128]{2,1,0:T(8,128)}, u32[]{:S(2)}, u32[]{:S(2)}) async-start(f32[64,9,128]{2,1,0:T(8,128)} %all_to_all.7), calls=%async_computation | async-start | bytes 1048576 | tf_op jit(solution)/shard_map/all_to_all | solution.py:330
  77.6 24.3 %collective-permute-start.7 = (f32[10,8,128]{2,1,0:T(8,128)}, f32[10,8,128]{2,1,0:T(8,128)S(1)}, u32[]{:S(2)}, u32[]{:S(2)}) collective-permute-start(f32[10,8,128]{2,1,0:T(8,128)} %get-tuple-element.19), channel_id=1, source_target_pairs={{128,192},{129,193},{130,194},{131,195},{132,196},{133,197},{134,1... | collective-permute-start | bytes 122888 | tf_op jit(solution)/shard_map/ppermute | solution.py:327
  78.9 24.4 %collective-permute-start.8 = (f32[10,8,128]{2,1,0:T(8,128)}, f32[10,8,128]{2,1,0:T(8,128)S(1)}, u32[]{:S(2)}, u32[]{:S(2)}) collective-permute-start(f32[10,8,128]{2,1,0:T(8,128)} %get-tuple-element.21), channel_id=1, source_target_pairs={{128,64},{129,65},{130,66},{131,67},{132,68},{133,69},{134,70},{13... | collective-permute-start | bytes 122888 | tf_op jit(solution)/shard_map/ppermute | solution.py:328
  81.4 21.9 %collective-permute-start.9 = (f32[10,8,128]{2,1,0:T(8,128)}, f32[10,8,128]{2,1,0:T(8,128)S(1)}, u32[]{:S(2)}, u32[]{:S(2)}) collective-permute-start(f32[10,8,128]{2,1,0:T(8,128)} %copy-done.21), channel_id=1, source_target_pairs={{128,0},{129,1},{130,2},{131,3},{132,4},{133,5},{134,6},{135,7},{1... | collective-permute-start | bytes 122888 | tf_op jit(solution)/shard_map/ppermute | solution.py:329
  98.1 12.8 %collective-permute-start.10 = (f32[64,128]{1,0:T(8,128)S(1)}, f32[64,128]{1,0:T(8,128)S(1)}, u32[]{:S(2)}, u32[]{:S(2)}) collective-permute-start(f32[64,128]{1,0:T(8,128)S(1)} %broadcast_select_fusion), channel_id=1, source_target_pairs={{128,0},{129,1},{130,2},{131,3},{132,4},{133,5},{134,6},{135,7},{1... | collective-permute-start | bytes 98312 | tf_op jit(solution)/shard_map/ppermute | solution.py:339
  99.4 11.5 %collective-permute-start.11 = (f32[64,128]{1,0:T(8,128)S(1)}, f32[64,128]{1,0:T(8,128)S(1)}, u32[]{:S(2)}, u32[]{:S(2)}) collective-permute-start(f32[64,128]{1,0:T(8,128)S(1)} %broadcast_select_fusion), channel_id=1, source_target_pairs={{128,64},{129,65},{130,66},{131,67},{132,68},{133,69},{134,70},{13... | collective-permute-start | bytes 98312 | tf_op jit(solution)/shard_map/ppermute | solution.py:339
  102.0 9.0 %collective-permute-start.12 = (f32[64,128]{1,0:T(8,128)S(1)}, f32[64,128]{1,0:T(8,128)S(1)}, u32[]{:S(2)}, u32[]{:S(2)}) collective-permute-start(f32[64,128]{1,0:T(8,128)S(1)} %broadcast_select_fusion), channel_id=1, source_target_pairs={{128,192},{129,193},{130,194},{131,195},{132,196},{133,197},{134,1... | collective-permute-start | bytes 98312 | tf_op jit(solution)/shard_map/ppermute | solution.py:339
  103.3 1.9 %copy-start.4 = (f32[10,10,8,8,128]{4,3,2,1,0:T(8,128)S(1)}, f32[10,10,8,8,128]{4,3,2,1,0:T(8,128)}, u32[]{:S(2)}) copy-start(f32[10,10,8,8,128]{4,3,2,1,0:T(8,128)} %d_ref.9) | copy-start | bytes 9830404
  105.2 1.9 %copy-start.7 = (f32[10,10,8,8,128]{4,3,2,1,0:T(8,128)S(1)}, f32[10,10,8,8,128]{4,3,2,1,0:T(8,128)}, u32[]{:S(2)}) copy-start(f32[10,10,8,8,128]{4,3,2,1,0:T(8,128)} %u_ref.9) | copy-start | bytes 9830404
  (7 other events, 5.7 us)

commit v2 on v1

--- a/solution.py
+++ b/solution.py
@@ -17,23 +17,38 @@
 
 VM = pl.BlockSpec(memory_space=pltpu.VMEM)
 SM = pl.BlockSpec(memory_space=pltpu.SMEM)
+HB = pl.BlockSpec(memory_space=pltpu.HBM)
 
 
 def f32(*shape):
     return jax.ShapeDtypeStruct(shape, F32)
 
 
-def call(body, out_shape, n_in, smem=(), scratch=(), flops=0, nbytes=0):
+def held(*shape):
+    return pltpu.VMEM(shape, F32)
+
+
+def away(*shape):
+    return pltpu.HBM(shape, F32)
+
+
+def far_off(x):
+    return pltpu.with_memory_space_constraint(x, pltpu.HBM)
+
+
+def call(name, body, out_shape, n_in, smem=(), far=(), scratch=(), flops=0, nbytes=0):
     single = not isinstance(out_shape, (tuple, list))
-    return pl.pallas_call(
+    run = pl.pallas_call(
         body,
+        name=name,
         out_shape=out_shape,
-        in_specs=[SM if i in smem else VM for i in range(n_in)],
+        in_specs=[SM if i in smem else HB if i in far else VM for i in range(n_in)],
         out_specs=VM if single else [VM] * len(out_shape),
         scratch_shapes=list(scratch),
-        compiler_params=pltpu.CompilerParams(vmem_limit_bytes=40 * 1024 * 1024),
+        compiler_params=pltpu.CompilerParams(vmem_limit_bytes=12 * 1024 * 1024),
         cost_estimate=pl.CostEstimate(flops=flops, bytes_accessed=nbytes, transcendentals=0),
     )
+    return run
 
 
 def block_dot(m_ref, k, x):
@@ -82,7 +97,36 @@
             hi_ref[at : at + 2, :] = cell[6:8]
 
 
-def interior_kernel(a_ref, src_ref, rad_ref, frq_ref, out_ref):
+def pair_dot(m_ref, k, xs):
+    accs = [None] * len(xs)
+    for j in range(NV):
+        m = m_ref[:, j, k]
+        for n, x in enumerate(xs):
+            term = m * x[j][None]
+            accs[n] = term if accs[n] is None else accs[n] + term
+    return accs
+
+
+def back_map(u_ref, w_ref, s_ref, cols):
+    xs = [u_ref[:, c, K - 1] for c in cols]
+    for n, x in enumerate(xs):
+        s_ref[K - 1, n] = x
+    for k in range(K - 2, -1, -1):
+        xs = pair_dot(u_ref, k, xs)
+        for n, x in enumerate(xs):
+            s_ref[k, n] = x
+    sums = []
+    for n in range(len(cols)):
+        total = None
+        for k in range(K):
+            weight = w_ref[k] if (K - k) % 2 == 0 else -w_ref[k]
+            term = s_ref[k, n] * weight
+            total = term if total is None else total + term
+        sums.append(total)
+    return sums
+
+
+def interior(a_ref, src_ref, rad_ref, frq_ref, out_ref):
     row = lax.broadcasted_iota(jnp.int32, (H, S), 0)
     lane = lax.broadcasted_iota(jnp.int32, (H, S), 1)
     for k in range(K):
@@ -105,32 +149,39 @@
         out_ref[half:, k] = src[half:] - frq * a[:half]
 
 
-def maps_kernel(pos_ref, w_ref, l_ref, d_ref, u_ref, ab_ref, q_ref, s_ref):
+def start_kernel(
+    pos_ref, w_in, a_in, src_in, rad_in, frq_in, l_in, d_in, u_in,
+    l_ref, d_ref, u_ref, r_ref, w_ref, ab_ref, q_ref, a_ref, src_ref, rad_ref, frq_ref, s_ref, sems,
+):
     wall = pos_ref[0]
-
-    def pair_dot(m_ref, k, xs):
-        accs = [None] * len(xs)
-        for j in range(NV):
-            m = m_ref[:, j, k]
-            for n, x in enumerate(xs):
-                term = m * x[j][None]
-                accs[n] = term if accs[n] is None else accs[n] + term
-        return accs
+    pairs = (
+        (a_in, a_ref), (src_in, src_ref), (rad_in, rad_ref), (frq_in, frq_ref),
+        (l_in, l_ref), (d_in, d_ref), (u_in, u_ref),
+    )
+    copies = [pltpu.make_async_copy(out_there, here, sems.at[n]) for n, (out_there, here) in enumerate(pairs)]
+    state, (lower, diag, upper) = copies[:4], copies[4:]
+    for copy in state + [upper, lower, diag]:
+        copy.start()
+    for k in range(K):
+        w_ref[k] = jnp.broadcast_to(w_in[:, k : k + 1], (H, S))
+    for copy in state:
+        copy.wait()
+    interior(a_ref, src_ref, rad_ref, frq_ref, r_ref)
+    upper.wait()
 
     @pl.when(wall <= 1)
     def _():
         @pl.loop(0, NV // 2)
         def _(pair):
             cols = [2 * pair, 2 * pair + 1]
-            bs = [-u_ref[:, c, K - 1] for c in cols]
-            ps = [b * w_ref[K - 1] for b in bs]
-            for k in range(K - 2, -1, -1):
-                bs = [-b for b in pair_dot(u_ref, k, bs)]
-                ps = [p + b * w_ref[k] for p, b in zip(ps, bs)]
-            for c, b, p in zip(cols, bs, ps):
-                ab_ref[c] = b
-                ab_ref[NV + c] = p
-                q_ref[c] = p
+            sums = back_map(u_ref, w_ref, s_ref, cols)
+            for n, c in enumerate(cols):
+                ab_ref[c] = s_ref[0, n]
+                ab_ref[NV + c] = sums[n]
+                q_ref[c] = sums[n]
+
+    lower.wait()
+    diag.wait()
 
     @pl.when(wall == 3)
     def _():
@@ -144,13 +195,16 @@
                 for n, s in enumerate(pair_dot(d_ref, k, gs)):
                     s_ref[k, n] = s
             cs = [s_ref[K - 1, n] for n in range(2)]
-            ps = [c * w_ref[K - 1] for c in cs]
             for k in range(K - 2, -1, -1):
                 cs = [s_ref[k, n] - c for n, c in enumerate(pair_dot(u_ref, k, cs))]
-                ps = [p + c * w_ref[k] for p, c in zip(ps, cs)]
-            for col, c, p in zip(cols, cs, ps):
-                ab_ref[col] = c
-                ab_ref[NV + col] = p
+                for n, c in enumerate(cs):
+                    s_ref[k, n] = c
+            for n, col in enumerate(cols):
+                ab_ref[col] = s_ref[0, n]
+                total = s_ref[0, n] * w_ref[0]
+                for k in range(1, K):
+                    total = total + s_ref[k, n] * w_ref[k]
+                ab_ref[NV + col] = total
 
 
 def residual_kernel(pos_ref, w_ref, r_ref, left_ref, right_ref, rad_ref, l_ref, d_ref, u_ref, out_ref, msg_ref, s_ref):
@@ -238,27 +292,26 @@
 
 
 def place_kernel(count_ref, w_ref, owner_ref, tag_ref, out_ref):
-    blocks = owner_ref.shape[0]
+    blocks = owner_ref.shape[1]
     owners = out_ref.shape[0] // ROWS_PER_OWNER
     owner = owner_ref[...]
-    index = lax.broadcasted_iota(jnp.int32, (blocks, 1), 0)
-    live = index < count_ref[0]
-    hits = (owner == lax.broadcasted_iota(jnp.int32, (blocks, owners), 1)).astype(F32)
-    earlier = lax.broadcasted_iota(jnp.int32, (blocks, blocks), 1) < lax.broadcasted_iota(jnp.int32, (blocks, blocks), 0)
-    before = jnp.dot(earlier.astype(F32), hits, preferred_element_type=F32)
-    slot = jnp.sum(before * hits, axis=1, keepdims=True).astype(jnp.int32)
-    column = lax.broadcasted_iota(jnp.int32, (blocks, owners * ROWS_PER_OWNER), 1)
-    placed = ((owner * ROWS_PER_OWNER + slot == column) & live).astype(F32)
-    tagged = ((owner * ROWS_PER_OWNER + SLOTS == column) & live).astype(F32)
+    live = lax.broadcasted_iota(jnp.int32, (1, blocks), 1) < count_ref[0]
+    hits = (owner == lax.broadcasted_iota(jnp.int32, (owners, blocks), 0)).astype(F32)
+    earlier = lax.broadcasted_iota(jnp.int32, (blocks, blocks), 0) < lax.broadcasted_iota(jnp.int32, (blocks, blocks), 1)
+    before = jnp.dot(hits, earlier.astype(F32), preferred_element_type=F32)
+    slot = jnp.sum(before * hits, axis=0, keepdims=True).astype(jnp.int32)
+    row = lax.broadcasted_iota(jnp.int32, (owners * ROWS_PER_OWNER, blocks), 0)
+    placed = ((owner * ROWS_PER_OWNER + slot == row) & live).astype(F32)
+    tagged = ((owner * ROWS_PER_OWNER + SLOTS == row) & live).astype(F32)
     width = NV * H
-    lanes = lax.broadcasted_iota(jnp.int32, (blocks, SLOTS), 1)
+    lanes = lax.broadcasted_iota(jnp.int32, (SLOTS, blocks), 0)
     tags = jnp.where(lanes == slot, (tag_ref[...] + 1).astype(F32), 0.0)
-    dims = (((0,), (0,)), ((), ()))
+    dims = (((1,), (1,)), ((), ()))
     out_ref[:, :width] = lax.dot_general(placed, w_ref[...], dims, precision=highest, preferred_element_type=F32)
     out_ref[:, width:] = lax.dot_general(tagged, tags, dims, precision=highest, preferred_element_type=F32)
 
 
-def pick_kernel(got_ref, out_ref):
+def pick_kernel(pos_ref, got_ref, out_ref):
     rows = got_ref.shape[0]
     sources = rows // ROWS_PER_OWNER
     tag_rows = got_ref[pl.ds(SLOTS, sources, stride=ROWS_PER_OWNER), :]
@@ -277,7 +330,8 @@
     tag = jnp.sum(jnp.where(mine, wide, 0.0), axis=0, keepdims=True)
     target = (lax.broadcasted_iota(jnp.int32, (PATCH_DEV, rows), 0) + 1).astype(F32)
     picker = (tag == target).astype(F32)
-    out_ref[...] = jnp.dot(picker, got_ref[...], precision=highest, preferred_element_type=F32)
+    sums = jnp.dot(picker, got_ref[...], precision=highest, preferred_element_type=F32)
+    out_ref[...] = jnp.where(pos_ref[0] == 2, sums, 0.0)
 
 
 def on_device(
@@ -285,55 +339,62 @@
     surface_weight, patch_owner, patch_row, surface_count,
 ):
     tiles = lax.axis_size("tile")
+    tie = lax.optimization_barrier
     pos = jnp.stack([lax.axis_index("wall"), lax.axis_index("tile"), jnp.int32(tiles - 1)]).astype(jnp.int32)
-    vm = lambda x: pltpu.with_memory_space_constraint(x, pltpu.VMEM)
-    lower, diag, upper = vm(lower), vm(diag), vm(upper)
-    vec = f32(NV, H, S)
     levels = pltpu.VMEM((K, NV, H, S), F32)
-
-    lo, hi = call(pack_kernel, (f32(22 * K, S), f32(22 * K, S)), 2, nbytes=800_000)(adjoint, radius)
+    pair_levels = pltpu.VMEM((K, 2, NV, H, S), F32)
+    block, state, cell = held(NV, NV, K, H, S), held(NV, K, H, S), held(K, H, S)
+    adjoint, source, radius, frequency, lower, diag, upper = (
+        far_off(x) for x in (adjoint, source, radius, frequency, lower, diag, upper)
+    )
+
+    lo, hi = call("pack", pack_kernel, (f32(22 * K, S), f32(22 * K, S)), 2, nbytes=800_000)(adjoint, radius)
     left = lax.ppermute(hi, "tile", [(i, (i + 1) % tiles) for i in range(tiles)])
     right = lax.ppermute(lo, "tile", [((i + 1) % tiles, i) for i in range(tiles)])
 
-    inner = call(interior_kernel, f32(NV, K, H, S), 4, flops=4_000_000, nbytes=1_200_000)(
-        adjoint, source, radius, frequency
-    )
-    maps, q0 = call(
-        maps_kernel, (f32(2 * NV, NV, H, S), f32(NV, NV, H, S)), 5, smem=(0, 1),
-        scratch=(pltpu.VMEM((K, 2, NV, H, S), F32),), flops=44_000_000, nbytes=11_000_000,
-    )(pos, wall_weight, lower, diag, upper)
+    lo, pos1 = tie((lo, pos))
+    lower, diag, upper, inner, weight, maps, q0 = call(
+        "start", start_kernel, (block, block, block, state, cell, f32(2 * NV, NV, H, S), f32(NV, NV, H, S)), 9, smem=(0,),
+        far=(2, 3, 4, 5, 6, 7, 8), scratch=(state, state, cell, cell, pair_levels, pltpu.SemaphoreType.DMA((7,))),
+        flops=44_000_000, nbytes=11_000_000,
+    )(pos1, wall_weight.reshape(1, K), adjoint, source, radius, frequency, lower, diag, upper)
+    maps, left, right = tie((maps, left, right))
+    map3 = lax.ppermute(maps, "wall", [(3, 2)])
     map1 = lax.ppermute(maps, "wall", [(1, 2)])
-    map3 = lax.ppermute(maps, "wall", [(3, 2)])
-    map0 = lax.ppermute(q0, "wall", [(0, 2)])
+    maps, pos2 = tie((maps, pos))
+    swt = surface_weight.transpose(1, 2, 0).reshape(NV * H, -1)
+    placed = call(
+        "place", place_kernel, held(tiles * ROWS_PER_OWNER, NV * H + SLOTS), 4, smem=(0,), flops=50_000_000, nbytes=1_000_000
+    )(surface_count, swt, patch_owner.reshape(1, -1), patch_row.reshape(1, -1))
 
     resid, first = call(
-        residual_kernel, (f32(NV, K, H, S), f32(2 * NV, H, S)), 9, smem=(0, 1), scratch=(levels,),
+        "residual", residual_kernel, (state, f32(2 * NV, H, S)), 9, smem=(0,), scratch=(levels,),
         flops=6_000_000, nbytes=2_000_000,
-    )(pos, wall_weight, inner, left, right, radius, lower, diag, upper)
+    )(pos2, weight, inner, left, right, radius, lower, diag, upper)
     low = lax.ppermute(first, "wall", [(0, 1), (3, 2)])
     second = call(
-        middle_kernel, f32(3 * NV, H, S), 7, smem=(0, 1), scratch=(levels,), flops=5_000_000, nbytes=2_000_000
-    )(pos, wall_weight, low, resid, lower, diag, upper)
+        "middle", middle_kernel, f32(3 * NV, H, S), 7, smem=(0,), scratch=(levels,), flops=5_000_000, nbytes=2_000_000
+    )(pos, weight, low, resid, lower, diag, upper)
     mid = lax.ppermute(second, "wall", [(1, 2)])
-
-    placed = call(
-        place_kernel, f32(tiles * ROWS_PER_OWNER, NV * H + SLOTS), 4, smem=(0,), flops=50_000_000, nbytes=1_000_000
-    )(surface_count, surface_weight.reshape(-1, NV * H), patch_owner, patch_row.reshape(-1, 1))
-
+    second, q0 = tie((second, q0))
+    map0 = lax.ppermute(q0, "wall", [(0, 2)])
+
+    vec = away(NV, H, S)
     x3, y2, y1, y0, rows = call(
-        decide_kernel, (vec, vec, vec, vec, f32(tiles * ROWS_PER_OWNER, S)), 12, smem=(0, 1),
+        "decide", decide_kernel, (vec, vec, vec, vec, away(tiles * ROWS_PER_OWNER, S)), 12, smem=(0,),
         scratch=(levels, pltpu.VMEM((NV * H + SLOTS, S), F32)), flops=20_000_000, nbytes=3_000_000,
-    )(pos, wall_weight, mid, low, map1, map3, map0, placed, resid, lower, diag, upper)
+    )(pos, weight, mid, low, map1, map3, map0, placed, resid, lower, diag, upper)
+    got = lax.all_to_all(rows.reshape(tiles, ROWS_PER_OWNER, 1, S), "tile", split_axis=0, concat_axis=0)
     x3 = lax.ppermute(x3, "wall", [(2, 3)])
     y1 = lax.ppermute(y1, "wall", [(2, 1)])
     y0 = lax.ppermute(y0, "wall", [(2, 0)])
-    got = lax.all_to_all(rows, "tile", split_axis=0, concat_axis=0, tiled=True)
     adjoint_next = call(
-        finish_kernel, f32(NV, K, H, S), 11, smem=(0,),
+        "finish", finish_kernel, f32(NV, K, H, S), 11, smem=(0,),
         scratch=(levels, pltpu.VMEM((NV, H, S), F32), pltpu.VMEM((NV, H, S), F32)), flops=5_000_000, nbytes=2_000_000,
     )(pos, low, mid, x3, y2, y1, y0, resid, lower, diag, upper)
-    part = call(pick_kernel, f32(PATCH_DEV, S), 1, flops=20_000_000, nbytes=400_000)(got)
-    part = jnp.where(lax.axis_index("wall") == 2, part, 0.0)
+    got, adjoint_next = tie((got, adjoint_next))
+    got = got.reshape(tiles * ROWS_PER_OWNER, S)
+    part = call("pick", pick_kernel, f32(PATCH_DEV, S), 2, smem=(0,), flops=20_000_000, nbytes=400_000)(pos, got)
     patch = part
     for w in (0, 1, 3):
         patch = patch + lax.ppermute(part, "wall", [(2, w)])

time: 112 us -> 99.9 us (0.89)
  the two profiles are of different devices: /device:TPU:23 before, /device:TPU:6 now
where the time goes in v2:
time: 99.9 us; the launch traced here: 99.1 us
  starting transfers between devices  52.9 us (53%)
  waiting for transfers between devices  21.5 us (22%)
  Pallas kernels  16.2 us (16%)
  local copies, waits for them, and re-layouts  6.28 us (6%)
  between operations  1.5 us (2%)
    ppermute x1, starting transfers between devices, on_device(): map0 = lax.ppermute(q0, 'wall', [(0, 2)])  20.1 us
    all_to_all x1, starting transfers between devices, on_device(): lax.all_to_all(rows.reshape(tiles, ROWS_PER_OWNER, 1, S), 'tile', split_a...  14.7 us
    ppermute x1, waiting for transfers between devices, on_device(): y0 = lax.ppermute(y0, 'wall', [(2, 0)])  11.6 us
    unnamed x22, local copies, waits for them, and re-layouts  6.28 us
    ppermute x1, starting transfers between devices, on_device(): lax.ppermute(lo, 'tile', [((i + 1) % tiles, i) for i in range(tiles)])  5.56 us
    ppermute x1, starting transfers between devices, on_device(): low = lax.ppermute(first, 'wall', [(0, 1), (3, 2)])  5.1 us
    pallas_call x1, Pallas kernels, on_device(): call('start', start_kernel, (block, block, block, state, cell, f32(2 * NV...  5 us
    ppermute x3, waiting for transfers between devices, on_device(): patch = patch + lax.ppermute(part, 'wall', [(2, w)])  4.68 us
  transfers between devices with their start and end apart: 14, of which 5 were waited for; matrix products, arithmetic and copies ran while one was open for 0% of the time, Pallas kernels for 12%

profile of v2, /device:TPU:6, one launch (start us, length us, event | category | flops | bytes accessed | tf_op | source)
XLA Modules:
  0.0 99.1 jit_solution(5481160150141803919)
XLA Ops:
  0.6 1.7 %pack.1 = (f32[176,128]{1,0:T(8,128)}, f32[176,128]{1,0:T(8,128)}) custom-call(f32[10,8,8,128]{3,2,1,0:T(8,128)} %a_in.1, f32[8,8,128]{2,1,0:T(8,128)} %rad_ref.3), custom_call_target="tpu_custom_call" | custom-call | bytes 800000 | tf_op jit(solution)/shard_map/pack/pallas_call | solution.py:351
  2.3 5.6 %collective-permute-start.1 = (f32[176,128]{1,0:T(8,128)}, f32[176,128]{1,0:T(8,128)S(1)}, u32[]{:S(2)}, u32[]{:S(2)}) collective-permute-start(f32[176,128]{1,0:T(8,128)} %get-tuple-element.26), channel_id=1, source_target_pairs={{1,0},{2,1},{3,2},{4,3},{5,4},{6,5},{7,6},{8,7},{9,8},{10,9},{11,1... | collective-permute-start | bytes 270344 | tf_op jit(solution)/shard_map/ppermute | solution.py:353
  7.9 0.7 copy-done.10
  8.6 5.0 %start.1 = (f32[10,10,8,8,128]{4,3,2,1,0:T(8,128)S(1)}, f32[10,10,8,8,128]{4,3,2,1,0:T(8,128)S(1)}, f32[10,10,8,8,128]{4,3,2,1,0:T(8,128)S(1)}, f32[10,8,8,128]{...) custom-call(s32[3]{0:T(128)S(1)} %pad_add_fusion.pos_ref, ...), custom_call_target="tpu_custom_call" | custom-call | flops 44000000 | bytes 11000000 | tf_op jit(solution)/shard_map/start/pallas_call | solution.py:356
  13.6 0.5 collective-permute-done.left_ref
  14.1 0.7 collective-permute-start.4
  14.8 0.7 collective-permute-start.5
  15.6 2.1 %residual.1 = (f32[10,8,8,128]{3,2,1,0:T(8,128)S(1)}, f32[20,8,128]{2,1,0:T(8,128)S(1)}) custom-call(s32[3]{0:T(128)S(1)} %pad_add_fusion.pos_ref, f32[8,8,128]{2,1,0:T(8,128)S(1)} %get-tuple-element.28.w_ref, f32[10,8,8,128]{3,2,1,0:T(8,128)S(1)} %get-tuple-element.33.r_ref, f32[176,128]{1,0:T(8,128)S(1)} %collective-permute-done.left_ref, ...), custom_call_target="tpu_custom_call" | custom-call | flops 6000000 | bytes 2000000 | tf_op jit(solution)/shard_map/residual/pallas_call | solution.py:370
  17.7 5.1 %collective-permute-start.2 = (f32[20,8,128]{2,1,0:T(8,128)S(1)}, f32[20,8,128]{2,1,0:T(8,128)S(1)}, u32[]{:S(2)}, u32[]{:S(2)}) collective-permute-start(f32[20,8,128]{2,1,0:T(8,128)S(1)} %get-tuple-element.39), channel_id=1, source_target_pairs={{0,64},{192,128},{1,65},{193,129},{2,66},{194,130},{3,67},{195,131... | collective-permute-start | bytes 245768 | tf_op jit(solution)/shard_map/ppermute | solution.py:374
  22.8 2.0 %collective-permute-done.2.msg_ref.high_ref.low_ref = f32[20,8,128]{2,1,0:T(8,128)S(1)} collective-permute-done((f32[20,8,128]{2,1,0:T(8,128)S(1)}, f32[20,8,128]{2,1,0:T(8,128)S(1)}, u32[]{:S(2)}, u32[]{:S(2)}) %collective-permute-start.2) | collective-permute-done | bytes 81952 | tf_op jit(solution)/shard_map/ppermute | solution.py:374
  24.8 0.5 middle.1
  25.4 20.1 %collective-permute-start.6 = (f32[10,10,8,128]{3,2,1,0:T(8,128)S(1)}, f32[10,10,8,128]{3,2,1,0:T(8,128)S(1)}, u32[]{:S(2)}, u32[]{:S(2)}) collective-permute-start(f32[10,10,8,128]{3,2,1,0:T(8,128)S(1)} %get-tuple-element.42), channel_id=1, source_target_pairs={{0,128},{1,129},{2,130},{3,131},{4,132},{5,133},{6,134},{7,135},{8... | collective-permute-start | bytes 1228808 | tf_op jit(solution)/shard_map/ppermute | solution.py:380
  45.5 0.7 collective-permute-start.3
  46.9 1.4 %place.1.pw_ref = f32[576,88]{1,0:T(8,128)S(1)} custom-call(s32[1]{0:T(128)S(6)} %copy.15.count_ref, f32[80,256]{1,0:T(8,128)S(1)} %bitcast.10, s32[1,256]{1,0:T(1,128)S(1)} %bitcast.11, s32[1,256]{1,0:T(1,128)S(1)} %bitcast.12), custom_call_target="tpu_custom_call" | custom-call | flops 50000000 | bytes 1000000 | tf_op jit(solution)/shard_map/place/pallas_call | solution.py:366
  48.3 2.7 %collective-permute-done.6.m0_ref = f32[10,10,8,128]{3,2,1,0:T(8,128)S(1)} collective-permute-done((f32[10,10,8,128]{3,2,1,0:T(8,128)S(1)}, f32[10,10,8,128]{3,2,1,0:T(8,128)S(1)}, u32[]{:S(2)}, u32[]{:S(2)}) %collective-permute-start.6) | collective-permute-done | bytes 409632 | tf_op jit(solution)/shard_map/ppermute | solution.py:380
  51.0 1.3 %decide.1 = (f32[10,8,128]{2,1,0:T(8,128)}, f32[10,8,128]{2,1,0:T(8,128)}, f32[10,8,128]{2,1,0:T(8,128)}, f32[10,8,128]{2,1,0:T(8,128)}, f32[576,128]{1,0:T(8,128)}) custom-call(s32[3]{0:T(128)S(1)} %pad_add_fusion.pos_ref, f32[8,8,128]{2,1,0:T(8,128)S(1)} %get-tuple-element.28.w_ref, f32[30,8,128]{2,1,0:T(8,128)S(1)} %collective-permute-done.3.low_ref.mid_ref, ...), custom_call_target="tpu_custom_call" | custom-call | flops 20000000 | bytes 3000000 | tf_op jit(solution)/shard_map/decide/pallas_call | solution.py:383
  52.4 14.7 %all-to-all-start = ((f32[64,9,1,128]{3,2,1,0:T(1,128)}), f32[64,9,1,128]{3,2,1,0:T(1,128)}, u32[]{:S(2)}, u32[]{:S(2)}) async-start(f32[64,9,1,128]{3,2,1,0:T(1,128)} %bitcast.14), calls=%async_computation | async-start | bytes 589824 | tf_op jit(solution)/shard_map/all_to_all | solution.py:387
  67.1 0.7 collective-permute-start.7
  67.8 0.7 collective-permute-start.8
  68.5 1.3 %collective-permute-start.9 = (f32[10,8,128]{2,1,0:T(8,128)}, f32[10,8,128]{2,1,0:T(8,128)S(1)}, u32[]{:S(2)}, u32[]{:S(2)}) collective-permute-start(f32[10,8,128]{2,1,0:T(8,128)} %get-tuple-element.47), channel_id=1, source_target_pairs={{128,0},{129,1},{130,2},{131,3},{132,4},{133,5},{134,6},{135,7},{1... | collective-permute-start | bytes 122888 | tf_op jit(solution)/shard_map/ppermute | solution.py:390
  69.8 11.6 %collective-permute-done.9.y0_ref = f32[10,8,128]{2,1,0:T(8,128)S(1)} collective-permute-done((f32[10,8,128]{2,1,0:T(8,128)}, f32[10,8,128]{2,1,0:T(8,128)S(1)}, u32[]{:S(2)}, u32[]{:S(2)}) %collective-permute-start.9) | collective-permute-done | bytes 40992 | tf_op jit(solution)/shard_map/ppermute | solution.py:390
  81.4 1.9 %copy-done.1 = f32[10,10,8,8,128]{4,3,2,1,0:T(8,128)S(1)} copy-done((f32[10,10,8,8,128]{4,3,2,1,0:T(8,128)S(1)}, f32[10,10,8,8,128]{4,3,2,1,0:T(8,128)}, u32[]{:S(2)}) %copy-start.1) | copy-done | bytes 3276824
  83.3 1.9 %copy-done.3 = f32[10,10,8,8,128]{4,3,2,1,0:T(8,128)S(1)} copy-done((f32[10,10,8,8,128]{4,3,2,1,0:T(8,128)S(1)}, f32[10,10,8,8,128]{4,3,2,1,0:T(8,128)}, u32[]{:S(2)}) %copy-start.3) | copy-done | bytes 3276824
  85.2 1.0 copy-done.5
  86.2 0.8 copy-done.7
  87.0 2.5 %finish.1 = f32[10,8,8,128]{3,2,1,0:T(8,128)} custom-call(s32[3]{0:T(128)S(1)} %pad_add_fusion.pos_ref, f32[20,8,128]{2,1,0:T(8,128)S(1)} %collective-permute-done.2.msg_ref.high_ref.low_ref, f32[30,8,128]{2,1,0:T(8,128)S(1)} %collective-permute-done.3.low_ref.mid_ref, f32[10,8,128]{2,1,0:T(8,128)S(1)} %collective-permute-done.7.x3_ref, ...), custom_call_target="tpu_custom_call" | custom-call | flops 5000000 | bytes 2000000 | tf_op jit(solution)/shard_map/finish/pallas_call | solution.py:391
  89.5 1.6 %pick.1 = f32[64,128]{1,0:T(8,128)S(1)} custom-call(s32[3]{0:T(128)S(1)} %pad_add_fusion.pos_ref, f32[576,128]{1,0:T(8,128)} %bitcast.8.got_ref), custom_call_target="tpu_custom_call" | custom-call | flops 20000000 | bytes 400000 | tf_op jit(solution)/shard_map/pick/pallas_call | solution.py:397
  91.1 1.3 %collective-permute-start.10 = (f32[64,128]{1,0:T(8,128)S(1)}, f32[64,128]{1,0:T(8,128)S(1)}, u32[]{:S(2)}, u32[]{:S(2)}) collective-permute-start(f32[64,128]{1,0:T(8,128)S(1)} %pick.1), channel_id=1, source_target_pairs={{128,0},{129,1},{130,2},{131,3},{132,4},{133,5},{134,6},{135,7},{1... | collective-permute-start | bytes 98312 | tf_op jit(solution)/shard_map/ppermute | solution.py:400
  92.4 0.7 collective-permute-start.11
  93.1 0.7 collective-permute-start.12
  93.8 4.7 %collective-permute-done.10 = f32[64,128]{1,0:T(8,128)S(1)} collective-permute-done((f32[64,128]{1,0:T(8,128)S(1)}, f32[64,128]{1,0:T(8,128)S(1)}, u32[]{:S(2)}, u32[]{:S(2)}) %collective-permute-start.10) | collective-permute-done | bytes 32800 | tf_op jit(solution)/shard_map/ppermute | solution.py:400
  98.4 0.6 add_add_fusion
  (28 shorter events, 0.1 us)
Async XLA Ops:
  2.3 11.3 %collective-permute-start.1 = (f32[176,128]{1,0:T(8,128)}, f32[176,128]{1,0:T(8,128)S(1)}, u32[]{:S(2)}, u32[]{:S(2)}) collective-permute-start(f32[176,128]{1,0:T(8,128)} %get-tuple-element.26), channel_id=1, source_target_pairs={{1,0},{2,1},{3,2},{4,3},{5,4},{6,5},{7,6},{8,7},{9,8},{10,9},{11,1... | collective-permute-start | bytes 270344 | tf_op jit(solution)/shard_map/ppermute | solution.py:353
  7.9 6.3 %collective-permute-start = (f32[176,128]{1,0:T(8,128)}, f32[176,128]{1,0:T(8,128)S(1)}, u32[]{:S(2)}, u32[]{:S(2)}) collective-permute-start(f32[176,128]{1,0:T(8,128)} %get-tuple-element.30), channel_id=1, source_target_pairs={{0,1},{1,2},{2,3},{3,4},{4,5},{5,6},{6,7},{7,8},{8,9},{9,10},{10,1... | collective-permute-start | bytes 270344 | tf_op jit(solution)/shard_map/ppermute | solution.py:352
  7.9 0.7 copy-start.10
  13.6 37.4 %copy-start = (f32[10,10,8,8,128]{4,3,2,1,0:T(8,128)}, f32[10,10,8,8,128]{4,3,2,1,0:T(8,128)S(1)}, u32[]{:S(2)}) copy-start(f32[10,10,8,8,128]{4,3,2,1,0:T(8,128)S(1)} %get-tuple-element.37.d_ref) | copy-start | bytes 9830404
  13.6 37.4 %copy-start.2 = (f32[10,10,8,8,128]{4,3,2,1,0:T(8,128)}, f32[10,10,8,8,128]{4,3,2,1,0:T(8,128)S(1)}, u32[]{:S(2)}) copy-start(f32[10,10,8,8,128]{4,3,2,1,0:T(8,128)S(1)} %get-tuple-element.38.u_ref) | copy-start | bytes 9830404
  14.1 36.9 %collective-permute-start.4 = (f32[20,10,8,128]{3,2,1,0:T(8,128)S(1)}, f32[20,10,8,128]{3,2,1,0:T(8,128)S(1)}, u32[]{:S(2)}, u32[]{:S(2)}) collective-permute-start(f32[20,10,8,128]{3,2,1,0:T(8,128)S(1)} %get-tuple-element.31), channel_id=1, source_target_pairs={{64,128},{65,129},{66,130},{67,131},{68,132},{69,133},{70,134},{71... | collective-permute-start | bytes 2457608 | tf_op jit(solution)/shard_map/ppermute | solution.py:363
  14.8 36.2 %collective-permute-start.5 = (f32[20,10,8,128]{3,2,1,0:T(8,128)S(1)}, f32[20,10,8,128]{3,2,1,0:T(8,128)S(1)}, u32[]{:S(2)}, u32[]{:S(2)}) collective-permute-start(f32[20,10,8,128]{3,2,1,0:T(8,128)S(1)} %get-tuple-element.31), channel_id=1, source_target_pairs={{192,128},{193,129},{194,130},{195,131},{196,132},{197,133},{198,1... | collective-permute-start | bytes 2457608 | tf_op jit(solution)/shard_map/ppermute | solution.py:362
  17.7 33.4 %copy-start.4 = (f32[10,8,8,128]{3,2,1,0:T(8,128)}, f32[10,8,8,128]{3,2,1,0:T(8,128)S(1)}, u32[]{:S(2)}) copy-start(f32[10,8,8,128]{3,2,1,0:T(8,128)S(1)} %get-tuple-element.40.r_ref) | copy-start | bytes 983044
  17.7 7.1 %collective-permute-start.2 = (f32[20,8,128]{2,1,0:T(8,128)S(1)}, f32[20,8,128]{2,1,0:T(8,128)S(1)}, u32[]{:S(2)}, u32[]{:S(2)}) collective-permute-start(f32[20,8,128]{2,1,0:T(8,128)S(1)} %get-tuple-element.39), channel_id=1, source_target_pairs={{0,64},{192,128},{1,65},{193,129},{2,66},{194,130},{3,67},{195,131... | collective-permute-start | bytes 245768 | tf_op jit(solution)/shard_map/ppermute | solution.py:374
  24.8 22.0 %copy-start.6 = (f32[256,10,8]{0,2,1:T(8,128)S(1)}, f32[256,10,8]{0,2,1:T(8,128)}, u32[]{:S(2)}) copy-start(f32[256,10,8]{0,2,1:T(8,128)} %param.20) | copy-start | bytes 245764
  24.8 22.0 %copy-start.8 = (s32[256,1]{0,1:T(1,128)S(1)}, s32[256,1]{0,1:T(1,128)}, u32[]{:S(2)}) copy-start(s32[256,1]{0,1:T(1,128)} %param.21) | copy-start | bytes 3076
  24.8 22.0 %copy-start.9 = (s32[256]{0:T(256)S(1)}, s32[256]{0:T(256)}, u32[]{:S(2)}) copy-start(s32[256]{0:T(256)} %param.22) | copy-start | bytes 3076
  25.4 25.6 %collective-permute-start.6 = (f32[10,10,8,128]{3,2,1,0:T(8,128)S(1)}, f32[10,10,8,128]{3,2,1,0:T(8,128)S(1)}, u32[]{:S(2)}, u32[]{:S(2)}) collective-permute-start(f32[10,10,8,128]{3,2,1,0:T(8,128)S(1)} %get-tuple-element.42), channel_id=1, source_target_pairs={{0,128},{1,129},{2,130},{3,131},{4,132},{5,133},{6,134},{7,135},{8... | collective-permute-start | bytes 1228808 | tf_op jit(solution)/shard_map/ppermute | solution.py:380
  45.5 2.8 %collective-permute-start.3 = (f32[30,8,128]{2,1,0:T(8,128)S(1)}, f32[30,8,128]{2,1,0:T(8,128)S(1)}, u32[]{:S(2)}, u32[]{:S(2)}) collective-permute-start(f32[30,8,128]{2,1,0:T(8,128)S(1)} %middle.1), channel_id=1, source_target_pairs={{64,128},{65,129},{66,130},{67,131},{68,132},{69,133},{70,134},{71... | collective-permute-start | bytes 368648 | tf_op jit(solution)/shard_map/ppermute | solution.py:378
  52.4 37.1 %all-to-all-start = ((f32[64,9,1,128]{3,2,1,0:T(1,128)}), f32[64,9,1,128]{3,2,1,0:T(1,128)}, u32[]{:S(2)}, u32[]{:S(2)}) async-start(f32[64,9,1,128]{3,2,1,0:T(1,128)} %bitcast.14), calls=%async_computation | async-start | bytes 589824 | tf_op jit(solution)/shard_map/all_to_all | solution.py:387
  67.1 2.6 %collective-permute-start.7 = (f32[10,8,128]{2,1,0:T(8,128)}, f32[10,8,128]{2,1,0:T(8,128)S(1)}, u32[]{:S(2)}, u32[]{:S(2)}) collective-permute-start(f32[10,8,128]{2,1,0:T(8,128)} %get-tuple-element.44), channel_id=1, source_target_pairs={{128,192},{129,193},{130,194},{131,195},{132,196},{133,197},{134,1... | collective-permute-start | bytes 122888 | tf_op jit(solution)/shard_map/ppermute | solution.py:388
  67.8 2.0 %collective-permute-start.8 = (f32[10,8,128]{2,1,0:T(8,128)}, f32[10,8,128]{2,1,0:T(8,128)S(1)}, u32[]{:S(2)}, u32[]{:S(2)}) collective-permute-start(f32[10,8,128]{2,1,0:T(8,128)} %get-tuple-element.46), channel_id=1, source_target_pairs={{128,64},{129,65},{130,66},{131,67},{132,68},{133,69},{134,70},{13... | collective-permute-start | bytes 122888 | tf_op jit(solution)/shard_map/ppermute | solution.py:389
  68.5 12.9 %collective-permute-start.9 = (f32[10,8,128]{2,1,0:T(8,128)}, f32[10,8,128]{2,1,0:T(8,128)S(1)}, u32[]{:S(2)}, u32[]{:S(2)}) collective-permute-start(f32[10,8,128]{2,1,0:T(8,128)} %get-tuple-element.47), channel_id=1, source_target_pairs={{128,0},{129,1},{130,2},{131,3},{132,4},{133,5},{134,6},{135,7},{1... | collective-permute-start | bytes 122888 | tf_op jit(solution)/shard_map/ppermute | solution.py:390
  81.4 1.9 %copy-start.1 = (f32[10,10,8,8,128]{4,3,2,1,0:T(8,128)S(1)}, f32[10,10,8,8,128]{4,3,2,1,0:T(8,128)}, u32[]{:S(2)}) copy-start(f32[10,10,8,8,128]{4,3,2,1,0:T(8,128)} %copy-done) | copy-start | bytes 9830404
  83.3 1.9 %copy-start.3 = (f32[10,10,8,8,128]{4,3,2,1,0:T(8,128)S(1)}, f32[10,10,8,8,128]{4,3,2,1,0:T(8,128)}, u32[]{:S(2)}) copy-start(f32[10,10,8,8,128]{4,3,2,1,0:T(8,128)} %copy-done.2) | copy-start | bytes 9830404
  85.2 1.0 copy-start.5
  86.2 0.8 copy-start.7
  91.1 7.3 %collective-permute-start.10 = (f32[64,128]{1,0:T(8,128)S(1)}, f32[64,128]{1,0:T(8,128)S(1)}, u32[]{:S(2)}, u32[]{:S(2)}) collective-permute-start(f32[64,128]{1,0:T(8,128)S(1)} %pick.1), channel_id=1, source_target_pairs={{128,0},{129,1},{130,2},{131,3},{132,4},{133,5},{134,6},{135,7},{1... | collective-permute-start | bytes 98312 | tf_op jit(solution)/shard_map/ppermute | solution.py:400
  92.4 6.0 %collective-permute-start.11 = (f32[64,128]{1,0:T(8,128)S(1)}, f32[64,128]{1,0:T(8,128)S(1)}, u32[]{:S(2)}, u32[]{:S(2)}) collective-permute-start(f32[64,128]{1,0:T(8,128)S(1)} %pick.1), channel_id=1, source_target_pairs={{128,64},{129,65},{130,66},{131,67},{132,68},{133,69},{134,70},{13... | collective-permute-start | bytes 98312 | tf_op jit(solution)/shard_map/ppermute | solution.py:400
  93.1 5.3 %collective-permute-start.12 = (f32[64,128]{1,0:T(8,128)S(1)}, f32[64,128]{1,0:T(8,128)S(1)}, u32[]{:S(2)}, u32[]{:S(2)}) collective-permute-start(f32[64,128]{1,0:T(8,128)S(1)} %pick.1), channel_id=1, source_target_pairs={{128,192},{129,193},{130,194},{131,195},{132,196},{133,197},{134,1... | collective-permute-start | bytes 98312 | tf_op jit(solution)/shard_map/ppermute | solution.py:400

commit v3 on v2

v3 whole, which is shorter than its diff:
```python
import jax
import jax.numpy as jnp
from jax import lax
from jax.experimental import pallas as pl
from jax.experimental.pallas import tpu as pltpu
from jax.sharding import PartitionSpec as P

NV = 10
K = 8
H = 8
S = 128
PATCH_DEV = 64
SLOTS = 8
ROWS_PER_OWNER = SLOTS + 1
F32 = jnp.float32
highest = lax.Precision.HIGHEST

VM = pl.BlockSpec(memory_space=pltpu.VMEM)
SM = pl.BlockSpec(memory_space=pltpu.SMEM)
HB = pl.BlockSpec(memory_space=pltpu.HBM)


def f32(*shape):
    return jax.ShapeDtypeStruct(shape, F32)


def held(*shape):
    return pltpu.VMEM(shape, F32)


def away(*shape):
    return pltpu.HBM(shape, F32)


def far_off(x):
    return pltpu.with_memory_space_constraint(x, pltpu.HBM)


def call(name, body, out_shape, n_in, smem=(), far=(), scratch=(), flops=0, nbytes=0):
    single = not isinstance(out_shape, (tuple, list))
    run = pl.pallas_call(
        body,
        name=name,
        out_shape=out_shape,
        in_specs=[SM if i in smem else HB if i in far else VM for i in range(n_in)],
        out_specs=VM if single else [VM] * len(out_shape),
        scratch_shapes=list(scratch),
        compiler_params=pltpu.CompilerParams(vmem_limit_bytes=12 * 1024 * 1024),
        cost_estimate=pl.CostEstimate(flops=flops, bytes_accessed=nbytes, transcendentals=0),
    )
    return run


def block_dot(m_ref, k, x):
    acc = None
    for j in range(NV):
        term = m_ref[:, j, k] * x[j][None]
        acc = term if acc is None else acc + term
    return acc


def forward_sweep(l_ref, d_ref, r_ref, s_ref, x):
    f = x
    for k in range(K):
        r = r_ref[:, k]
        f = r if f is None else r + block_dot(l_ref, k, f)
        s_ref[k] = block_dot(d_ref, k, f)
    return f


def backward_sweep(u_ref, s_ref, w_ref, y, emit=None):
    b, p = y, None
    for k in range(K - 1, -1, -1):
        s = s_ref[k]
        b = s if b is None else s - block_dot(u_ref, k, b)
        if w_ref is not None:
            p = b * w_ref[k] if p is None else p + b * w_ref[k]
        if emit is not None:
            emit(k, b)
    return b, p


def map_dot(m_ref, base, x):
    acc = None
    for j in range(NV):
        term = m_ref[base + j] * x[j][None]
        acc = term if acc is None else acc + term
    return acc


def pack_kernel(a_ref, rad_ref, lo_ref, hi_ref):
    for v in range(NV + 1):
        for k in range(K):
            cell = a_ref[v, k] if v < NV else rad_ref[k]
            at = 2 * (v * K + k)
            lo_ref[at : at + 2, :] = cell[0:2]
            hi_ref[at : at + 2, :] = cell[6:8]


def pair_dot(m_ref, k, xs):
    accs = [None] * len(xs)
    for j in range(NV):
        m = m_ref[:, j, k]
        for n, x in enumerate(xs):
            term = m * x[j][None]
            accs[n] = term if accs[n] is None else accs[n] + term
    return accs


def pair_map(m_ref, half, xs):
    accs = [None] * len(xs)
    for j in range(NV):
        m = m_ref[half, j]
        for n, x in enumerate(xs):
            term = m * x[j][None]
            accs[n] = term if accs[n] is None else accs[n] + term
    return accs


def interior(a_ref, src_ref, rad_ref, frq_ref, out_ref):
    row = lax.broadcasted_iota(jnp.int32, (H, S), 0)
    lane = lax.broadcasted_iota(jnp.int32, (H, S), 1)
    for k in range(K):
        a = a_ref[:, k]
        rad = rad_ref[k]
        applied = None
        for d, w in ((-2, -0.0625), (-1, 0.25), (1, 0.25), (2, -0.0625)):
            inside = (row + d >= 0) & (row + d < H)
            coef = jnp.where(inside, w * (rad + pltpu.roll(rad, (-d) % H, 0)), 0.0)
            term = coef[None] * pltpu.roll(a, (-d) % H, 1)
            applied = term if applied is None else applied + term
        for d in (-1, 1):
            inside = (lane + d >= 0) & (lane + d < S)
            coef = jnp.where(inside, 0.25 * (rad + pltpu.roll(rad, (-d) % S, 1)), 0.0)
            applied = applied + coef[None] * pltpu.roll(a, (-d) % S, 2)
        frq = frq_ref[k][None]
        half = NV // 2
        src = src_ref[:, k] - applied
        out_ref[:half, k] = src[:half] + frq * a[half:]
        out_ref[half:, k] = src[half:] - frq * a[:half]


def start_kernel(
    pos_ref, w_in, a_in, src_in, rad_in, frq_in, l_in, d_in, u_in,
    l_ref, d_ref, u_ref, r_ref, w_ref, map_ref, a_ref, src_ref, rad_ref, frq_ref, s_ref, state_sems, block_sems,
):
    wall = pos_ref[0]
    state = [
        pltpu.make_async_copy(there, here, state_sems.at[n])
        for n, (there, here) in enumerate(((a_in, a_ref), (src_in, src_ref), (rad_in, rad_ref), (frq_in, frq_ref)))
    ]
    blocks = [
        [
            pltpu.make_async_copy(there.at[:, :, k], here.at[:, :, k], block_sems.at[k, n])
            for n, (there, here) in enumerate(((l_in, l_ref), (d_in, d_ref), (u_in, u_ref)))
        ]
        for k in range(K)
    ]
    for copy in state:
        copy.start()
    for k in range(K - 1, -1, -1):
        for copy in blocks[k]:
            copy.start()
    for k in range(K):
        w_ref[k] = jnp.broadcast_to(w_in[:, k : k + 1], (H, S))
    for copy in state:
        copy.wait()
    interior(a_ref, src_ref, rad_ref, frq_ref, r_ref)

    def arrived(k):
        for copy in blocks[k]:
            copy.wait()

    @pl.when((wall == 0) | (wall == 2))
    def _():
        for k in range(K - 1, -1, -1):
            arrived(k)

    @pl.when(wall == 1)
    def _():
        arrived(K - 1)
        for c in range(NV):
            s_ref[(K - 1) % 2, c] = u_ref[:, c, K - 1]
        for k in range(K - 2, -1, -1):
            arrived(k)

            @pl.loop(0, NV // 2)
            def _(pair):
                cols = [2 * pair, 2 * pair + 1]
                outs = pair_dot(u_ref, k, [s_ref[(k + 1) % 2, c] for c in cols])
                for c, out in zip(cols, outs):
                    if k > 0:
                        s_ref[k % 2, c] = out
                    else:
                        map_ref[c] = out

    @pl.when(wall == 3)
    def _():
        arrived(K - 1)
        for c in range(NV):
            s_ref[(K - 1) % 2, c] = d_ref[:, c, K - 1]
        for k in range(K - 2, -1, -1):
            arrived(k)

            @pl.loop(0, NV // 2)
            def _(pair):
                cols = [2 * pair, 2 * pair + 1]
                outs = pair_map(s_ref, (k + 1) % 2, [l_ref[:, c, k + 1] for c in cols])
                outs = pair_dot(u_ref, k, outs)
                for c, out in zip(cols, outs):
                    s_ref[k % 2, c] = d_ref[:, c, k] - out

        @pl.loop(0, NV // 2)
        def _(pair):
            cols = [2 * pair, 2 * pair + 1]
            for c, out in zip(cols, pair_map(s_ref, 0, [l_ref[:, c, 0] for c in cols])):
                map_ref[c] = out


def residual_kernel(pos_ref, r_ref, left_ref, right_ref, rad_ref, l_ref, d_ref, u_ref, out_ref, msg_ref, s_ref):
    wall, tile, last = pos_ref[0], pos_ref[1], pos_ref[2]
    row = lax.broadcasted_iota(jnp.int32, (H, S), 0)
    has_left = tile > 0
    has_right = tile < last

    def line(ref, v, k, c):
        at = 2 * (v * K + k) + c
        return jnp.broadcast_to(ref[at : at + 1, :], (H, S))

    for k in range(K):
        rad = rad_ref[k]
        l0, l1, r0, r1 = (line(ref, NV, k, c) for ref in (left_ref, right_ref) for c in (0, 1))
        zero = jnp.zeros((H, S), F32)
        f_l0 = jnp.where((row == 0) & has_left, -0.0625 * (rad + l0), zero)
        f_l1 = jnp.where(row == 0, 0.25 * (rad + l1), jnp.where(row == 1, -0.0625 * (rad + l1), zero))
        f_l1 = jnp.where(has_left, f_l1, zero)
        f_r0 = jnp.where(row == 7, 0.25 * (rad + r0), jnp.where(row == 6, -0.0625 * (rad + r0), zero))
        f_r0 = jnp.where(has_right, f_r0, zero)
        f_r1 = jnp.where((row == 7) & has_right, -0.0625 * (rad + r1), zero)
        for v in range(NV):
            applied = f_l0 * line(left_ref, v, k, 0) + f_l1 * line(left_ref, v, k, 1)
            applied = applied + (f_r0 * line(right_ref, v, k, 0) + f_r1 * line(right_ref, v, k, 1))
            out_ref[v, k] = r_ref[v, k] - applied

    @pl.when((wall == 0) | (wall == 3))
    def _():
        f = forward_sweep(l_ref, d_ref, out_ref, s_ref, None)
        b, _ = backward_sweep(u_ref, s_ref, None, None)
        msg_ref[...] = jnp.where(wall == 0, f, b)


def middle_kernel(pos_ref, x_ref, map_ref, r_ref, l_ref, d_ref, u_ref, out_ref, below_ref, s_ref):
    @pl.when(pos_ref[0] == 1)
    def _():
        out_ref[...] = forward_sweep(l_ref, d_ref, r_ref, s_ref, x_ref[...])
        below_ref[NV] = backward_sweep(u_ref, s_ref, None, None)[0]
        for c in range(NV):
            below_ref[c] = map_ref[c]


def decide_kernel(pos_ref, x_ref, b_ref, map_ref, r_ref, l_ref, d_ref, u_ref, x3_ref, y2_ref, y1_ref, s_ref):
    @pl.when(pos_ref[0] == 2)
    def _():
        x3 = forward_sweep(l_ref, d_ref, r_ref, s_ref, x_ref[...])
        x3_ref[...] = x3
        y2 = b_ref[...] + map_dot(map_ref, 0, x3)
        y2_ref[...] = y2
        y1_ref[...] = backward_sweep(u_ref, s_ref, None, y2)[0]


def finish_kernel(
    pos_ref, x1_ref, x2_ref, x3_ref, y2_ref, y1_ref, y10_ref, below_ref, w_ref, pw_ref, r_ref, l_ref, d_ref, u_ref,
    out_ref, rows_ref, s_ref, x_ref, y_ref, prof_ref,
):
    wall = pos_ref[0]

    @pl.when(wall == 0)
    def _():
        x_ref[...] = jnp.zeros((NV, H, S), F32)
        y_ref[...] = below_ref[NV] + map_dot(below_ref, 0, y10_ref[...])

    @pl.when(wall == 1)
    def _():
        x_ref[...] = x1_ref[...]
        y_ref[...] = y1_ref[...]

    @pl.when(wall == 2)
    def _():
        x_ref[...] = x2_ref[...]
        y_ref[...] = y2_ref[...]

    @pl.when(wall == 3)
    def _():
        x_ref[...] = x3_ref[...]
        y_ref[...] = jnp.zeros((NV, H, S), F32)

    forward_sweep(l_ref, d_ref, r_ref, s_ref, x_ref[...])

    def emit(k, b):
        out_ref[:, k] = b

    _, profile = backward_sweep(u_ref, s_ref, w_ref, y_ref[...], emit)
    for v in range(NV):
        prof_ref[v * H : (v + 1) * H, :] = profile[v]
    row = lax.broadcasted_iota(jnp.int32, (SLOTS, S), 0)
    lane = lax.broadcasted_iota(jnp.int32, (SLOTS, S), 1)
    prof_ref[NV * H :, :] = (row == lane).astype(F32)
    rows_ref[...] = jnp.dot(pw_ref[...], prof_ref[...], precision=highest, preferred_element_type=F32)


def place_kernel(count_ref, w_ref, owner_ref, tag_ref, out_ref):
    blocks = owner_ref.shape[1]
    owners = out_ref.shape[0] // ROWS_PER_OWNER
    owner = owner_ref[...]
    live = lax.broadcasted_iota(jnp.int32, (1, blocks), 1) < count_ref[0]
    hits = (owner == lax.broadcasted_iota(jnp.int32, (owners, blocks), 0)).astype(F32)
    earlier = lax.broadcasted_iota(jnp.int32, (blocks, blocks), 0) < lax.broadcasted_iota(jnp.int32, (blocks, blocks), 1)
    before = jnp.dot(hits, earlier.astype(F32), preferred_element_type=F32)
    slot = jnp.sum(before * hits, axis=0, keepdims=True).astype(jnp.int32)
    row = lax.broadcasted_iota(jnp.int32, (owners * ROWS_PER_OWNER, blocks), 0)
    placed = ((owner * ROWS_PER_OWNER + slot == row) & live).astype(F32)
    tagged = ((owner * ROWS_PER_OWNER + SLOTS == row) & live).astype(F32)
    width = NV * H
    lanes = lax.broadcasted_iota(jnp.int32, (SLOTS, blocks), 0)
    tags = jnp.where(lanes == slot, (tag_ref[...] + 1).astype(F32), 0.0)
    dims = (((1,), (1,)), ((), ()))
    out_ref[:, :width] = lax.dot_general(placed, w_ref[...], dims, precision=highest, preferred_element_type=F32)
    out_ref[:, width:] = lax.dot_general(tagged, tags, dims, precision=highest, preferred_element_type=F32)


def pick_kernel(got_ref, out_ref):
    rows = got_ref.shape[0]
    sources = rows // ROWS_PER_OWNER
    tag_rows = got_ref[pl.ds(SLOTS, sources, stride=ROWS_PER_OWNER), :]
    lane_of = (
        lax.broadcasted_iota(jnp.int32, (SLOTS, S), 0) == lax.broadcasted_iota(jnp.int32, (SLOTS, S), 1)
    ).astype(F32)
    tags = lax.dot_general(
        lane_of, tag_rows, (((1,), (1,)), ((), ())), precision=highest, preferred_element_type=F32
    )
    column = lax.broadcasted_iota(jnp.int32, (sources, rows), 1)
    first = lax.broadcasted_iota(jnp.int32, (sources, rows), 0) * ROWS_PER_OWNER
    spread = ((column >= first) & (column < first + ROWS_PER_OWNER)).astype(F32)
    wide = jnp.dot(tags, spread, precision=highest, preferred_element_type=F32)
    slot = lax.broadcasted_iota(jnp.int32, (SLOTS, rows), 1) % ROWS_PER_OWNER
    mine = slot == lax.broadcasted_iota(jnp.int32, (SLOTS, rows), 0)
    tag = jnp.sum(jnp.where(mine, wide, 0.0), axis=0, keepdims=True)
    target = (lax.broadcasted_iota(jnp.int32, (PATCH_DEV, rows), 0) + 1).astype(F32)
    picker = (tag == target).astype(F32)
    out_ref[...] = jnp.dot(picker, got_ref[...], precision=highest, preferred_element_type=F32)


def on_device(
    adjoint, source, radius, frequency, lower, diag, upper, wall_weight,
    surface_weight, patch_owner, patch_row, surface_count,
):
    tiles = lax.axis_size("tile")
    tie = lax.optimization_barrier
    pos = jnp.stack([lax.axis_index("wall"), lax.axis_index("tile"), jnp.int32(tiles - 1)]).astype(jnp.int32)
    levels = held(K, NV, H, S)
    block, state, cell, vec = held(NV, NV, K, H, S), held(NV, K, H, S), held(K, H, S), f32(NV, H, S)
    adjoint, source, radius, frequency, lower, diag, upper, wall_weight = (
        far_off(x)
        for x in (adjoint, source, radius, frequency, lower, diag, upper, wall_weight.reshape(1, K))
    )

    lo, hi = call("pack", pack_kernel, (f32(22 * K, S), f32(22 * K, S)), 2, nbytes=800_000)(adjoint, radius)
    left = lax.ppermute(hi, "tile", [(i, (i + 1) % tiles) for i in range(tiles)])
    right = lax.ppermute(lo, "tile", [((i + 1) % tiles, i) for i in range(tiles)])

    lo, pos1 = tie((lo, pos))
    lower, diag, upper, inner, weight, maps = call(
        "start", start_kernel, (block, block, block, state, cell, f32(NV, NV, H, S)), 9, smem=(0,),
        far=(2, 3, 4, 5, 6, 7, 8),
        scratch=(
            state, state, cell, cell, held(2, NV, NV, H, S), pltpu.SemaphoreType.DMA((4,)), pltpu.SemaphoreType.DMA((K, 3)),
        ),
        flops=30_000_000, nbytes=11_000_000,
    )(pos1, wall_weight, adjoint, source, radius, frequency, lower, diag, upper)
    maps, left, right = tie((maps, left, right))
    map3 = lax.ppermute(maps, "wall", [(3, 2)])

    resid, first = call(
        "residual", residual_kernel, (state, vec), 8, smem=(0,), scratch=(levels,),
        flops=6_000_000, nbytes=2_000_000,
    )(pos, inner, left, right, radius, lower, diag, upper)
    x1 = b3 = lax.ppermute(first, "wall", [(0, 1), (3, 2)])
    x2, below = call(
        "middle", middle_kernel, (vec, f32(NV + 1, NV, H, S)), 7, smem=(0,), scratch=(levels,), flops=5_000_000, nbytes=2_000_000
    )(pos, x1, maps, resid, lower, diag, upper)
    x2 = lax.ppermute(x2, "wall", [(1, 2)])
    x2, below = tie((x2, below))
    below = lax.ppermute(below, "wall", [(1, 0)])

    swt = surface_weight.transpose(1, 2, 0).reshape(NV * H, -1)
    placed = call(
        "place", place_kernel, held(tiles * ROWS_PER_OWNER, NV * H + SLOTS), 4, smem=(0,), flops=50_000_000, nbytes=1_000_000
    )(surface_count, swt, patch_owner.reshape(1, -1), patch_row.reshape(1, -1))

    x3, y2, y1 = call(
        "decide", decide_kernel, (vec, vec, vec), 8, smem=(0,), scratch=(levels,), flops=20_000_000, nbytes=3_000_000,
    )(pos, x2, b3, map3, resid, lower, diag, upper)
    x3 = lax.ppermute(x3, "wall", [(2, 3)])
    y11 = lax.ppermute(y1, "wall", [(2, 1)])
    y10 = lax.ppermute(y1, "wall", [(2, 0)])
    adjoint_next, rows = call(
        "finish", finish_kernel, (f32(NV, K, H, S), away(tiles * ROWS_PER_OWNER, S)), 14, smem=(0,),
        scratch=(levels, held(NV, H, S), held(NV, H, S), held(NV * H + SLOTS, S)), flops=5_000_000, nbytes=2_000_000,
    )(pos, x1, x2, x3, y2, y11, y10, below, weight, placed, resid, lower, diag, upper)
    got = lax.all_to_all(rows.reshape(tiles, ROWS_PER_OWNER, 1, S), "tile", split_axis=0, concat_axis=0)
    got = got.reshape(tiles * ROWS_PER_OWNER, S)
    part = call("pick", pick_kernel, f32(PATCH_DEV, S), 1, flops=20_000_000, nbytes=400_000)(got)
    walls = lax.axis_size("wall")
    patch = part
    for d in range(1, walls):
        patch = patch + lax.ppermute(part, "wall", [(w, (w + d) % walls) for w in range(walls)])
    return adjoint_next, patch


def solution(mesh):
    in_specs = (
        P(None, "wall", "tile", None),
        P(None, "wall", "tile", None),
        P("wall", "tile", None),
        P("wall", "tile", None),
        P(None, None, "wall", "tile", None),
        P(None, None, "wall", "tile", None),
        P(None, None, "wall", "tile", None),
        P("wall"),
        P("tile", None, None),
        P("tile", None),
        P("tile"),
        P("tile"),
    )
    out_specs = (P(None, "wall", "tile", None), P("tile", None))
    return jax.shard_map(
        on_device, mesh=mesh, in_specs=in_specs, out_specs=out_specs, check_vma=False
    )
```

time: 99.9 us -> 80.4 us (0.80)
  starting transfers between devices: 52.9 us -> 17.9 us
  blocking collectives: 0 us -> 23 us
  local copies, waits for them, and re-layouts: 6.28 us -> 0.02 us
  Pallas kernels: 16.2 us -> 14.3 us
  waiting for transfers between devices: 21.5 us -> 22.6 us
    all_to_all x0 -> x1, blocking collectives: none -> 23 us  [on_device(): lax.all_to_all(rows.reshape(tiles, ROWS_PER_OWNER, 1, S), 'tile', split_a...]
    ppermute x9 -> x8, starting transfers between devices: 31.2 us -> 11 us  [the longest x1 4.67 us: on_device(): x1 = b3 = lax.ppermute(first, 'wall', [(0, 1), (3, 2)])]
    all_to_all x1 -> x0, starting transfers between devices: 14.7 us -> none  [on_device(): lax.all_to_all(rows.reshape(tiles, ROWS_PER_OWNER, 1, S), 'tile', split_a...]
    unnamed x22 -> x6, local copies, waits for them, and re-layouts: 6.28 us -> 0.02 us
    pallas_call x6, Pallas kernels: 13.1 us -> 11.8 us  [the longest x1 5.09 us: on_device(): call('start', start_kernel, (block, block, block, state, cell, f32(NV, NV...]
    ppermute x9 -> x8, waiting for transfers between devices: 21 us -> 21.7 us  [the longest x1 15.7 us: on_device(): y10 = lax.ppermute(y1, 'wall', [(2, 0)])]
  transfers between devices with their start and end apart: 14 -> 12, of which waited for: 5 -> 5; matrix products, arithmetic and copies ran while one was open for 0% -> 0% of each run, Pallas kernels for 12% -> 9%
where the time goes in v3:
time: 80.4 us; the launch traced here: 80 us
  blocking collectives  23 us (29%)
  waiting for transfers between devices  22.6 us (28%)
  starting transfers between devices  17.9 us (22%)
  Pallas kernels  14.3 us (18%)
  between operations  1.45 us (2%)
    all_to_all x1, blocking collectives, on_device(): lax.all_to_all(rows.reshape(tiles, ROWS_PER_OWNER, 1, S), 'tile', split_a...  23 us
    ppermute x1, waiting for transfers between devices, on_device(): y10 = lax.ppermute(y1, 'wall', [(2, 0)])  15.7 us
    ppermute x1, starting transfers between devices, on_device(): lax.ppermute(lo, 'tile', [((i + 1) % tiles, i) for i in range(tiles)])  5.64 us
    pallas_call x1, Pallas kernels, on_device(): call('start', start_kernel, (block, block, block, state, cell, f32(NV, NV...  5.09 us
    ppermute x1, starting transfers between devices, on_device(): x1 = b3 = lax.ppermute(first, 'wall', [(0, 1), (3, 2)])  4.67 us
    ppermute x3, waiting for transfers between devices, on_device(): lax.ppermute(part, 'wall', [(w, (w + d) % walls) for w in range(walls)])  4.26 us
    pallas_call x1, Pallas kernels, on_device(): call('finish', finish_kernel, (f32(NV, K, H, S), away(tiles * ROWS_PER_OW...  2.94 us
    ppermute x3, starting transfers between devices, on_device(): lax.ppermute(part, 'wall', [(w, (w + d) % walls) for w in range(walls)])  2.24 us
  transfers between devices with their start and end apart: 12, of which 5 were waited for; matrix products, arithmetic and copies ran while one was open for 0% of the time, Pallas kernels for 9%

profile of v3, /device:TPU:6, one launch (start us, length us, event | category | flops | bytes accessed | tf_op | source)
XLA Modules:
  0.0 80.0 jit_solution(15468620662912396094)
XLA Ops:
  0.6 1.0 %pack.1 = (f32[176,128]{1,0:T(8,128)S(1)}, f32[176,128]{1,0:T(8,128)S(1)}) custom-call(f32[10,8,8,128]{3,2,1,0:T(8,128)} %a_in.1, f32[8,8,128]{2,1,0:T(8,128)} %rad_ref.3), custom_call_target="tpu_custom_call" | custom-call | bytes 800000 | tf_op jit(solution)/shard_map/pack/pallas_call | solution.py:367
  1.7 5.6 %collective-permute-start.1 = (f32[176,128]{1,0:T(8,128)S(1)}, f32[176,128]{1,0:T(8,128)S(1)}, u32[]{:S(2)}, u32[]{:S(2)}) collective-permute-start(f32[176,128]{1,0:T(8,128)S(1)} %get-tuple-element.25), channel_id=1, source_target_pairs={{1,0},{2,1},{3,2},{4,3},{5,4},{6,5},{7,6},{8,7},{9,8},{10,9},{11,1... | collective-permute-start | bytes 270344 | tf_op jit(solution)/shard_map/ppermute | solution.py:369
  7.3 0.1 pad_add_fusion.pos_ref
  7.4 5.1 %start.1 = (f32[10,10,8,8,128]{4,3,2,1,0:T(8,128)S(1)}, f32[10,10,8,8,128]{4,3,2,1,0:T(8,128)S(1)}, f32[10,10,8,8,128]{4,3,2,1,0:T(8,128)S(1)}, f32[10,8,8,128]{...) custom-call(s32[3]{0:T(128)S(1)} %pad_add_fusion.pos_ref, f32[1,8]{1,0:T(1,128)} %bitcast.15, ...), custom_call_target="tpu_custom_call" | custom-call | flops 30000000 | bytes 11000000 | tf_op jit(solution)/shard_map/start/pallas_call | solution.py:372
  12.5 0.0 collective-permute-done.1.right_ref
  12.5 0.9 %collective-permute-done.left_ref = f32[176,128]{1,0:T(8,128)S(1)} collective-permute-done((f32[176,128]{1,0:T(8,128)S(1)}, f32[176,128]{1,0:T(8,128)S(1)}, u32[]{:S(2)}, u32[]{:S(2)}) %collective-permute-start) | collective-permute-done | bytes 90144 | tf_op jit(solution)/shard_map/ppermute | solution.py:368
  13.4 2.0 %residual.1 = (f32[10,8,8,128]{3,2,1,0:T(8,128)S(1)}, f32[10,8,128]{2,1,0:T(8,128)S(1)}) custom-call(s32[3]{0:T(128)S(1)} %pad_add_fusion.pos_ref, f32[10,8,8,128]{3,2,1,0:T(8,128)S(1)} %get-tuple-element.27.r_ref, f32[176,128]{1,0:T(8,128)S(1)} %collective-permute-done.left_ref, f32[176,128]{1,0:T(8,128)S(1)} %collective-permute-done.1.right_ref, ...), custom_call_target="tpu_custom_call" | custom-call | flops 6000000 | bytes 2000000 | tf_op jit(solution)/shard_map/residual/pallas_call | solution.py:383
  15.4 4.7 %collective-permute-start.2 = (f32[10,8,128]{2,1,0:T(8,128)S(1)}, f32[10,8,128]{2,1,0:T(8,128)S(1)}, u32[]{:S(2)}, u32[]{:S(2)}) collective-permute-start(f32[10,8,128]{2,1,0:T(8,128)S(1)} %get-tuple-element.35), channel_id=1, source_target_pairs={{0,64},{192,128},{1,65},{193,129},{2,66},{194,130},{3,67},{195,131... | collective-permute-start | bytes 122888 | tf_op jit(solution)/shard_map/ppermute | solution.py:387
  20.1 1.7 %collective-permute-done.2.x_ref.b_ref.x1_ref = f32[10,8,128]{2,1,0:T(8,128)S(1)} collective-permute-done((f32[10,8,128]{2,1,0:T(8,128)S(1)}, f32[10,8,128]{2,1,0:T(8,128)S(1)}, u32[]{:S(2)}, u32[]{:S(2)}) %collective-permute-start.2) | collective-permute-done | bytes 40992 | tf_op jit(solution)/shard_map/ppermute | solution.py:387
  21.7 0.5 middle.1
  22.3 0.7 collective-permute-start.3
  22.9 0.7 collective-permute-start.4
  23.7 0.0 copy-start
  23.7 0.0 copy-start.1
  23.7 0.0 copy-start.2
  23.7 1.4 %collective-permute-start.8 = (f32[11,10,8,128]{3,2,1,0:T(8,128)S(1)}, f32[11,10,8,128]{3,2,1,0:T(8,128)S(1)}, u32[]{:S(2)}, u32[]{:S(2)}) collective-permute-start(f32[11,10,8,128]{3,2,1,0:T(8,128)S(1)} %get-tuple-element.44), channel_id=1, source_target_pairs={{64,0},{65,1},{66,2},{67,3},{68,4},{69,5},{70,6},{71,7},{72,8},{73... | collective-permute-start | bytes 1351688 | tf_op jit(solution)/shard_map/ppermute | solution.py:393
  25.1 0.0 collective-permute-done.4.map_ref
  25.1 0.6 decide.1
  25.7 0.7 collective-permute-start.5
  26.4 0.7 collective-permute-start.6
  27.0 1.3 %collective-permute-start.7 = (f32[10,8,128]{2,1,0:T(8,128)S(1)}, f32[10,8,128]{2,1,0:T(8,128)S(1)}, u32[]{:S(2)}, u32[]{:S(2)}) collective-permute-start(f32[10,8,128]{2,1,0:T(8,128)S(1)} %get-tuple-element.43), channel_id=1, source_target_pairs={{128,0},{129,1},{130,2},{131,3},{132,4},{133,5},{134,6},{135,7},{1... | collective-permute-start | bytes 122888 | tf_op jit(solution)/shard_map/ppermute | solution.py:405
  29.0 1.4 %place.1.pw_ref = f32[576,88]{1,0:T(8,128)S(1)} custom-call(s32[1]{0:T(128)S(6)} %copy.15.count_ref, f32[80,256]{1,0:T(8,128)S(1)} %bitcast.11, s32[1,256]{1,0:T(1,128)S(1)} %bitcast.12, s32[1,256]{1,0:T(1,128)S(1)} %bitcast.13), custom_call_target="tpu_custom_call" | custom-call | flops 50000000 | bytes 1000000 | tf_op jit(solution)/shard_map/place/pallas_call | solution.py:396
  30.4 15.7 %collective-permute-done.7.y10_ref = f32[10,8,128]{2,1,0:T(8,128)S(1)} collective-permute-done((f32[10,8,128]{2,1,0:T(8,128)S(1)}, f32[10,8,128]{2,1,0:T(8,128)S(1)}, u32[]{:S(2)}, u32[]{:S(2)}) %collective-permute-start.7) | collective-permute-done | bytes 40992 | tf_op jit(solution)/shard_map/ppermute | solution.py:405
  46.2 2.9 %finish.1 = (f32[10,8,8,128]{3,2,1,0:T(8,128)}, f32[576,128]{1,0:T(8,128)}) custom-call(s32[3]{0:T(128)S(1)} %pad_add_fusion.pos_ref, f32[10,8,128]{2,1,0:T(8,128)S(1)} %collective-permute-done.2.x_ref.b_ref.x1_ref, f32[10,8,128]{2,1,0:T(8,128)S(1)} %collective-permute-done.3.x_ref.x2_ref, f32[10,8,128]{2,1,0:T(8,128)S(1)} %collective-permute-done.5.x3_ref, ...), custom_call_target="tpu_custom_call" | custom-call | flops 5000000 | bytes 2000000 | tf_op jit(solution)/shard_map/finish/pallas_call | solution.py:406
  49.1 23.0 %all_to_all.5 = f32[64,9,1,128]{3,2,1,0:T(1,128)S(1)} all-to-all(f32[64,9,1,128]{3,2,1,0:T(1,128)} %bitcast.14), channel_id=1, replica_groups=mesh['wall'=4,'tile'=64] {'tile'}, dimensions={0} | all-to-all | bytes 589824 | tf_op jit(solution)/shard_map/all_to_all | solution.py:410
  72.1 0.7 pick.1
  72.8 0.2 collective-permute-start.10
  73.0 1.2 %collective-permute-start.11 = (f32[64,128]{1,0:T(8,128)S(1)}, f32[64,128]{1,0:T(8,128)S(1)}, u32[]{:S(2)}, u32[]{:S(2)}) collective-permute-start(f32[64,128]{1,0:T(8,128)S(1)} %pick.1), channel_id=1, source_target_pairs={{0,192},{64,0},{128,64},{192,128},{1,193},{65,1},{129,65},{193,129... | collective-permute-start | bytes 98312 | tf_op jit(solution)/shard_map/ppermute | solution.py:416
  74.2 0.9 %collective-permute-start.9 = (f32[64,128]{1,0:T(8,128)S(1)}, f32[64,128]{1,0:T(8,128)S(1)}, u32[]{:S(2)}, u32[]{:S(2)}) collective-permute-start(f32[64,128]{1,0:T(8,128)S(1)} %pick.1), channel_id=1, source_target_pairs={{0,64},{64,128},{128,192},{192,0},{1,65},{65,129},{129,193},{193,1... | collective-permute-start | bytes 98312 | tf_op jit(solution)/shard_map/ppermute | solution.py:416
  75.1 3.3 %collective-permute-done.10 = f32[64,128]{1,0:T(8,128)S(1)} collective-permute-done((f32[64,128]{1,0:T(8,128)S(1)}, f32[64,128]{1,0:T(8,128)S(1)}, u32[]{:S(2)}, u32[]{:S(2)}) %collective-permute-start.10) | collective-permute-done | bytes 32800 | tf_op jit(solution)/shard_map/ppermute | solution.py:416
  78.3 1.0 %collective-permute-done.9 = f32[64,128]{1,0:T(8,128)S(1)} collective-permute-done((f32[64,128]{1,0:T(8,128)S(1)}, f32[64,128]{1,0:T(8,128)S(1)}, u32[]{:S(2)}, u32[]{:S(2)}) %collective-permute-start.9) | collective-permute-done | bytes 32800 | tf_op jit(solution)/shard_map/ppermute | solution.py:416
  79.3 0.6 add_add_fusion
  (9 shorter events, 0.0 us)
Async XLA Ops:
  1.7 10.8 %collective-permute-start.1 = (f32[176,128]{1,0:T(8,128)S(1)}, f32[176,128]{1,0:T(8,128)S(1)}, u32[]{:S(2)}, u32[]{:S(2)}) collective-permute-start(f32[176,128]{1,0:T(8,128)S(1)} %get-tuple-element.25), channel_id=1, source_target_pairs={{1,0},{2,1},{3,2},{4,3},{5,4},{6,5},{7,6},{8,7},{9,8},{10,9},{11,1... | collective-permute-start | bytes 270344 | tf_op jit(solution)/shard_map/ppermute | solution.py:369
  7.3 6.1 %collective-permute-start = (f32[176,128]{1,0:T(8,128)S(1)}, f32[176,128]{1,0:T(8,128)S(1)}, u32[]{:S(2)}, u32[]{:S(2)}) collective-permute-start(f32[176,128]{1,0:T(8,128)S(1)} %get-tuple-element.29), channel_id=1, source_target_pairs={{0,1},{1,2},{2,3},{3,4},{4,5},{5,6},{6,7},{7,8},{8,9},{9,10},{10,1... | collective-permute-start | bytes 270344 | tf_op jit(solution)/shard_map/ppermute | solution.py:368
  15.4 6.3 %collective-permute-start.2 = (f32[10,8,128]{2,1,0:T(8,128)S(1)}, f32[10,8,128]{2,1,0:T(8,128)S(1)}, u32[]{:S(2)}, u32[]{:S(2)}) collective-permute-start(f32[10,8,128]{2,1,0:T(8,128)S(1)} %get-tuple-element.35), channel_id=1, source_target_pairs={{0,64},{192,128},{1,65},{193,129},{2,66},{194,130},{3,67},{195,131... | collective-permute-start | bytes 122888 | tf_op jit(solution)/shard_map/ppermute | solution.py:387
  22.3 1.4 %collective-permute-start.3 = (f32[10,8,128]{2,1,0:T(8,128)S(1)}, f32[10,8,128]{2,1,0:T(8,128)S(1)}, u32[]{:S(2)}, u32[]{:S(2)}) collective-permute-start(f32[10,8,128]{2,1,0:T(8,128)S(1)} %get-tuple-element.38), channel_id=1, source_target_pairs={{64,128},{65,129},{66,130},{67,131},{68,132},{69,133},{70,134},{71... | collective-permute-start | bytes 122888 | tf_op jit(solution)/shard_map/ppermute | solution.py:391
  22.9 2.2 %collective-permute-start.4 = (f32[10,10,8,128]{3,2,1,0:T(8,128)S(1)}, f32[10,10,8,128]{3,2,1,0:T(8,128)S(1)}, u32[]{:S(2)}, u32[]{:S(2)}) collective-permute-start(f32[10,10,8,128]{3,2,1,0:T(8,128)S(1)} %get-tuple-element.36.map_ref), channel_id=1, source_target_pairs={{192,128},{193,129},{194,130},{195,131},{196,132},{197,133},{198,1... | collective-permute-start | bytes 1228808 | tf_op jit(solution)/shard_map/ppermute | solution.py:381
  23.7 5.3 %copy-start = (f32[256,10,8]{0,2,1:T(8,128)S(1)}, f32[256,10,8]{0,2,1:T(8,128)}, u32[]{:S(2)}) copy-start(f32[256,10,8]{0,2,1:T(8,128)} %param.20) | copy-start | bytes 245764
  23.7 5.3 %copy-start.1 = (s32[256,1]{0,1:T(1,128)S(1)}, s32[256,1]{0,1:T(1,128)}, u32[]{:S(2)}) copy-start(s32[256,1]{0,1:T(1,128)} %param.21) | copy-start | bytes 3076
  23.7 5.3 %copy-start.2 = (s32[256]{0:T(256)S(1)}, s32[256]{0:T(256)}, u32[]{:S(2)}) copy-start(s32[256]{0:T(256)} %param.22) | copy-start | bytes 3076
  23.7 22.5 %collective-permute-start.8 = (f32[11,10,8,128]{3,2,1,0:T(8,128)S(1)}, f32[11,10,8,128]{3,2,1,0:T(8,128)S(1)}, u32[]{:S(2)}, u32[]{:S(2)}) collective-permute-start(f32[11,10,8,128]{3,2,1,0:T(8,128)S(1)} %get-tuple-element.44), channel_id=1, source_target_pairs={{64,0},{65,1},{66,2},{67,3},{68,4},{69,5},{70,6},{71,7},{72,8},{73... | collective-permute-start | bytes 1351688 | tf_op jit(solution)/shard_map/ppermute | solution.py:393
  25.7 4.7 %collective-permute-start.5 = (f32[10,8,128]{2,1,0:T(8,128)S(1)}, f32[10,8,128]{2,1,0:T(8,128)S(1)}, u32[]{:S(2)}, u32[]{:S(2)}) collective-permute-start(f32[10,8,128]{2,1,0:T(8,128)S(1)} %get-tuple-element.41), channel_id=1, source_target_pairs={{128,192},{129,193},{130,194},{131,195},{132,196},{133,197},{134,1... | collective-permute-start | bytes 122888 | tf_op jit(solution)/shard_map/ppermute | solution.py:403
  26.4 4.1 %collective-permute-start.6 = (f32[10,8,128]{2,1,0:T(8,128)S(1)}, f32[10,8,128]{2,1,0:T(8,128)S(1)}, u32[]{:S(2)}, u32[]{:S(2)}) collective-permute-start(f32[10,8,128]{2,1,0:T(8,128)S(1)} %get-tuple-element.43), channel_id=1, source_target_pairs={{128,64},{129,65},{130,66},{131,67},{132,68},{133,69},{134,70},{13... | collective-permute-start | bytes 122888 | tf_op jit(solution)/shard_map/ppermute | solution.py:404
  27.0 19.2 %collective-permute-start.7 = (f32[10,8,128]{2,1,0:T(8,128)S(1)}, f32[10,8,128]{2,1,0:T(8,128)S(1)}, u32[]{:S(2)}, u32[]{:S(2)}) collective-permute-start(f32[10,8,128]{2,1,0:T(8,128)S(1)} %get-tuple-element.43), channel_id=1, source_target_pairs={{128,0},{129,1},{130,2},{131,3},{132,4},{133,5},{134,6},{135,7},{1... | collective-permute-start | bytes 122888 | tf_op jit(solution)/shard_map/ppermute | solution.py:405
  72.8 5.5 %collective-permute-start.10 = (f32[64,128]{1,0:T(8,128)S(1)}, f32[64,128]{1,0:T(8,128)S(1)}, u32[]{:S(2)}, u32[]{:S(2)}) collective-permute-start(f32[64,128]{1,0:T(8,128)S(1)} %pick.1), channel_id=1, source_target_pairs={{0,128},{64,192},{128,0},{192,64},{1,129},{65,193},{129,1},{193,65... | collective-permute-start | bytes 98312 | tf_op jit(solution)/shard_map/ppermute | solution.py:416
  73.0 5.3 %collective-permute-start.11 = (f32[64,128]{1,0:T(8,128)S(1)}, f32[64,128]{1,0:T(8,128)S(1)}, u32[]{:S(2)}, u32[]{:S(2)}) collective-permute-start(f32[64,128]{1,0:T(8,128)S(1)} %pick.1), channel_id=1, source_target_pairs={{0,192},{64,0},{128,64},{192,128},{1,193},{65,1},{129,65},{193,129... | collective-permute-start | bytes 98312 | tf_op jit(solution)/shard_map/ppermute | solution.py:416
  74.2 5.1 %collective-permute-start.9 = (f32[64,128]{1,0:T(8,128)S(1)}, f32[64,128]{1,0:T(8,128)S(1)}, u32[]{:S(2)}, u32[]{:S(2)}) collective-permute-start(f32[64,128]{1,0:T(8,128)S(1)} %pick.1), channel_id=1, source_target_pairs={{0,64},{64,128},{128,192},{192,0},{1,65},{65,129},{129,193},{193,1... | collective-permute-start | bytes 98312 | tf_op jit(solution)/shard_map/ppermute | solution.py:416

commit v4 on v3

--- a/solution.py
+++ b/solution.py
@@ -156,51 +156,46 @@
         ]
         for k in range(K)
     ]
+    def depart(k):
+        if k >= 0:
+            for copy in blocks[k]:
+                copy.start()
+
+    def arrived(k):
+        for copy in blocks[k]:
+            copy.wait()
+
+    ahead = 2
     for copy in state:
         copy.start()
-    for k in range(K - 1, -1, -1):
-        for copy in blocks[k]:
-            copy.start()
+    for k in range(K - 1, K - 1 - ahead, -1):
+        depart(k)
     for k in range(K):
         w_ref[k] = jnp.broadcast_to(w_in[:, k : k + 1], (H, S))
     for copy in state:
         copy.wait()
+
+    @pl.when(wall != 3)
+    def _():
+        for k in range(K - 1 - ahead, -1, -1):
+            depart(k)
+
     interior(a_ref, src_ref, rad_ref, frq_ref, r_ref)
 
-    def arrived(k):
-        for copy in blocks[k]:
-            copy.wait()
-
-    @pl.when((wall == 0) | (wall == 2))
+    @pl.when(wall != 3)
     def _():
         for k in range(K - 1, -1, -1):
             arrived(k)
 
-    @pl.when(wall == 1)
+    @pl.when(wall == 3)
     def _():
         arrived(K - 1)
-        for c in range(NV):
-            s_ref[(K - 1) % 2, c] = u_ref[:, c, K - 1]
-        for k in range(K - 2, -1, -1):
-            arrived(k)
-
-            @pl.loop(0, NV // 2)
-            def _(pair):
-                cols = [2 * pair, 2 * pair + 1]
-                outs = pair_dot(u_ref, k, [s_ref[(k + 1) % 2, c] for c in cols])
-                for c, out in zip(cols, outs):
-                    if k > 0:
-                        s_ref[k % 2, c] = out
-                    else:
-                        map_ref[c] = out
-
-    @pl.when(wall == 3)
-    def _():
-        arrived(K - 1)
+        depart(K - 1 - ahead)
         for c in range(NV):
             s_ref[(K - 1) % 2, c] = d_ref[:, c, K - 1]
         for k in range(K - 2, -1, -1):
             arrived(k)
+            depart(k - ahead)
 
             @pl.loop(0, NV // 2)
             def _(pair):
@@ -217,7 +212,7 @@
                 map_ref[c] = out
 
 
-def residual_kernel(pos_ref, r_ref, left_ref, right_ref, rad_ref, l_ref, d_ref, u_ref, out_ref, msg_ref, s_ref):
+def residual_kernel(pos_ref, map_ref, r_ref, left_ref, right_ref, rad_ref, l_ref, d_ref, u_ref, out_ref, up_ref, down_ref, s_ref):
     wall, tile, last = pos_ref[0], pos_ref[1], pos_ref[2]
     row = lax.broadcasted_iota(jnp.int32, (H, S), 0)
     has_left = tile > 0
@@ -245,25 +240,46 @@
     @pl.when((wall == 0) | (wall == 3))
     def _():
         f = forward_sweep(l_ref, d_ref, out_ref, s_ref, None)
-        b, _ = backward_sweep(u_ref, s_ref, None, None)
-        msg_ref[...] = jnp.where(wall == 0, f, b)
-
-
-def middle_kernel(pos_ref, x_ref, map_ref, r_ref, l_ref, d_ref, u_ref, out_ref, below_ref, s_ref):
+        up_ref[...] = f
+        down_ref[NV] = backward_sweep(u_ref, s_ref, None, None)[0]
+
+    @pl.when(wall == 3)
+    def _():
+        for c in range(NV):
+            down_ref[c] = map_ref[c]
+
+
+def middle_kernel(pos_ref, x_ref, r_ref, l_ref, d_ref, u_ref, out_ref, s_ref):
     @pl.when(pos_ref[0] == 1)
     def _():
-        out_ref[...] = forward_sweep(l_ref, d_ref, r_ref, s_ref, x_ref[...])
+        f = x_ref[...]
+        for k in range(K):
+            f = r_ref[:, k] + block_dot(l_ref, k, f)
+        out_ref[...] = f
+
+
+def below_kernel(pos_ref, x_ref, r_ref, l_ref, d_ref, u_ref, below_ref, s_ref):
+    @pl.when(pos_ref[0] == 1)
+    def _():
+        forward_sweep(l_ref, d_ref, r_ref, s_ref, x_ref[...])
         below_ref[NV] = backward_sweep(u_ref, s_ref, None, None)[0]
-        for c in range(NV):
-            below_ref[c] = map_ref[c]
-
-
-def decide_kernel(pos_ref, x_ref, b_ref, map_ref, r_ref, l_ref, d_ref, u_ref, x3_ref, y2_ref, y1_ref, s_ref):
+
+        @pl.loop(0, NV // 2)
+        def _(pair):
+            cols = [2 * pair, 2 * pair + 1]
+            xs = [u_ref[:, c, K - 1] for c in cols]
+            for k in range(K - 2, -1, -1):
+                xs = pair_dot(u_ref, k, xs)
+            for c, x in zip(cols, xs):
+                below_ref[c] = x
+
+
+def decide_kernel(pos_ref, x_ref, map_ref, r_ref, l_ref, d_ref, u_ref, x3_ref, y2_ref, y1_ref, s_ref):
     @pl.when(pos_ref[0] == 2)
     def _():
         x3 = forward_sweep(l_ref, d_ref, r_ref, s_ref, x_ref[...])
         x3_ref[...] = x3
-        y2 = b_ref[...] + map_dot(map_ref, 0, x3)
+        y2 = map_ref[NV] + map_dot(map_ref, 0, x3)
         y2_ref[...] = y2
         y1_ref[...] = backward_sweep(u_ref, s_ref, None, y2)[0]
 
@@ -377,39 +393,39 @@
         ),
         flops=30_000_000, nbytes=11_000_000,
     )(pos1, wall_weight, adjoint, source, radius, frequency, lower, diag, upper)
-    maps, left, right = tie((maps, left, right))
-    map3 = lax.ppermute(maps, "wall", [(3, 2)])
-
-    resid, first = call(
-        "residual", residual_kernel, (state, vec), 8, smem=(0,), scratch=(levels,),
-        flops=6_000_000, nbytes=2_000_000,
-    )(pos, inner, left, right, radius, lower, diag, upper)
-    x1 = b3 = lax.ppermute(first, "wall", [(0, 1), (3, 2)])
-    x2, below = call(
-        "middle", middle_kernel, (vec, f32(NV + 1, NV, H, S)), 7, smem=(0,), scratch=(levels,), flops=5_000_000, nbytes=2_000_000
-    )(pos, x1, maps, resid, lower, diag, upper)
+
+    resid, up, down = call(
+        "residual", residual_kernel, (state, vec, f32(NV + 1, NV, H, S)), 9, smem=(0,), scratch=(levels,)
+    )(pos, maps, inner, left, right, radius, lower, diag, upper)
+    x1 = lax.ppermute(up, "wall", [(0, 1)])
+    above = lax.ppermute(down, "wall", [(3, 2)])
+    x2 = call("middle", middle_kernel, vec, 6, smem=(0,), scratch=(levels,))(pos, x1, resid, lower, diag, upper)
+    x2, pos2 = tie((x2, pos))
     x2 = lax.ppermute(x2, "wall", [(1, 2)])
-    x2, below = tie((x2, below))
+    below = call("below", below_kernel, f32(NV + 1, NV, H, S), 6, smem=(0,), scratch=(levels,))(
+        pos2, x1, resid, lower, diag, upper
+    )
+    swt = surface_weight.transpose(1, 2, 0).reshape(NV * H, -1)
+    placed = call("place", place_kernel, held(tiles * ROWS_PER_OWNER, NV * H + SLOTS), 4, smem=(0,))(
+        surface_count, swt, patch_owner.reshape(1, -1), patch_row.reshape(1, -1)
+    )
+
+    x2, placed = tie((x2, placed))
+    x3, y2, y1 = call(
+        "decide", decide_kernel, (vec, vec, vec), 7, smem=(0,), scratch=(levels,)
+    )(pos, x2, above, resid, lower, diag, upper)
+    x3, below = tie((x3, below))
     below = lax.ppermute(below, "wall", [(1, 0)])
-
-    swt = surface_weight.transpose(1, 2, 0).reshape(NV * H, -1)
-    placed = call(
-        "place", place_kernel, held(tiles * ROWS_PER_OWNER, NV * H + SLOTS), 4, smem=(0,), flops=50_000_000, nbytes=1_000_000
-    )(surface_count, swt, patch_owner.reshape(1, -1), patch_row.reshape(1, -1))
-
-    x3, y2, y1 = call(
-        "decide", decide_kernel, (vec, vec, vec), 8, smem=(0,), scratch=(levels,), flops=20_000_000, nbytes=3_000_000,
-    )(pos, x2, b3, map3, resid, lower, diag, upper)
     x3 = lax.ppermute(x3, "wall", [(2, 3)])
     y11 = lax.ppermute(y1, "wall", [(2, 1)])
     y10 = lax.ppermute(y1, "wall", [(2, 0)])
     adjoint_next, rows = call(
         "finish", finish_kernel, (f32(NV, K, H, S), away(tiles * ROWS_PER_OWNER, S)), 14, smem=(0,),
-        scratch=(levels, held(NV, H, S), held(NV, H, S), held(NV * H + SLOTS, S)), flops=5_000_000, nbytes=2_000_000,
+        scratch=(levels, held(NV, H, S), held(NV, H, S), held(NV * H + SLOTS, S)),
     )(pos, x1, x2, x3, y2, y11, y10, below, weight, placed, resid, lower, diag, upper)
     got = lax.all_to_all(rows.reshape(tiles, ROWS_PER_OWNER, 1, S), "tile", split_axis=0, concat_axis=0)
     got = got.reshape(tiles * ROWS_PER_OWNER, S)
-    part = call("pick", pick_kernel, f32(PATCH_DEV, S), 1, flops=20_000_000, nbytes=400_000)(got)
+    part = call("pick", pick_kernel, f32(PATCH_DEV, S), 1)(got)
     walls = lax.axis_size("wall")
     patch = part
     for d in range(1, walls):

time: 80.4 us -> 74.4 us (0.925)
  waiting for transfers between devices: 22.6 us -> 18.9 us
  starting transfers between devices: 17.9 us -> 15.4 us
  blocking collectives: 23 us -> 21.7 us
  Pallas kernels: 14.3 us -> 15.6 us
    ppermute x1, waiting for transfers between devices: 15.7 us -> 12.7 us  [on_device(): y10 = lax.ppermute(y1, 'wall', [(2, 0)])]
    ppermute x2, starting transfers between devices: 5.35 us -> 3.06 us  [the longest x1 2.37 us: on_device(): x1 = lax.ppermute(up, 'wall', [(0, 1)])]
    all_to_all x1, blocking collectives: 23 us -> 21.7 us  [on_device(): lax.all_to_all(rows.reshape(tiles, ROWS_PER_OWNER, 1, S), 'tile', split_a...]
    ppermute x1, waiting for transfers between devices: 0.88 us -> 0.01 us  [on_device(): lax.ppermute(hi, 'tile', [(i, (i + 1) % tiles) for i in range(tiles)])]
    pallas_call x4 -> x5, Pallas kernels: 3.81 us -> 4.36 us  [the longest x1 2.03 us: on_device(): call('residual', residual_kernel, (state, vec, f32(NV + 1, NV, H, S)), 9,...]
  transfers between devices with their start and end apart: 12 -> 12, of which waited for: 5 -> 5; matrix products, arithmetic and copies ran while one was open for 0% -> 0% of each run, Pallas kernels for 9% -> 11%
where the time goes in v4:
time: 74.4 us; the launch traced here: 73.8 us
  blocking collectives  21.7 us (29%)
  waiting for transfers between devices  18.9 us (25%)
  Pallas kernels  15.6 us (21%)
  starting transfers between devices  15.4 us (21%)
  between operations  1.47 us (2%)
    all_to_all x1, blocking collectives, on_device(): lax.all_to_all(rows.reshape(tiles, ROWS_PER_OWNER, 1, S), 'tile', split_a...  21.7 us
    ppermute x1, waiting for transfers between devices, on_device(): y10 = lax.ppermute(y1, 'wall', [(2, 0)])  12.7 us
    pallas_call x1, Pallas kernels, on_device(): call('start', start_kernel, (block, block, block, state, cell, f32(NV, NV...  5.82 us
    ppermute x1, starting transfers between devices, on_device(): lax.ppermute(lo, 'tile', [((i + 1) % tiles, i) for i in range(tiles)])  5.64 us
    ppermute x3, waiting for transfers between devices, on_device(): lax.ppermute(part, 'wall', [(w, (w + d) % walls) for w in range(walls)])  4.56 us
    pallas_call x1, Pallas kernels, on_device(): call('finish', finish_kernel, (f32(NV, K, H, S), away(tiles * ROWS_PER_OW...  2.94 us
    ppermute x1, starting transfers between devices, on_device(): x1 = lax.ppermute(up, 'wall', [(0, 1)])  2.37 us
    ppermute x3, starting transfers between devices, on_device(): lax.ppermute(part, 'wall', [(w, (w + d) % walls) for w in range(walls)])  2.09 us
  transfers between devices with their start and end apart: 12, of which 5 were waited for; matrix products, arithmetic and copies ran while one was open for 0% of the time, Pallas kernels for 11%

profile of v4, /device:TPU:6, one launch (start us, length us, event | category | flops | bytes accessed | tf_op | source)
XLA Modules:
  0.0 73.8 jit_solution(11407671209714464033)
XLA Ops:
  0.6 1.0 %pack.1 = (f32[176,128]{1,0:T(8,128)S(1)}, f32[176,128]{1,0:T(8,128)S(1)}) custom-call(f32[10,8,8,128]{3,2,1,0:T(8,128)} %a_in.1, f32[8,8,128]{2,1,0:T(8,128)} %rad_ref.3), custom_call_target="tpu_custom_call" | custom-call | bytes 800000 | tf_op jit(solution)/shard_map/pack/pallas_call | solution.py:383
  1.7 0.1 collective-permute-start
  1.7 5.6 %collective-permute-start.1 = (f32[176,128]{1,0:T(8,128)S(1)}, f32[176,128]{1,0:T(8,128)S(1)}, u32[]{:S(2)}, u32[]{:S(2)}) collective-permute-start(f32[176,128]{1,0:T(8,128)S(1)} %get-tuple-element.25), channel_id=1, source_target_pairs={{1,0},{2,1},{3,2},{4,3},{5,4},{6,5},{7,6},{8,7},{9,8},{10,9},{11,1... | collective-permute-start | bytes 270344 | tf_op jit(solution)/shard_map/ppermute | solution.py:385
  7.4 0.1 pad_add_fusion.pos_ref
  7.5 5.8 %start.1 = (f32[10,10,8,8,128]{4,3,2,1,0:T(8,128)S(1)}, f32[10,10,8,8,128]{4,3,2,1,0:T(8,128)S(1)}, f32[10,10,8,8,128]{4,3,2,1,0:T(8,128)S(1)}, f32[10,8,8,128]{...) custom-call(s32[3]{0:T(128)S(1)} %pad_add_fusion.pos_ref, f32[1,8]{1,0:T(1,128)} %bitcast.15, ...), custom_call_target="tpu_custom_call" | custom-call | flops 30000000 | bytes 11000000 | tf_op jit(solution)/shard_map/start/pallas_call | solution.py:388
  13.3 0.0 collective-permute-done.1.right_ref
  13.3 2.0 %residual.1 = (f32[10,8,8,128]{3,2,1,0:T(8,128)S(1)}, f32[10,8,128]{2,1,0:T(8,128)S(1)}, f32[11,10,8,128]{3,2,1,0:T(8,128)S(1)}) custom-call(s32[3]{0:T(128)S(1)} %pad_add_fusion.pos_ref, f32[10,10,8,128]{3,2,1,0:T(8,128)S(1)} %get-tuple-element.27.map_ref, f32[10,8,8,128]{3,2,1,0:T(8,128)S(1)} %get-tuple-element.28.r_ref, ...), custom_call_target="tpu_custom_call" | custom-call | tf_op jit(solution)/shard_map/residual/pallas_call | solution.py:397
  15.3 0.7 collective-permute-start.4
  16.0 2.4 %collective-permute-start.2 = (f32[10,8,128]{2,1,0:T(8,128)S(1)}, f32[10,8,128]{2,1,0:T(8,128)S(1)}, u32[]{:S(2)}, u32[]{:S(2)}) collective-permute-start(f32[10,8,128]{2,1,0:T(8,128)S(1)} %get-tuple-element.33), channel_id=1, source_target_pairs={{0,64},{1,65},{2,66},{3,67},{4,68},{5,69},{6,70},{7,71},{8,72},{9,... | collective-permute-start | bytes 122888 | tf_op jit(solution)/shard_map/ppermute | solution.py:400
  18.4 1.7 %collective-permute-done.2.x_ref.x1_ref = f32[10,8,128]{2,1,0:T(8,128)S(1)} collective-permute-done((f32[10,8,128]{2,1,0:T(8,128)S(1)}, f32[10,8,128]{2,1,0:T(8,128)S(1)}, u32[]{:S(2)}, u32[]{:S(2)}) %collective-permute-start.2) | collective-permute-done | bytes 40992 | tf_op jit(solution)/shard_map/ppermute | solution.py:400
  20.1 0.5 middle.1
  20.6 0.7 collective-permute-start.3
  22.0 1.4 %place.1.pw_ref = f32[576,88]{1,0:T(8,128)S(1)} custom-call(s32[1]{0:T(128)S(6)} %copy.15.count_ref, f32[80,256]{1,0:T(8,128)S(1)} %bitcast.11, s32[1,256]{1,0:T(1,128)S(1)} %bitcast.12, s32[1,256]{1,0:T(1,128)S(1)} %bitcast.13), custom_call_target="tpu_custom_call" | custom-call | tf_op jit(solution)/shard_map/place/pallas_call | solution.py:409
  23.4 0.6 below.1
  24.0 0.0 collective-permute-done.3.x_ref.x2_ref
  24.0 0.6 decide.1
  24.5 1.3 %collective-permute-start.8 = (f32[11,10,8,128]{3,2,1,0:T(8,128)S(1)}, f32[11,10,8,128]{3,2,1,0:T(8,128)S(1)}, u32[]{:S(2)}, u32[]{:S(2)}) collective-permute-start(f32[11,10,8,128]{3,2,1,0:T(8,128)S(1)} %below.1), channel_id=1, source_target_pairs={{64,0},{65,1},{66,2},{67,3},{68,4},{69,5},{70,6},{71,7},{72,8},{73... | collective-permute-start | bytes 1351688 | tf_op jit(solution)/shard_map/ppermute | solution.py:418
  25.8 0.7 collective-permute-start.5
  26.5 0.7 collective-permute-start.6
  27.2 1.3 %collective-permute-start.7 = (f32[10,8,128]{2,1,0:T(8,128)S(1)}, f32[10,8,128]{2,1,0:T(8,128)S(1)}, u32[]{:S(2)}, u32[]{:S(2)}) collective-permute-start(f32[10,8,128]{2,1,0:T(8,128)S(1)} %get-tuple-element.42), channel_id=1, source_target_pairs={{128,0},{129,1},{130,2},{131,3},{132,4},{133,5},{134,6},{135,7},{1... | collective-permute-start | bytes 122888 | tf_op jit(solution)/shard_map/ppermute | solution.py:421
  28.5 0.0 collective-permute-done.5.x3_ref
  28.5 12.7 %collective-permute-done.7.y10_ref = f32[10,8,128]{2,1,0:T(8,128)S(1)} collective-permute-done((f32[10,8,128]{2,1,0:T(8,128)S(1)}, f32[10,8,128]{2,1,0:T(8,128)S(1)}, u32[]{:S(2)}, u32[]{:S(2)}) %collective-permute-start.7) | collective-permute-done | bytes 40992 | tf_op jit(solution)/shard_map/ppermute | solution.py:421
  41.2 2.9 %finish.1 = (f32[10,8,8,128]{3,2,1,0:T(8,128)}, f32[576,128]{1,0:T(8,128)}) custom-call(s32[3]{0:T(128)S(1)} %pad_add_fusion.pos_ref, f32[10,8,128]{2,1,0:T(8,128)S(1)} %collective-permute-done.2.x_ref.x1_ref, f32[10,8,128]{2,1,0:T(8,128)S(1)} %collective-permute-done.3.x_ref.x2_ref, f32[10,8,128]{2,1,0:T(8,128)S(1)} %collective-permute-done.5.x3_ref, ...), custom_call_target="tpu_custom_call" | custom-call | tf_op jit(solution)/shard_map/finish/pallas_call | solution.py:422
  44.1 21.7 %all_to_all.5 = f32[64,9,1,128]{3,2,1,0:T(1,128)S(1)} all-to-all(f32[64,9,1,128]{3,2,1,0:T(1,128)} %bitcast.14), channel_id=1, replica_groups=mesh['wall'=4,'tile'=64] {'tile'}, dimensions={0} | all-to-all | bytes 589824 | tf_op jit(solution)/shard_map/all_to_all | solution.py:426
  65.8 0.7 pick.1
  66.5 0.1 collective-permute-start.11
  66.6 1.1 %collective-permute-start.10 = (f32[64,128]{1,0:T(8,128)S(1)}, f32[64,128]{1,0:T(8,128)S(1)}, u32[]{:S(2)}, u32[]{:S(2)}) collective-permute-start(f32[64,128]{1,0:T(8,128)S(1)} %pick.1), channel_id=1, source_target_pairs={{0,128},{64,192},{128,0},{192,64},{1,129},{65,193},{129,1},{193,65... | collective-permute-start | bytes 98312 | tf_op jit(solution)/shard_map/ppermute | solution.py:432
  67.7 0.9 %collective-permute-start.9 = (f32[64,128]{1,0:T(8,128)S(1)}, f32[64,128]{1,0:T(8,128)S(1)}, u32[]{:S(2)}, u32[]{:S(2)}) collective-permute-start(f32[64,128]{1,0:T(8,128)S(1)} %pick.1), channel_id=1, source_target_pairs={{0,64},{64,128},{128,192},{192,0},{1,65},{65,129},{129,193},{193,1... | collective-permute-start | bytes 98312 | tf_op jit(solution)/shard_map/ppermute | solution.py:432
  68.6 1.9 %collective-permute-done.11 = f32[64,128]{1,0:T(8,128)S(1)} collective-permute-done((f32[64,128]{1,0:T(8,128)S(1)}, f32[64,128]{1,0:T(8,128)S(1)}, u32[]{:S(2)}, u32[]{:S(2)}) %collective-permute-start.11) | collective-permute-done | bytes 32800 | tf_op jit(solution)/shard_map/ppermute | solution.py:432
  70.5 1.7 %collective-permute-done.10 = f32[64,128]{1,0:T(8,128)S(1)} collective-permute-done((f32[64,128]{1,0:T(8,128)S(1)}, f32[64,128]{1,0:T(8,128)S(1)}, u32[]{:S(2)}, u32[]{:S(2)}) %collective-permute-start.10) | collective-permute-done | bytes 32800 | tf_op jit(solution)/shard_map/ppermute | solution.py:432
  72.2 1.0 %collective-permute-done.9 = f32[64,128]{1,0:T(8,128)S(1)} collective-permute-done((f32[64,128]{1,0:T(8,128)S(1)}, f32[64,128]{1,0:T(8,128)S(1)}, u32[]{:S(2)}, u32[]{:S(2)}) %collective-permute-start.9) | collective-permute-done | bytes 32800 | tf_op jit(solution)/shard_map/ppermute | solution.py:432
  73.1 0.6 add_add_fusion
  (10 shorter events, 0.0 us)
Async XLA Ops:
  1.7 11.6 %collective-permute-start = (f32[176,128]{1,0:T(8,128)S(1)}, f32[176,128]{1,0:T(8,128)S(1)}, u32[]{:S(2)}, u32[]{:S(2)}) collective-permute-start(f32[176,128]{1,0:T(8,128)S(1)} %get-tuple-element.29), channel_id=1, source_target_pairs={{0,1},{1,2},{2,3},{3,4},{4,5},{5,6},{6,7},{7,8},{8,9},{9,10},{10,1... | collective-permute-start | bytes 270344 | tf_op jit(solution)/shard_map/ppermute | solution.py:384
  1.7 11.6 %collective-permute-start.1 = (f32[176,128]{1,0:T(8,128)S(1)}, f32[176,128]{1,0:T(8,128)S(1)}, u32[]{:S(2)}, u32[]{:S(2)}) collective-permute-start(f32[176,128]{1,0:T(8,128)S(1)} %get-tuple-element.25), channel_id=1, source_target_pairs={{1,0},{2,1},{3,2},{4,3},{5,4},{6,5},{7,6},{8,7},{9,8},{10,9},{11,1... | collective-permute-start | bytes 270344 | tf_op jit(solution)/shard_map/ppermute | solution.py:385
  15.3 8.6 %collective-permute-start.4 = (f32[11,10,8,128]{3,2,1,0:T(8,128)S(1)}, f32[11,10,8,128]{3,2,1,0:T(8,128)S(1)}, u32[]{:S(2)}, u32[]{:S(2)}) collective-permute-start(f32[11,10,8,128]{3,2,1,0:T(8,128)S(1)} %get-tuple-element.37), channel_id=1, source_target_pairs={{192,128},{193,129},{194,130},{195,131},{196,132},{197,133},{198,1... | collective-permute-start | bytes 1351688 | tf_op jit(solution)/shard_map/ppermute | solution.py:401
  16.0 4.0 %collective-permute-start.2 = (f32[10,8,128]{2,1,0:T(8,128)S(1)}, f32[10,8,128]{2,1,0:T(8,128)S(1)}, u32[]{:S(2)}, u32[]{:S(2)}) collective-permute-start(f32[10,8,128]{2,1,0:T(8,128)S(1)} %get-tuple-element.33), channel_id=1, source_target_pairs={{0,64},{1,65},{2,66},{3,67},{4,68},{5,69},{6,70},{7,71},{8,72},{9,... | collective-permute-start | bytes 122888 | tf_op jit(solution)/shard_map/ppermute | solution.py:400
  20.1 1.9 %copy-start = (f32[256,10,8]{0,2,1:T(8,128)S(1)}, f32[256,10,8]{0,2,1:T(8,128)}, u32[]{:S(2)}) copy-start(f32[256,10,8]{0,2,1:T(8,128)} %param.20) | copy-start | bytes 245764
  20.1 1.9 %copy-start.1 = (s32[256,1]{0,1:T(1,128)S(1)}, s32[256,1]{0,1:T(1,128)}, u32[]{:S(2)}) copy-start(s32[256,1]{0,1:T(1,128)} %param.21) | copy-start | bytes 3076
  20.1 1.9 %copy-start.2 = (s32[256]{0:T(256)S(1)}, s32[256]{0:T(256)}, u32[]{:S(2)}) copy-start(s32[256]{0:T(256)} %param.22) | copy-start | bytes 3076
  20.6 3.3 %collective-permute-start.3 = (f32[10,8,128]{2,1,0:T(8,128)S(1)}, f32[10,8,128]{2,1,0:T(8,128)S(1)}, u32[]{:S(2)}, u32[]{:S(2)}) collective-permute-start(f32[10,8,128]{2,1,0:T(8,128)S(1)} %middle.1), channel_id=1, source_target_pairs={{64,128},{65,129},{66,130},{67,131},{68,132},{69,133},{70,134},{71... | collective-permute-start | bytes 122888 | tf_op jit(solution)/shard_map/ppermute | solution.py:404
  24.5 16.6 %collective-permute-start.8 = (f32[11,10,8,128]{3,2,1,0:T(8,128)S(1)}, f32[11,10,8,128]{3,2,1,0:T(8,128)S(1)}, u32[]{:S(2)}, u32[]{:S(2)}) collective-permute-start(f32[11,10,8,128]{3,2,1,0:T(8,128)S(1)} %below.1), channel_id=1, source_target_pairs={{64,0},{65,1},{66,2},{67,3},{68,4},{69,5},{70,6},{71,7},{72,8},{73... | collective-permute-start | bytes 1351688 | tf_op jit(solution)/shard_map/ppermute | solution.py:418
  25.8 2.6 %collective-permute-start.5 = (f32[10,8,128]{2,1,0:T(8,128)S(1)}, f32[10,8,128]{2,1,0:T(8,128)S(1)}, u32[]{:S(2)}, u32[]{:S(2)}) collective-permute-start(f32[10,8,128]{2,1,0:T(8,128)S(1)} %get-tuple-element.40), channel_id=1, source_target_pairs={{128,192},{129,193},{130,194},{131,195},{132,196},{133,197},{134,1... | collective-permute-start | bytes 122888 | tf_op jit(solution)/shard_map/ppermute | solution.py:419
  26.5 2.0 %collective-permute-start.6 = (f32[10,8,128]{2,1,0:T(8,128)S(1)}, f32[10,8,128]{2,1,0:T(8,128)S(1)}, u32[]{:S(2)}, u32[]{:S(2)}) collective-permute-start(f32[10,8,128]{2,1,0:T(8,128)S(1)} %get-tuple-element.42), channel_id=1, source_target_pairs={{128,64},{129,65},{130,66},{131,67},{132,68},{133,69},{134,70},{13... | collective-permute-start | bytes 122888 | tf_op jit(solution)/shard_map/ppermute | solution.py:420
  27.2 14.0 %collective-permute-start.7 = (f32[10,8,128]{2,1,0:T(8,128)S(1)}, f32[10,8,128]{2,1,0:T(8,128)S(1)}, u32[]{:S(2)}, u32[]{:S(2)}) collective-permute-start(f32[10,8,128]{2,1,0:T(8,128)S(1)} %get-tuple-element.42), channel_id=1, source_target_pairs={{128,0},{129,1},{130,2},{131,3},{132,4},{133,5},{134,6},{135,7},{1... | collective-permute-start | bytes 122888 | tf_op jit(solution)/shard_map/ppermute | solution.py:421
  66.5 4.0 %collective-permute-start.11 = (f32[64,128]{1,0:T(8,128)S(1)}, f32[64,128]{1,0:T(8,128)S(1)}, u32[]{:S(2)}, u32[]{:S(2)}) collective-permute-start(f32[64,128]{1,0:T(8,128)S(1)} %pick.1), channel_id=1, source_target_pairs={{0,192},{64,0},{128,64},{192,128},{1,193},{65,1},{129,65},{193,129... | collective-permute-start | bytes 98312 | tf_op jit(solution)/shard_map/ppermute | solution.py:432
  66.6 5.6 %collective-permute-start.10 = (f32[64,128]{1,0:T(8,128)S(1)}, f32[64,128]{1,0:T(8,128)S(1)}, u32[]{:S(2)}, u32[]{:S(2)}) collective-permute-start(f32[64,128]{1,0:T(8,128)S(1)} %pick.1), channel_id=1, source_target_pairs={{0,128},{64,192},{128,0},{192,64},{1,129},{65,193},{129,1},{193,65... | collective-permute-start | bytes 98312 | tf_op jit(solution)/shard_map/ppermute | solution.py:432
  67.7 5.4 %collective-permute-start.9 = (f32[64,128]{1,0:T(8,128)S(1)}, f32[64,128]{1,0:T(8,128)S(1)}, u32[]{:S(2)}, u32[]{:S(2)}) collective-permute-start(f32[64,128]{1,0:T(8,128)S(1)} %pick.1), channel_id=1, source_target_pairs={{0,64},{64,128},{128,192},{192,0},{1,65},{65,129},{129,193},{193,1... | collective-permute-start | bytes 98312 | tf_op jit(solution)/shard_map/ppermute | solution.py:432

commit v5 on v4

--- a/solution.py
+++ b/solution.py
@@ -68,6 +68,13 @@
     return f
 
 
+def forward_chain(l_ref, r_ref, f):
+    for k in range(K):
+        r = r_ref[:, k]
+        f = r if f is None else r + block_dot(l_ref, k, f)
+    return f
+
+
 def backward_sweep(u_ref, s_ref, w_ref, y, emit=None):
     b, p = y, None
     for k in range(K - 1, -1, -1):
@@ -107,10 +114,10 @@
     return accs
 
 
-def pair_map(m_ref, half, xs):
+def pair_map(m_ref, xs):
     accs = [None] * len(xs)
     for j in range(NV):
-        m = m_ref[half, j]
+        m = m_ref[j]
         for n, x in enumerate(xs):
             term = m * x[j][None]
             accs[n] = term if accs[n] is None else accs[n] + term
@@ -142,44 +149,43 @@
 
 def start_kernel(
     pos_ref, w_in, a_in, src_in, rad_in, frq_in, l_in, d_in, u_in,
-    l_ref, d_ref, u_ref, r_ref, w_ref, map_ref, a_ref, src_ref, rad_ref, frq_ref, s_ref, state_sems, block_sems,
+    l_ref, d_ref, u_ref, r_ref, w_ref, map_ref, a_ref, src_ref, rad_ref, frq_ref, s0_ref, s1_ref, state_sems, block_sems,
 ):
     wall = pos_ref[0]
     state = [
         pltpu.make_async_copy(there, here, state_sems.at[n])
         for n, (there, here) in enumerate(((a_in, a_ref), (src_in, src_ref), (rad_in, rad_ref), (frq_in, frq_ref)))
     ]
-    blocks = [
-        [
+    def block_copies(k):
+        pairs = ((l_in, l_ref), (d_in, d_ref), (u_in, u_ref))
+        return [
             pltpu.make_async_copy(there.at[:, :, k], here.at[:, :, k], block_sems.at[k, n])
-            for n, (there, here) in enumerate(((l_in, l_ref), (d_in, d_ref), (u_in, u_ref)))
+            for n, (there, here) in enumerate(pairs)
         ]
-        for k in range(K)
-    ]
+
     def depart(k):
-        if k >= 0:
-            for copy in blocks[k]:
-                copy.start()
+        for copy in block_copies(k):
+            copy.start()
 
     def arrived(k):
-        for copy in blocks[k]:
+        for copy in block_copies(k):
             copy.wait()
 
-    ahead = 2
+    ahead = 3
     for copy in state:
         copy.start()
     for k in range(K - 1, K - 1 - ahead, -1):
         depart(k)
+
+    @pl.when(wall != 3)
+    def _():
+        for k in range(K - 1 - ahead, -1, -1):
+            depart(k)
+
     for k in range(K):
         w_ref[k] = jnp.broadcast_to(w_in[:, k : k + 1], (H, S))
     for copy in state:
         copy.wait()
-
-    @pl.when(wall != 3)
-    def _():
-        for k in range(K - 1 - ahead, -1, -1):
-            depart(k)
-
     interior(a_ref, src_ref, rad_ref, frq_ref, r_ref)
 
     @pl.when(wall != 3)
@@ -189,26 +195,34 @@
 
     @pl.when(wall == 3)
     def _():
+        pairs = [(c, c + 1) for c in range(0, NV, 2)]
+
+        def descend(k, old_ref, new_ref):
+            arrived(k)
+
+            @pl.when(k >= ahead)
+            def _():
+                depart(k - ahead)
+
+            for cols in pairs:
+                outs = pair_map(old_ref, [l_ref[:, c, k + 1] for c in cols])
+                outs = pair_dot(u_ref, k, outs)
+                for c, out in zip(cols, outs):
+                    new_ref[c] = d_ref[:, c, k] - out
+
         arrived(K - 1)
         depart(K - 1 - ahead)
         for c in range(NV):
-            s_ref[(K - 1) % 2, c] = d_ref[:, c, K - 1]
-        for k in range(K - 2, -1, -1):
-            arrived(k)
-            depart(k - ahead)
-
-            @pl.loop(0, NV // 2)
-            def _(pair):
-                cols = [2 * pair, 2 * pair + 1]
-                outs = pair_map(s_ref, (k + 1) % 2, [l_ref[:, c, k + 1] for c in cols])
-                outs = pair_dot(u_ref, k, outs)
-                for c, out in zip(cols, outs):
-                    s_ref[k % 2, c] = d_ref[:, c, k] - out
-
-        @pl.loop(0, NV // 2)
-        def _(pair):
-            cols = [2 * pair, 2 * pair + 1]
-            for c, out in zip(cols, pair_map(s_ref, 0, [l_ref[:, c, 0] for c in cols])):
+            s0_ref[c] = d_ref[:, c, K - 1]
+
+        @pl.loop(0, K // 2 - 1)
+        def _(step):
+            descend(K - 2 - 2 * step, s0_ref, s1_ref)
+            descend(K - 3 - 2 * step, s1_ref, s0_ref)
+
+        descend(jnp.int32(0), s0_ref, s1_ref)
+        for cols in pairs:
+            for c, out in zip(cols, pair_map(s1_ref, [l_ref[:, c, 0] for c in cols])):
                 map_ref[c] = out
 
 
@@ -237,25 +251,22 @@
             applied = applied + (f_r0 * line(right_ref, v, k, 0) + f_r1 * line(right_ref, v, k, 1))
             out_ref[v, k] = r_ref[v, k] - applied
 
-    @pl.when((wall == 0) | (wall == 3))
-    def _():
-        f = forward_sweep(l_ref, d_ref, out_ref, s_ref, None)
-        up_ref[...] = f
+    @pl.when(wall == 0)
+    def _():
+        up_ref[...] = forward_chain(l_ref, out_ref, None)
+
+    @pl.when(wall == 3)
+    def _():
+        forward_sweep(l_ref, d_ref, out_ref, s_ref, None)
         down_ref[NV] = backward_sweep(u_ref, s_ref, None, None)[0]
-
-    @pl.when(wall == 3)
-    def _():
         for c in range(NV):
             down_ref[c] = map_ref[c]
 
 
-def middle_kernel(pos_ref, x_ref, r_ref, l_ref, d_ref, u_ref, out_ref, s_ref):
+def middle_kernel(pos_ref, x_ref, r_ref, l_ref, out_ref):
     @pl.when(pos_ref[0] == 1)
     def _():
-        f = x_ref[...]
-        for k in range(K):
-            f = r_ref[:, k] + block_dot(l_ref, k, f)
-        out_ref[...] = f
+        out_ref[...] = forward_chain(l_ref, r_ref, x_ref[...])
 
 
 def below_kernel(pos_ref, x_ref, r_ref, l_ref, d_ref, u_ref, below_ref, s_ref):
@@ -274,43 +285,64 @@
                 below_ref[c] = x
 
 
-def decide_kernel(pos_ref, x_ref, map_ref, r_ref, l_ref, d_ref, u_ref, x3_ref, y2_ref, y1_ref, s_ref):
+def rise_kernel(pos_ref, x_ref, r_ref, l_ref, d_ref, x3_ref, s_ref):
     @pl.when(pos_ref[0] == 2)
     def _():
-        x3 = forward_sweep(l_ref, d_ref, r_ref, s_ref, x_ref[...])
-        x3_ref[...] = x3
-        y2 = map_ref[NV] + map_dot(map_ref, 0, x3)
+        x3_ref[...] = forward_sweep(l_ref, d_ref, r_ref, s_ref, x_ref[...])
+
+
+def decide_kernel(pos_ref, x3_ref, map_ref, s_ref, u_ref, y2_ref, y1_ref):
+    @pl.when(pos_ref[0] == 2)
+    def _():
+        y2 = map_ref[NV] + map_dot(map_ref, 0, x3_ref[...])
         y2_ref[...] = y2
         y1_ref[...] = backward_sweep(u_ref, s_ref, None, y2)[0]
 
 
+def scale_kernel(pos_ref, x1_ref, x3_ref, s2_ref, r_ref, l_ref, d_ref, s_ref, x_ref):
+    wall = pos_ref[0]
+
+    @pl.when(wall == 0)
+    def _():
+        x_ref[...] = jnp.zeros((NV, H, S), F32)
+
+    @pl.when(wall == 1)
+    def _():
+        x_ref[...] = x1_ref[...]
+
+    @pl.when(wall == 3)
+    def _():
+        x_ref[...] = x3_ref[...]
+
+    @pl.when(wall == 2)
+    def _():
+        s_ref[...] = s2_ref[...]
+
+    @pl.when(wall != 2)
+    def _():
+        forward_sweep(l_ref, d_ref, r_ref, s_ref, x_ref[...])
+
+
 def finish_kernel(
-    pos_ref, x1_ref, x2_ref, x3_ref, y2_ref, y1_ref, y10_ref, below_ref, w_ref, pw_ref, r_ref, l_ref, d_ref, u_ref,
-    out_ref, rows_ref, s_ref, x_ref, y_ref, prof_ref,
+    pos_ref, y2_ref, y1_ref, y10_ref, below_ref, w_ref, pw_ref, s_ref, u_ref, out_ref, rows_ref, y_ref, prof_ref
 ):
     wall = pos_ref[0]
 
     @pl.when(wall == 0)
     def _():
-        x_ref[...] = jnp.zeros((NV, H, S), F32)
         y_ref[...] = below_ref[NV] + map_dot(below_ref, 0, y10_ref[...])
 
     @pl.when(wall == 1)
     def _():
-        x_ref[...] = x1_ref[...]
         y_ref[...] = y1_ref[...]
 
     @pl.when(wall == 2)
     def _():
-        x_ref[...] = x2_ref[...]
         y_ref[...] = y2_ref[...]
 
     @pl.when(wall == 3)
     def _():
-        x_ref[...] = x3_ref[...]
         y_ref[...] = jnp.zeros((NV, H, S), F32)
-
-    forward_sweep(l_ref, d_ref, r_ref, s_ref, x_ref[...])
 
     def emit(k, b):
         out_ref[:, k] = b
@@ -389,7 +421,7 @@
         "start", start_kernel, (block, block, block, state, cell, f32(NV, NV, H, S)), 9, smem=(0,),
         far=(2, 3, 4, 5, 6, 7, 8),
         scratch=(
-            state, state, cell, cell, held(2, NV, NV, H, S), pltpu.SemaphoreType.DMA((4,)), pltpu.SemaphoreType.DMA((K, 3)),
+            state, state, cell, cell, held(NV, NV, H, S), held(NV, NV, H, S), pltpu.SemaphoreType.DMA((4,)), pltpu.SemaphoreType.DMA((K, 3)),
         ),
         flops=30_000_000, nbytes=11_000_000,
     )(pos1, wall_weight, adjoint, source, radius, frequency, lower, diag, upper)
@@ -399,7 +431,7 @@
     )(pos, maps, inner, left, right, radius, lower, diag, upper)
     x1 = lax.ppermute(up, "wall", [(0, 1)])
     above = lax.ppermute(down, "wall", [(3, 2)])
-    x2 = call("middle", middle_kernel, vec, 6, smem=(0,), scratch=(levels,))(pos, x1, resid, lower, diag, upper)
+    x2 = call("middle", middle_kernel, vec, 4, smem=(0,))(pos, x1, resid, lower)
     x2, pos2 = tie((x2, pos))
     x2 = lax.ppermute(x2, "wall", [(1, 2)])
     below = call("below", below_kernel, f32(NV + 1, NV, H, S), 6, smem=(0,), scratch=(levels,))(
@@ -411,18 +443,20 @@
     )
 
     x2, placed = tie((x2, placed))
-    x3, y2, y1 = call(
-        "decide", decide_kernel, (vec, vec, vec), 7, smem=(0,), scratch=(levels,)
-    )(pos, x2, above, resid, lower, diag, upper)
+    x3, scaled2 = call("rise", rise_kernel, (vec, levels), 5, smem=(0,))(pos, x2, resid, lower, diag)
     x3, below = tie((x3, below))
     below = lax.ppermute(below, "wall", [(1, 0)])
-    x3 = lax.ppermute(x3, "wall", [(2, 3)])
+    x33 = lax.ppermute(x3, "wall", [(2, 3)])
+    y2, y1 = call("decide", decide_kernel, (vec, vec), 5, smem=(0,))(pos, x3, above, scaled2, upper)
+    y10 = lax.ppermute(y1, "wall", [(2, 0)])
     y11 = lax.ppermute(y1, "wall", [(2, 1)])
-    y10 = lax.ppermute(y1, "wall", [(2, 0)])
+    scaled = call("scale", scale_kernel, levels, 7, smem=(0,), scratch=(held(NV, H, S),))(
+        pos, x1, x33, scaled2, resid, lower, diag
+    )
     adjoint_next, rows = call(
-        "finish", finish_kernel, (f32(NV, K, H, S), away(tiles * ROWS_PER_OWNER, S)), 14, smem=(0,),
-        scratch=(levels, held(NV, H, S), held(NV, H, S), held(NV * H + SLOTS, S)),
-    )(pos, x1, x2, x3, y2, y11, y10, below, weight, placed, resid, lower, diag, upper)
+        "finish", finish_kernel, (f32(NV, K, H, S), away(tiles * ROWS_PER_OWNER, S)), 9, smem=(0,),
+        scratch=(held(NV, H, S), held(NV * H + SLOTS, S)),
+    )(pos, y2, y11, y10, below, weight, placed, scaled, upper)
     got = lax.all_to_all(rows.reshape(tiles, ROWS_PER_OWNER, 1, S), "tile", split_axis=0, concat_axis=0)
     got = got.reshape(tiles * ROWS_PER_OWNER, S)
     part = call("pick", pick_kernel, f32(PATCH_DEV, S), 1)(got)

time: 74.4 us -> 73.2 us (0.984)
  waiting for transfers between devices: 18.9 us -> 15.7 us
  starting transfers between devices: 15.4 us -> 16.7 us
  blocking collectives: 21.7 us -> 22.9 us
    ppermute x1, waiting for transfers between devices: 12.7 us -> 7.15 us  [on_device(): y10 = lax.ppermute(y1, 'wall', [(2, 0)])]
    pallas_call x2 -> x4, Pallas kernels: 1.1 us -> 3.21 us  [the longest x1 1.56 us: on_device(): call('scale', scale_kernel, levels, 7, smem=(0,), scratch=(held(NV, H, S),))]
    ppermute x1, waiting for transfers between devices: 0.01 us -> 1.75 us  [on_device(): below = lax.ppermute(below, 'wall', [(1, 0)])]
    all_to_all x1, blocking collectives: 21.7 us -> 22.9 us  [on_device(): lax.all_to_all(rows.reshape(tiles, ROWS_PER_OWNER, 1, S), 'tile', split_a...]
    ppermute x1, starting transfers between devices: 2.37 us -> 3.29 us  [on_device(): x1 = lax.ppermute(up, 'wall', [(0, 1)])]
    pallas_call x1, Pallas kernels: 2.94 us -> 2.09 us  [on_device(): call('finish', finish_kernel, (f32(NV, K, H, S), away(tiles * ROWS_PER_OW...]
    pallas_call x1, Pallas kernels: 2.03 us -> 1.23 us  [on_device(): call('residual', residual_kernel, (state, vec, f32(NV + 1, NV, H, S)), 9,...]
  transfers between devices with their start and end apart: 12 -> 12, of which waited for: 5 -> 6; matrix products, arithmetic and copies ran while one was open for 0% -> 0% of each run, Pallas kernels for 11% -> 13%
where the time goes in v5:
time: 73.2 us; the launch traced here: 72.8 us
  blocking collectives  22.9 us (31%)
  starting transfers between devices  16.7 us (23%)
  waiting for transfers between devices  15.7 us (21%)
  Pallas kernels  15.3 us (21%)
  between operations  1.5 us (2%)
    all_to_all x1, blocking collectives, on_device(): lax.all_to_all(rows.reshape(tiles, ROWS_PER_OWNER, 1, S), 'tile', split_a...  22.9 us
    ppermute x1, waiting for transfers between devices, on_device(): y10 = lax.ppermute(y1, 'wall', [(2, 0)])  7.15 us
    ppermute x1, starting transfers between devices, on_device(): lax.ppermute(lo, 'tile', [((i + 1) % tiles, i) for i in range(tiles)])  5.64 us
    ppermute x3, waiting for transfers between devices, on_device(): lax.ppermute(part, 'wall', [(w, (w + d) % walls) for w in range(walls)])  5.12 us
    pallas_call x1, Pallas kernels, on_device(): call('start', start_kernel, (block, block, block, state, cell, f32(NV, NV...  5.09 us
    ppermute x1, starting transfers between devices, on_device(): x1 = lax.ppermute(up, 'wall', [(0, 1)])  3.29 us
    ppermute x3, starting transfers between devices, on_device(): lax.ppermute(part, 'wall', [(w, (w + d) % walls) for w in range(walls)])  2.42 us
    pallas_call x1, Pallas kernels, on_device(): call('finish', finish_kernel, (f32(NV, K, H, S), away(tiles * ROWS_PER_OW...  2.09 us
  transfers between devices with their start and end apart: 12, of which 6 were waited for; matrix products, arithmetic and copies ran while one was open for 0% of the time, Pallas kernels for 13%

profile of v5, /device:TPU:6, one launch (start us, length us, event | category | flops | bytes accessed | tf_op | source)
XLA Modules:
  0.0 72.8 jit_solution(12044005225638321406)
XLA Ops:
  0.6 1.0 %pack.1 = (f32[176,128]{1,0:T(8,128)S(1)}, f32[176,128]{1,0:T(8,128)S(1)}) custom-call(f32[10,8,8,128]{3,2,1,0:T(8,128)} %a_in.1, f32[8,8,128]{2,1,0:T(8,128)} %rad_ref.3), custom_call_target="tpu_custom_call" | custom-call | bytes 800000 | tf_op jit(solution)/shard_map/pack/pallas_call | solution.py:415
  1.7 0.1 collective-permute-start
  1.7 5.6 %collective-permute-start.1 = (f32[176,128]{1,0:T(8,128)S(1)}, f32[176,128]{1,0:T(8,128)S(1)}, u32[]{:S(2)}, u32[]{:S(2)}) collective-permute-start(f32[176,128]{1,0:T(8,128)S(1)} %get-tuple-element.26), channel_id=1, source_target_pairs={{1,0},{2,1},{3,2},{4,3},{5,4},{6,5},{7,6},{8,7},{9,8},{10,9},{11,1... | collective-permute-start | bytes 270344 | tf_op jit(solution)/shard_map/ppermute | solution.py:417
  7.4 0.1 pad_add_fusion.pos_ref
  7.5 5.1 %start.1 = (f32[10,10,8,8,128]{4,3,2,1,0:T(8,128)S(1)}, f32[10,10,8,8,128]{4,3,2,1,0:T(8,128)S(1)}, f32[10,10,8,8,128]{4,3,2,1,0:T(8,128)S(1)}, f32[10,8,8,128]{...) custom-call(s32[3]{0:T(128)S(1)} %pad_add_fusion.pos_ref, f32[1,8]{1,0:T(1,128)} %bitcast.15, ...), custom_call_target="tpu_custom_call" | custom-call | flops 30000000 | bytes 11000000 | tf_op jit(solution)/shard_map/start/pallas_call | solution.py:420
  12.6 1.2 %residual.1 = (f32[10,8,8,128]{3,2,1,0:T(8,128)S(1)}, f32[10,8,128]{2,1,0:T(8,128)S(1)}, f32[11,10,8,128]{3,2,1,0:T(8,128)S(1)}) custom-call(s32[3]{0:T(128)S(1)} %pad_add_fusion.pos_ref, f32[10,10,8,128]{3,2,1,0:T(8,128)S(1)} %get-tuple-element.28.map_ref, f32[10,8,8,128]{3,2,1,0:T(8,128)S(1)} %get-tuple-element.29.r_ref, ...), custom_call_target="tpu_custom_call" | custom-call | tf_op jit(solution)/shard_map/residual/pallas_call | solution.py:429
  13.8 0.0 copy-start.2
  13.9 3.3 %collective-permute-start.2 = (f32[10,8,128]{2,1,0:T(8,128)S(1)}, f32[10,8,128]{2,1,0:T(8,128)S(1)}, u32[]{:S(2)}, u32[]{:S(2)}) collective-permute-start(f32[10,8,128]{2,1,0:T(8,128)S(1)} %get-tuple-element.34), channel_id=1, source_target_pairs={{0,64},{1,65},{2,66},{3,67},{4,68},{5,69},{6,70},{7,71},{8,72},{9,... | collective-permute-start | bytes 122888 | tf_op jit(solution)/shard_map/ppermute | solution.py:432
  17.2 1.7 %collective-permute-done.2.x_ref.x1_ref = f32[10,8,128]{2,1,0:T(8,128)S(1)} collective-permute-done((f32[10,8,128]{2,1,0:T(8,128)S(1)}, f32[10,8,128]{2,1,0:T(8,128)S(1)}, u32[]{:S(2)}, u32[]{:S(2)}) %collective-permute-start.2) | collective-permute-done | bytes 40992 | tf_op jit(solution)/shard_map/ppermute | solution.py:432
  18.8 0.5 middle.1
  19.4 0.7 collective-permute-start.3
  20.0 0.7 collective-permute-start.4
  21.4 1.4 %place.1.pw_ref = f32[576,88]{1,0:T(8,128)S(1)} custom-call(s32[1]{0:T(128)S(6)} %copy.15.count_ref, f32[80,256]{1,0:T(8,128)S(1)} %bitcast.11, s32[1,256]{1,0:T(1,128)S(1)} %bitcast.12, s32[1,256]{1,0:T(1,128)S(1)} %bitcast.13), custom_call_target="tpu_custom_call" | custom-call | tf_op jit(solution)/shard_map/place/pallas_call | solution.py:441
  22.8 0.6 below.1
  23.4 0.6 rise.1
  24.0 1.3 %collective-permute-start.7 = (f32[11,10,8,128]{3,2,1,0:T(8,128)S(1)}, f32[11,10,8,128]{3,2,1,0:T(8,128)S(1)}, u32[]{:S(2)}, u32[]{:S(2)}) collective-permute-start(f32[11,10,8,128]{3,2,1,0:T(8,128)S(1)} %below.1), channel_id=1, source_target_pairs={{64,0},{65,1},{66,2},{67,3},{68,4},{69,5},{70,6},{71,7},{72,8},{73... | collective-permute-start | bytes 1351688 | tf_op jit(solution)/shard_map/ppermute | solution.py:448
  25.3 0.7 collective-permute-start.8
  25.9 0.6 decide.1
  26.5 1.3 %collective-permute-start.6 = (f32[10,8,128]{2,1,0:T(8,128)S(1)}, f32[10,8,128]{2,1,0:T(8,128)S(1)}, u32[]{:S(2)}, u32[]{:S(2)}) collective-permute-start(f32[10,8,128]{2,1,0:T(8,128)S(1)} %get-tuple-element.44), channel_id=1, source_target_pairs={{128,0},{129,1},{130,2},{131,3},{132,4},{133,5},{134,6},{135,7},{1... | collective-permute-start | bytes 122888 | tf_op jit(solution)/shard_map/ppermute | solution.py:451
  27.8 0.7 collective-permute-start.5
  28.5 1.6 %scale.1.s_ref = f32[8,10,8,128]{3,2,1,0:T(8,128)S(1)} custom-call(s32[3]{0:T(128)S(1)} %pad_add_fusion.pos_ref, f32[10,8,128]{2,1,0:T(8,128)S(1)} %collective-permute-done.2.x_ref.x1_ref, f32[10,8,128]{2,1,0:T(8,128)S(1)} %collective-permute-done.8.x3_ref, f32[8,10,8,128]{3,2,1,0:T(8,128)S(1)} %get-tuple-element.42.s_ref.s2_ref, ...), custom_call_target="tpu_custom_call" | custom-call | tf_op jit(solution)/shard_map/scale/pallas_call | solution.py:453
  30.0 7.2 %collective-permute-done.6.y10_ref = f32[10,8,128]{2,1,0:T(8,128)S(1)} collective-permute-done((f32[10,8,128]{2,1,0:T(8,128)S(1)}, f32[10,8,128]{2,1,0:T(8,128)S(1)}, u32[]{:S(2)}, u32[]{:S(2)}) %collective-permute-start.6) | collective-permute-done | bytes 40992 | tf_op jit(solution)/shard_map/ppermute | solution.py:451
  37.2 1.7 %collective-permute-done.7.below_ref = f32[11,10,8,128]{3,2,1,0:T(8,128)S(1)} collective-permute-done((f32[11,10,8,128]{3,2,1,0:T(8,128)S(1)}, f32[11,10,8,128]{3,2,1,0:T(8,128)S(1)}, u32[]{:S(2)}, u32[]{:S(2)}) %collective-permute-start.7) | collective-permute-done | bytes 450592 | tf_op jit(solution)/shard_map/ppermute | solution.py:448
  39.0 2.1 %finish.1 = (f32[10,8,8,128]{3,2,1,0:T(8,128)}, f32[576,128]{1,0:T(8,128)}) custom-call(s32[3]{0:T(128)S(1)} %pad_add_fusion.pos_ref, f32[10,8,128]{2,1,0:T(8,128)S(1)} %get-tuple-element.43.y2_ref, f32[10,8,128]{2,1,0:T(8,128)S(1)} %collective-permute-done.5.y1_ref, f32[10,8,128]{2,1,0:T(8,128)S(1)} %collective-permute-done.6.y10_ref, ...), custom_call_target="tpu_custom_call" | custom-call | tf_op jit(solution)/shard_map/finish/pallas_call | solution.py:456
  41.0 22.9 %all_to_all.5 = f32[64,9,1,128]{3,2,1,0:T(1,128)S(1)} all-to-all(f32[64,9,1,128]{3,2,1,0:T(1,128)} %bitcast.14), channel_id=1, replica_groups=mesh['wall'=4,'tile'=64] {'tile'}, dimensions={0} | all-to-all | bytes 589824 | tf_op jit(solution)/shard_map/all_to_all | solution.py:460
  63.9 0.7 pick.1
  64.6 0.1 collective-permute-start.11
  64.7 2.3 %collective-permute-start.10 = (f32[64,128]{1,0:T(8,128)S(1)}, f32[64,128]{1,0:T(8,128)S(1)}, u32[]{:S(2)}, u32[]{:S(2)}) collective-permute-start(f32[64,128]{1,0:T(8,128)S(1)} %pick.1), channel_id=1, source_target_pairs={{0,128},{64,192},{128,0},{192,64},{1,129},{65,193},{129,1},{193,65... | collective-permute-start | bytes 98312 | tf_op jit(solution)/shard_map/ppermute | solution.py:466
  67.0 1.5 %collective-permute-done.11 = f32[64,128]{1,0:T(8,128)S(1)} collective-permute-done((f32[64,128]{1,0:T(8,128)S(1)}, f32[64,128]{1,0:T(8,128)S(1)}, u32[]{:S(2)}, u32[]{:S(2)}) %collective-permute-start.11) | collective-permute-done | bytes 32800 | tf_op jit(solution)/shard_map/ppermute | solution.py:466
  68.6 1.6 %collective-permute-done.10 = f32[64,128]{1,0:T(8,128)S(1)} collective-permute-done((f32[64,128]{1,0:T(8,128)S(1)}, f32[64,128]{1,0:T(8,128)S(1)}, u32[]{:S(2)}, u32[]{:S(2)}) %collective-permute-start.10) | collective-permute-done | bytes 32800 | tf_op jit(solution)/shard_map/ppermute | solution.py:466
  70.2 2.0 %collective-permute-done.9 = f32[64,128]{1,0:T(8,128)S(1)} collective-permute-done((f32[64,128]{1,0:T(8,128)S(1)}, f32[64,128]{1,0:T(8,128)S(1)}, u32[]{:S(2)}, u32[]{:S(2)}) %collective-permute-start.9) | collective-permute-done | bytes 32800 | tf_op jit(solution)/shard_map/ppermute | solution.py:466
  72.2 0.6 add_add_fusion
  (12 shorter events, 0.0 us)
Async XLA Ops:
  1.7 10.9 %collective-permute-start = (f32[176,128]{1,0:T(8,128)S(1)}, f32[176,128]{1,0:T(8,128)S(1)}, u32[]{:S(2)}, u32[]{:S(2)}) collective-permute-start(f32[176,128]{1,0:T(8,128)S(1)} %get-tuple-element.30), channel_id=1, source_target_pairs={{0,1},{1,2},{2,3},{3,4},{4,5},{5,6},{6,7},{7,8},{8,9},{9,10},{10,1... | collective-permute-start | bytes 270344 | tf_op jit(solution)/shard_map/ppermute | solution.py:416
  1.7 10.8 %collective-permute-start.1 = (f32[176,128]{1,0:T(8,128)S(1)}, f32[176,128]{1,0:T(8,128)S(1)}, u32[]{:S(2)}, u32[]{:S(2)}) collective-permute-start(f32[176,128]{1,0:T(8,128)S(1)} %get-tuple-element.26), channel_id=1, source_target_pairs={{1,0},{2,1},{3,2},{4,3},{5,4},{6,5},{7,6},{8,7},{9,8},{10,9},{11,1... | collective-permute-start | bytes 270344 | tf_op jit(solution)/shard_map/ppermute | solution.py:417
  13.8 7.6 %copy-start = (f32[256,10,8]{0,2,1:T(8,128)S(1)}, f32[256,10,8]{0,2,1:T(8,128)}, u32[]{:S(2)}) copy-start(f32[256,10,8]{0,2,1:T(8,128)} %param.20) | copy-start | bytes 245764
  13.8 7.6 %copy-start.1 = (s32[256,1]{0,1:T(1,128)S(1)}, s32[256,1]{0,1:T(1,128)}, u32[]{:S(2)}) copy-start(s32[256,1]{0,1:T(1,128)} %param.21) | copy-start | bytes 3076
  13.8 7.6 %copy-start.2 = (s32[256]{0:T(256)S(1)}, s32[256]{0:T(256)}, u32[]{:S(2)}) copy-start(s32[256]{0:T(256)} %param.22) | copy-start | bytes 3076
  13.9 5.0 %collective-permute-start.2 = (f32[10,8,128]{2,1,0:T(8,128)S(1)}, f32[10,8,128]{2,1,0:T(8,128)S(1)}, u32[]{:S(2)}, u32[]{:S(2)}) collective-permute-start(f32[10,8,128]{2,1,0:T(8,128)S(1)} %get-tuple-element.34), channel_id=1, source_target_pairs={{0,64},{1,65},{2,66},{3,67},{4,68},{5,69},{6,70},{7,71},{8,72},{9,... | collective-permute-start | bytes 122888 | tf_op jit(solution)/shard_map/ppermute | solution.py:432
  19.4 4.0 %collective-permute-start.3 = (f32[10,8,128]{2,1,0:T(8,128)S(1)}, f32[10,8,128]{2,1,0:T(8,128)S(1)}, u32[]{:S(2)}, u32[]{:S(2)}) collective-permute-start(f32[10,8,128]{2,1,0:T(8,128)S(1)} %middle.1), channel_id=1, source_target_pairs={{64,128},{65,129},{66,130},{67,131},{68,132},{69,133},{70,134},{71... | collective-permute-start | bytes 122888 | tf_op jit(solution)/shard_map/ppermute | solution.py:436
  20.0 5.9 %collective-permute-start.4 = (f32[11,10,8,128]{3,2,1,0:T(8,128)S(1)}, f32[11,10,8,128]{3,2,1,0:T(8,128)S(1)}, u32[]{:S(2)}, u32[]{:S(2)}) collective-permute-start(f32[11,10,8,128]{3,2,1,0:T(8,128)S(1)} %get-tuple-element.41), channel_id=1, source_target_pairs={{192,128},{193,129},{194,130},{195,131},{196,132},{197,133},{198,1... | collective-permute-start | bytes 1351688 | tf_op jit(solution)/shard_map/ppermute | solution.py:433
  24.0 15.0 %collective-permute-start.7 = (f32[11,10,8,128]{3,2,1,0:T(8,128)S(1)}, f32[11,10,8,128]{3,2,1,0:T(8,128)S(1)}, u32[]{:S(2)}, u32[]{:S(2)}) collective-permute-start(f32[11,10,8,128]{3,2,1,0:T(8,128)S(1)} %below.1), channel_id=1, source_target_pairs={{64,0},{65,1},{66,2},{67,3},{68,4},{69,5},{70,6},{71,7},{72,8},{73... | collective-permute-start | bytes 1351688 | tf_op jit(solution)/shard_map/ppermute | solution.py:448
  25.3 3.2 %collective-permute-start.8 = (f32[10,8,128]{2,1,0:T(8,128)S(1)}, f32[10,8,128]{2,1,0:T(8,128)S(1)}, u32[]{:S(2)}, u32[]{:S(2)}) collective-permute-start(f32[10,8,128]{2,1,0:T(8,128)S(1)} %get-tuple-element.40.x3_ref), channel_id=1, source_target_pairs={{128,192},{129,193},{130,194},{131,195},{132,196},{133,197},{134,1... | collective-permute-start | bytes 122888 | tf_op jit(solution)/shard_map/ppermute | solution.py:449
  26.5 10.7 %collective-permute-start.6 = (f32[10,8,128]{2,1,0:T(8,128)S(1)}, f32[10,8,128]{2,1,0:T(8,128)S(1)}, u32[]{:S(2)}, u32[]{:S(2)}) collective-permute-start(f32[10,8,128]{2,1,0:T(8,128)S(1)} %get-tuple-element.44), channel_id=1, source_target_pairs={{128,0},{129,1},{130,2},{131,3},{132,4},{133,5},{134,6},{135,7},{1... | collective-permute-start | bytes 122888 | tf_op jit(solution)/shard_map/ppermute | solution.py:451
  27.8 9.4 %collective-permute-start.5 = (f32[10,8,128]{2,1,0:T(8,128)S(1)}, f32[10,8,128]{2,1,0:T(8,128)S(1)}, u32[]{:S(2)}, u32[]{:S(2)}) collective-permute-start(f32[10,8,128]{2,1,0:T(8,128)S(1)} %get-tuple-element.44), channel_id=1, source_target_pairs={{128,64},{129,65},{130,66},{131,67},{132,68},{133,69},{134,70},{13... | collective-permute-start | bytes 122888 | tf_op jit(solution)/shard_map/ppermute | solution.py:452
  64.6 4.0 %collective-permute-start.11 = (f32[64,128]{1,0:T(8,128)S(1)}, f32[64,128]{1,0:T(8,128)S(1)}, u32[]{:S(2)}, u32[]{:S(2)}) collective-permute-start(f32[64,128]{1,0:T(8,128)S(1)} %pick.1), channel_id=1, source_target_pairs={{0,192},{64,0},{128,64},{192,128},{1,193},{65,1},{129,65},{193,129... | collective-permute-start | bytes 98312 | tf_op jit(solution)/shard_map/ppermute | solution.py:466
  64.7 5.5 %collective-permute-start.10 = (f32[64,128]{1,0:T(8,128)S(1)}, f32[64,128]{1,0:T(8,128)S(1)}, u32[]{:S(2)}, u32[]{:S(2)}) collective-permute-start(f32[64,128]{1,0:T(8,128)S(1)} %pick.1), channel_id=1, source_target_pairs={{0,128},{64,192},{128,0},{192,64},{1,129},{65,193},{129,1},{193,65... | collective-permute-start | bytes 98312 | tf_op jit(solution)/shard_map/ppermute | solution.py:466
  67.0 5.1 %collective-permute-start.9 = (f32[64,128]{1,0:T(8,128)S(1)}, f32[64,128]{1,0:T(8,128)S(1)}, u32[]{:S(2)}, u32[]{:S(2)}) collective-permute-start(f32[64,128]{1,0:T(8,128)S(1)} %pick.1), channel_id=1, source_target_pairs={{0,64},{64,128},{128,192},{192,0},{1,65},{65,129},{129,193},{193,1... | collective-permute-start | bytes 98312 | tf_op jit(solution)/shard_map/ppermute | solution.py:466

commit v6 on v5

--- a/solution.py
+++ b/solution.py
@@ -226,7 +226,7 @@
                 map_ref[c] = out
 
 
-def residual_kernel(pos_ref, map_ref, r_ref, left_ref, right_ref, rad_ref, l_ref, d_ref, u_ref, out_ref, up_ref, down_ref, s_ref):
+def residual_kernel(pos_ref, r_ref, left_ref, right_ref, rad_ref, l_ref, d_ref, u_ref, out_ref, up_ref, down_ref, s_ref):
     wall, tile, last = pos_ref[0], pos_ref[1], pos_ref[2]
     row = lax.broadcasted_iota(jnp.int32, (H, S), 0)
     has_left = tile > 0
@@ -258,9 +258,7 @@
     @pl.when(wall == 3)
     def _():
         forward_sweep(l_ref, d_ref, out_ref, s_ref, None)
-        down_ref[NV] = backward_sweep(u_ref, s_ref, None, None)[0]
-        for c in range(NV):
-            down_ref[c] = map_ref[c]
+        down_ref[...] = backward_sweep(u_ref, s_ref, None, None)[0]
 
 
 def middle_kernel(pos_ref, x_ref, r_ref, l_ref, out_ref):
@@ -269,12 +267,16 @@
         out_ref[...] = forward_chain(l_ref, r_ref, x_ref[...])
 
 
-def below_kernel(pos_ref, x_ref, r_ref, l_ref, d_ref, u_ref, below_ref, s_ref):
+def shift_kernel(pos_ref, x_ref, r_ref, l_ref, d_ref, u_ref, shift_ref, s_ref):
     @pl.when(pos_ref[0] == 1)
     def _():
         forward_sweep(l_ref, d_ref, r_ref, s_ref, x_ref[...])
-        below_ref[NV] = backward_sweep(u_ref, s_ref, None, None)[0]
-
+        shift_ref[...] = backward_sweep(u_ref, s_ref, None, None)[0]
+
+
+def below_kernel(pos_ref, u_ref, below_ref):
+    @pl.when(pos_ref[0] == 1)
+    def _():
         @pl.loop(0, NV // 2)
         def _(pair):
             cols = [2 * pair, 2 * pair + 1]
@@ -291,10 +293,10 @@
         x3_ref[...] = forward_sweep(l_ref, d_ref, r_ref, s_ref, x_ref[...])
 
 
-def decide_kernel(pos_ref, x3_ref, map_ref, s_ref, u_ref, y2_ref, y1_ref):
+def decide_kernel(pos_ref, x3_ref, b_ref, map_ref, s_ref, u_ref, y2_ref, y1_ref):
     @pl.when(pos_ref[0] == 2)
     def _():
-        y2 = map_ref[NV] + map_dot(map_ref, 0, x3_ref[...])
+        y2 = b_ref[...] + map_dot(map_ref, 0, x3_ref[...])
         y2_ref[...] = y2
         y1_ref[...] = backward_sweep(u_ref, s_ref, None, y2)[0]
 
@@ -324,13 +326,13 @@
 
 
 def finish_kernel(
-    pos_ref, y2_ref, y1_ref, y10_ref, below_ref, w_ref, pw_ref, s_ref, u_ref, out_ref, rows_ref, y_ref, prof_ref
+    pos_ref, y2_ref, y1_ref, y10_ref, below_ref, shift_ref, w_ref, pw_ref, s_ref, u_ref, out_ref, rows_ref, y_ref, prof_ref
 ):
     wall = pos_ref[0]
 
     @pl.when(wall == 0)
     def _():
-        y_ref[...] = below_ref[NV] + map_dot(below_ref, 0, y10_ref[...])
+        y_ref[...] = shift_ref[...] + map_dot(below_ref, 0, y10_ref[...])
 
     @pl.when(wall == 1)
     def _():
@@ -426,17 +428,21 @@
         flops=30_000_000, nbytes=11_000_000,
     )(pos1, wall_weight, adjoint, source, radius, frequency, lower, diag, upper)
 
+    maps, left, right = tie((maps, left, right))
+    above = lax.ppermute(maps, "wall", [(3, 2)])
     resid, up, down = call(
-        "residual", residual_kernel, (state, vec, f32(NV + 1, NV, H, S)), 9, smem=(0,), scratch=(levels,)
-    )(pos, maps, inner, left, right, radius, lower, diag, upper)
+        "residual", residual_kernel, (state, vec, vec), 8, smem=(0,), scratch=(levels,)
+    )(pos, inner, left, right, radius, lower, diag, upper)
     x1 = lax.ppermute(up, "wall", [(0, 1)])
-    above = lax.ppermute(down, "wall", [(3, 2)])
+    b3 = lax.ppermute(down, "wall", [(3, 2)])
+    up, pos1 = tie((up, pos))
+    below = call("below", below_kernel, f32(NV, NV, H, S), 2, smem=(0,))(pos1, upper)
+    x1, below = tie((x1, below))
+    below = lax.ppermute(below, "wall", [(1, 0)])
     x2 = call("middle", middle_kernel, vec, 4, smem=(0,))(pos, x1, resid, lower)
     x2, pos2 = tie((x2, pos))
     x2 = lax.ppermute(x2, "wall", [(1, 2)])
-    below = call("below", below_kernel, f32(NV + 1, NV, H, S), 6, smem=(0,), scratch=(levels,))(
-        pos2, x1, resid, lower, diag, upper
-    )
+    shift = call("shift", shift_kernel, vec, 6, smem=(0,), scratch=(levels,))(pos2, x1, resid, lower, diag, upper)
     swt = surface_weight.transpose(1, 2, 0).reshape(NV * H, -1)
     placed = call("place", place_kernel, held(tiles * ROWS_PER_OWNER, NV * H + SLOTS), 4, smem=(0,))(
         surface_count, swt, patch_owner.reshape(1, -1), patch_row.reshape(1, -1)
@@ -444,19 +450,19 @@
 
     x2, placed = tie((x2, placed))
     x3, scaled2 = call("rise", rise_kernel, (vec, levels), 5, smem=(0,))(pos, x2, resid, lower, diag)
-    x3, below = tie((x3, below))
-    below = lax.ppermute(below, "wall", [(1, 0)])
     x33 = lax.ppermute(x3, "wall", [(2, 3)])
-    y2, y1 = call("decide", decide_kernel, (vec, vec), 5, smem=(0,))(pos, x3, above, scaled2, upper)
+    y2, y1 = call("decide", decide_kernel, (vec, vec), 6, smem=(0,))(pos, x3, b3, above, scaled2, upper)
+    y1, shift = tie((y1, shift))
     y10 = lax.ppermute(y1, "wall", [(2, 0)])
     y11 = lax.ppermute(y1, "wall", [(2, 1)])
+    shift = lax.ppermute(shift, "wall", [(1, 0)])
     scaled = call("scale", scale_kernel, levels, 7, smem=(0,), scratch=(held(NV, H, S),))(
         pos, x1, x33, scaled2, resid, lower, diag
     )
     adjoint_next, rows = call(
-        "finish", finish_kernel, (f32(NV, K, H, S), away(tiles * ROWS_PER_OWNER, S)), 9, smem=(0,),
+        "finish", finish_kernel, (f32(NV, K, H, S), away(tiles * ROWS_PER_OWNER, S)), 10, smem=(0,),
         scratch=(held(NV, H, S), held(NV * H + SLOTS, S)),
-    )(pos, y2, y11, y10, below, weight, placed, scaled, upper)
+    )(pos, y2, y11, y10, below, shift, weight, placed, scaled, upper)
     got = lax.all_to_all(rows.reshape(tiles, ROWS_PER_OWNER, 1, S), "tile", split_axis=0, concat_axis=0)
     got = got.reshape(tiles * ROWS_PER_OWNER, S)
     part = call("pick", pick_kernel, f32(PATCH_DEV, S), 1)(got)

time: 73.2 us -> 70.8 us (0.967)
  waiting for transfers between devices: 15.7 us -> 12.3 us
  starting transfers between devices: 16.7 us -> 19.4 us
  blocking collectives: 22.9 us -> 20.3 us
    all_to_all x1, blocking collectives: 22.9 us -> 20.3 us  [on_device(): lax.all_to_all(rows.reshape(tiles, ROWS_PER_OWNER, 1, S), 'tile', split_a...]
    ppermute x3, waiting for transfers between devices: 5.12 us -> 3.09 us  [on_device(): lax.ppermute(part, 'wall', [(w, (w + d) % walls) for w in range(walls)])]
    ppermute x1 -> x3, starting transfers between devices: 0.69 us -> 2.63 us  [the longest x1 1.29 us: on_device(): shift = lax.ppermute(shift, 'wall', [(1, 0)])]
    ppermute x1, waiting for transfers between devices: 1.75 us -> 0.01 us  [on_device(): below = lax.ppermute(below, 'wall', [(1, 0)])]
    ppermute x1, waiting for transfers between devices: 0.01 us -> 0.88 us  [on_device(): lax.ppermute(hi, 'tile', [(i, (i + 1) % tiles) for i in range(tiles)])]
    ppermute x3, starting transfers between devices: 2.42 us -> 3.29 us  [on_device(): lax.ppermute(part, 'wall', [(w, (w + d) % walls) for w in range(walls)])]
    pallas_call x3 -> x4, Pallas kernels: 2.34 us -> 2.89 us  [the longest x1 1.23 us: on_device(): call('residual', residual_kernel, (state, vec, vec), 8, smem=(0,), scratc...]
  transfers between devices with their start and end apart: 12 -> 14, of which waited for: 6 -> 6; matrix products, arithmetic and copies ran while one was open for 0% -> 0% of each run, Pallas kernels for 13% -> 17%
where the time goes in v6:
time: 70.8 us; the launch traced here: 70.1 us
  blocking collectives  20.3 us (29%)
  starting transfers between devices  19.4 us (27%)
  Pallas kernels  15.9 us (22%)
  waiting for transfers between devices  12.3 us (17%)
  between operations  1.53 us (2%)
    all_to_all x1, blocking collectives, on_device(): lax.all_to_all(rows.reshape(tiles, ROWS_PER_OWNER, 1, S), 'tile', split_a...  20.3 us
    ppermute x1, waiting for transfers between devices, on_device(): y10 = lax.ppermute(y1, 'wall', [(2, 0)])  7.2 us
    ppermute x1, starting transfers between devices, on_device(): lax.ppermute(lo, 'tile', [((i + 1) % tiles, i) for i in range(tiles)])  5.64 us
    pallas_call x1, Pallas kernels, on_device(): call('start', start_kernel, (block, block, block, state, cell, f32(NV, NV...  5.09 us
    ppermute x3, starting transfers between devices, on_device(): lax.ppermute(part, 'wall', [(w, (w + d) % walls) for w in range(walls)])  3.29 us
    ppermute x1, starting transfers between devices, on_device(): x1 = lax.ppermute(up, 'wall', [(0, 1)])  3.29 us
    ppermute x3, waiting for transfers between devices, on_device(): lax.ppermute(part, 'wall', [(w, (w + d) % walls) for w in range(walls)])  3.09 us
    pallas_call x1, Pallas kernels, on_device(): call('finish', finish_kernel, (f32(NV, K, H, S), away(tiles * ROWS_PER_OW...  2.11 us
  transfers between devices with their start and end apart: 14, of which 6 were waited for; matrix products, arithmetic and copies ran while one was open for 0% of the time, Pallas kernels for 17%

profile of v6, /device:TPU:6, one launch (start us, length us, event | category | flops | bytes accessed | tf_op | source)
XLA Modules:
  0.0 70.1 jit_solution(94408513663940851)
XLA Ops:
  0.6 1.0 %pack.1 = (f32[176,128]{1,0:T(8,128)S(1)}, f32[176,128]{1,0:T(8,128)S(1)}) custom-call(f32[10,8,8,128]{3,2,1,0:T(8,128)} %a_in.1, f32[8,8,128]{2,1,0:T(8,128)} %rad_ref.3), custom_call_target="tpu_custom_call" | custom-call | bytes 800000 | tf_op jit(solution)/shard_map/pack/pallas_call | solution.py:417
  1.7 5.6 %collective-permute-start.1 = (f32[176,128]{1,0:T(8,128)S(1)}, f32[176,128]{1,0:T(8,128)S(1)}, u32[]{:S(2)}, u32[]{:S(2)}) collective-permute-start(f32[176,128]{1,0:T(8,128)S(1)} %get-tuple-element.32), channel_id=1, source_target_pairs={{1,0},{2,1},{3,2},{4,3},{5,4},{6,5},{7,6},{8,7},{9,8},{10,9},{11,1... | collective-permute-start | bytes 270344 | tf_op jit(solution)/shard_map/ppermute | solution.py:419
  7.4 5.1 %start.1 = (f32[10,10,8,8,128]{4,3,2,1,0:T(8,128)S(1)}, f32[10,10,8,8,128]{4,3,2,1,0:T(8,128)S(1)}, f32[10,10,8,8,128]{4,3,2,1,0:T(8,128)S(1)}, f32[10,8,8,128]{...) custom-call(s32[3]{0:T(128)S(1)} %pad_add_fusion.pos_ref, f32[1,8]{1,0:T(1,128)} %bitcast.15, ...), custom_call_target="tpu_custom_call" | custom-call | flops 30000000 | bytes 11000000 | tf_op jit(solution)/shard_map/start/pallas_call | solution.py:422
  12.5 0.9 %collective-permute-done.left_ref = f32[176,128]{1,0:T(8,128)S(1)} collective-permute-done((f32[176,128]{1,0:T(8,128)S(1)}, f32[176,128]{1,0:T(8,128)S(1)}, u32[]{:S(2)}, u32[]{:S(2)}) %collective-permute-start) | collective-permute-done | bytes 90144 | tf_op jit(solution)/shard_map/ppermute | solution.py:418
  13.4 0.7 collective-permute-start.5
  14.0 1.2 %residual.1 = (f32[10,8,8,128]{3,2,1,0:T(8,128)S(1)}, f32[10,8,128]{2,1,0:T(8,128)S(1)}, f32[10,8,128]{2,1,0:T(8,128)S(1)}) custom-call(s32[3]{0:T(128)S(1)} %pad_add_fusion.pos_ref, f32[10,8,8,128]{3,2,1,0:T(8,128)S(1)} %get-tuple-element.34.r_ref, f32[176,128]{1,0:T(8,128)S(1)} %collective-permute-done.left_ref, ...), custom_call_target="tpu_custom_call" | custom-call | tf_op jit(solution)/shard_map/residual/pallas_call | solution.py:433
  15.3 3.3 %collective-permute-start.2 = (f32[10,8,128]{2,1,0:T(8,128)S(1)}, f32[10,8,128]{2,1,0:T(8,128)S(1)}, u32[]{:S(2)}, u32[]{:S(2)}) collective-permute-start(f32[10,8,128]{2,1,0:T(8,128)S(1)} %get-tuple-element.42), channel_id=1, source_target_pairs={{0,64},{1,65},{2,66},{3,67},{4,68},{5,69},{6,70},{7,71},{8,72},{9,... | collective-permute-start | bytes 122888 | tf_op jit(solution)/shard_map/ppermute | solution.py:436
  18.6 0.6 below.1
  19.2 1.1 %collective-permute-done.2.x_ref.x1_ref = f32[10,8,128]{2,1,0:T(8,128)S(1)} collective-permute-done((f32[10,8,128]{2,1,0:T(8,128)S(1)}, f32[10,8,128]{2,1,0:T(8,128)S(1)}, u32[]{:S(2)}, u32[]{:S(2)}) %collective-permute-start.2) | collective-permute-done | bytes 40992 | tf_op jit(solution)/shard_map/ppermute | solution.py:436
  20.3 1.3 %collective-permute-start.8 = (f32[10,10,8,128]{3,2,1,0:T(8,128)S(1)}, f32[10,10,8,128]{3,2,1,0:T(8,128)S(1)}, u32[]{:S(2)}, u32[]{:S(2)}) collective-permute-start(f32[10,10,8,128]{3,2,1,0:T(8,128)S(1)} %below.1), channel_id=1, source_target_pairs={{64,0},{65,1},{66,2},{67,3},{68,4},{69,5},{70,6},{71,7},{72,8},{73... | collective-permute-start | bytes 1228808 | tf_op jit(solution)/shard_map/ppermute | solution.py:441
  21.6 0.6 middle.1
  22.1 0.7 collective-permute-start.3
  22.8 0.7 collective-permute-start.4
  24.1 1.4 %place.1.pw_ref = f32[576,88]{1,0:T(8,128)S(1)} custom-call(s32[1]{0:T(128)S(6)} %copy.15.count_ref, f32[80,256]{1,0:T(8,128)S(1)} %bitcast.11, s32[1,256]{1,0:T(1,128)S(1)} %bitcast.12, s32[1,256]{1,0:T(1,128)S(1)} %bitcast.13), custom_call_target="tpu_custom_call" | custom-call | tf_op jit(solution)/shard_map/place/pallas_call | solution.py:447
  25.6 0.6 shift.1
  26.1 0.6 rise.1
  26.7 0.7 collective-permute-start.10
  27.4 0.6 decide.1
  27.9 0.7 collective-permute-start.6
  28.6 1.3 %collective-permute-start.7 = (f32[10,8,128]{2,1,0:T(8,128)S(1)}, f32[10,8,128]{2,1,0:T(8,128)S(1)}, u32[]{:S(2)}, u32[]{:S(2)}) collective-permute-start(f32[10,8,128]{2,1,0:T(8,128)S(1)} %get-tuple-element.55), channel_id=1, source_target_pairs={{128,0},{129,1},{130,2},{131,3},{132,4},{133,5},{134,6},{135,7},{1... | collective-permute-start | bytes 122888 | tf_op jit(solution)/shard_map/ppermute | solution.py:456
  29.9 1.3 %collective-permute-start.9 = (f32[10,8,128]{2,1,0:T(8,128)S(1)}, f32[10,8,128]{2,1,0:T(8,128)S(1)}, u32[]{:S(2)}, u32[]{:S(2)}) collective-permute-start(f32[10,8,128]{2,1,0:T(8,128)S(1)} %shift.1), channel_id=1, source_target_pairs={{64,0},{65,1},{66,2},{67,3},{68,4},{69,5},{70,6},{71,7},{72,8},{73... | collective-permute-start | bytes 122888 | tf_op jit(solution)/shard_map/ppermute | solution.py:458
  31.2 1.6 %scale.1.s_ref = f32[8,10,8,128]{3,2,1,0:T(8,128)S(1)} custom-call(s32[3]{0:T(128)S(1)} %pad_add_fusion.pos_ref, f32[10,8,128]{2,1,0:T(8,128)S(1)} %collective-permute-done.2.x_ref.x1_ref, f32[10,8,128]{2,1,0:T(8,128)S(1)} %collective-permute-done.10.x3_ref, f32[8,10,8,128]{3,2,1,0:T(8,128)S(1)} %get-tuple-element.51.s_ref.s2_ref, ...), custom_call_target="tpu_custom_call" | custom-call | tf_op jit(solution)/shard_map/scale/pallas_call | solution.py:459
  32.8 7.2 %collective-permute-done.7.y10_ref = f32[10,8,128]{2,1,0:T(8,128)S(1)} collective-permute-done((f32[10,8,128]{2,1,0:T(8,128)S(1)}, f32[10,8,128]{2,1,0:T(8,128)S(1)}, u32[]{:S(2)}, u32[]{:S(2)}) %collective-permute-start.7) | collective-permute-done | bytes 40992 | tf_op jit(solution)/shard_map/ppermute | solution.py:456
  40.0 2.1 %finish.1 = (f32[10,8,8,128]{3,2,1,0:T(8,128)}, f32[576,128]{1,0:T(8,128)}) custom-call(s32[3]{0:T(128)S(1)} %pad_add_fusion.pos_ref, f32[10,8,128]{2,1,0:T(8,128)S(1)} %get-tuple-element.52.y2_ref, f32[10,8,128]{2,1,0:T(8,128)S(1)} %collective-permute-done.6.y1_ref, f32[10,8,128]{2,1,0:T(8,128)S(1)} %collective-permute-done.7.y10_ref, ...), custom_call_target="tpu_custom_call" | custom-call | tf_op jit(solution)/shard_map/finish/pallas_call | solution.py:462
  42.1 20.3 %all_to_all.5 = f32[64,9,1,128]{3,2,1,0:T(1,128)S(1)} all-to-all(f32[64,9,1,128]{3,2,1,0:T(1,128)} %bitcast.14), channel_id=1, replica_groups=mesh['wall'=4,'tile'=64] {'tile'}, dimensions={0} | all-to-all | bytes 589824 | tf_op jit(solution)/shard_map/all_to_all | solution.py:466
  62.4 0.7 pick.1
  63.2 0.1 collective-permute-start.12
  63.3 3.1 %collective-permute-start.13 = (f32[64,128]{1,0:T(8,128)S(1)}, f32[64,128]{1,0:T(8,128)S(1)}, u32[]{:S(2)}, u32[]{:S(2)}) collective-permute-start(f32[64,128]{1,0:T(8,128)S(1)} %pick.1), channel_id=1, source_target_pairs={{0,192},{64,0},{128,64},{192,128},{1,193},{65,1},{129,65},{193,129... | collective-permute-start | bytes 98312 | tf_op jit(solution)/shard_map/ppermute | solution.py:472
  66.4 1.9 %collective-permute-done.11 = f32[64,128]{1,0:T(8,128)S(1)} collective-permute-done((f32[64,128]{1,0:T(8,128)S(1)}, f32[64,128]{1,0:T(8,128)S(1)}, u32[]{:S(2)}, u32[]{:S(2)}) %collective-permute-start.11) | collective-permute-done | bytes 32800 | tf_op jit(solution)/shard_map/ppermute | solution.py:472
  68.3 0.4 collective-permute-done.12
  68.7 0.8 %collective-permute-done.13 = f32[64,128]{1,0:T(8,128)S(1)} collective-permute-done((f32[64,128]{1,0:T(8,128)S(1)}, f32[64,128]{1,0:T(8,128)S(1)}, u32[]{:S(2)}, u32[]{:S(2)}) %collective-permute-start.13) | collective-permute-done | bytes 32800 | tf_op jit(solution)/shard_map/ppermute | solution.py:472
  69.5 0.6 add_add_fusion
  (17 shorter events, 0.2 us)
Async XLA Ops:
  1.7 10.8 %collective-permute-start.1 = (f32[176,128]{1,0:T(8,128)S(1)}, f32[176,128]{1,0:T(8,128)S(1)}, u32[]{:S(2)}, u32[]{:S(2)}) collective-permute-start(f32[176,128]{1,0:T(8,128)S(1)} %get-tuple-element.32), channel_id=1, source_target_pairs={{1,0},{2,1},{3,2},{4,3},{5,4},{6,5},{7,6},{8,7},{9,8},{10,9},{11,1... | collective-permute-start | bytes 270344 | tf_op jit(solution)/shard_map/ppermute | solution.py:419
  7.3 6.1 %collective-permute-start = (f32[176,128]{1,0:T(8,128)S(1)}, f32[176,128]{1,0:T(8,128)S(1)}, u32[]{:S(2)}, u32[]{:S(2)}) collective-permute-start(f32[176,128]{1,0:T(8,128)S(1)} %get-tuple-element.36), channel_id=1, source_target_pairs={{0,1},{1,2},{2,3},{3,4},{4,5},{5,6},{6,7},{7,8},{8,9},{9,10},{10,1... | collective-permute-start | bytes 270344 | tf_op jit(solution)/shard_map/ppermute | solution.py:418
  13.4 14.0 %collective-permute-start.5 = (f32[10,10,8,128]{3,2,1,0:T(8,128)S(1)}, f32[10,10,8,128]{3,2,1,0:T(8,128)S(1)}, u32[]{:S(2)}, u32[]{:S(2)}) collective-permute-start(f32[10,10,8,128]{3,2,1,0:T(8,128)S(1)} %get-tuple-element.50), channel_id=1, source_target_pairs={{192,128},{193,129},{194,130},{195,131},{196,132},{197,133},{198,1... | collective-permute-start | bytes 1228808 | tf_op jit(solution)/shard_map/ppermute | solution.py:432
  15.3 8.8 %copy-start = (f32[256,10,8]{0,2,1:T(8,128)S(1)}, f32[256,10,8]{0,2,1:T(8,128)}, u32[]{:S(2)}) copy-start(f32[256,10,8]{0,2,1:T(8,128)} %param.20) | copy-start | bytes 245764
  15.3 8.8 %copy-start.1 = (s32[256,1]{0,1:T(1,128)S(1)}, s32[256,1]{0,1:T(1,128)}, u32[]{:S(2)}) copy-start(s32[256,1]{0,1:T(1,128)} %param.21) | copy-start | bytes 3076
  15.3 8.8 %copy-start.2 = (s32[256]{0:T(256)S(1)}, s32[256]{0:T(256)}, u32[]{:S(2)}) copy-start(s32[256]{0:T(256)} %param.22) | copy-start | bytes 3076
  15.3 5.0 %collective-permute-start.2 = (f32[10,8,128]{2,1,0:T(8,128)S(1)}, f32[10,8,128]{2,1,0:T(8,128)S(1)}, u32[]{:S(2)}, u32[]{:S(2)}) collective-permute-start(f32[10,8,128]{2,1,0:T(8,128)S(1)} %get-tuple-element.42), channel_id=1, source_target_pairs={{0,64},{1,65},{2,66},{3,67},{4,68},{5,69},{6,70},{7,71},{8,72},{9,... | collective-permute-start | bytes 122888 | tf_op jit(solution)/shard_map/ppermute | solution.py:436
  20.3 19.7 %collective-permute-start.8 = (f32[10,10,8,128]{3,2,1,0:T(8,128)S(1)}, f32[10,10,8,128]{3,2,1,0:T(8,128)S(1)}, u32[]{:S(2)}, u32[]{:S(2)}) collective-permute-start(f32[10,10,8,128]{3,2,1,0:T(8,128)S(1)} %below.1), channel_id=1, source_target_pairs={{64,0},{65,1},{66,2},{67,3},{68,4},{69,5},{70,6},{71,7},{72,8},{73... | collective-permute-start | bytes 1228808 | tf_op jit(solution)/shard_map/ppermute | solution.py:441
  22.1 4.0 %collective-permute-start.3 = (f32[10,8,128]{2,1,0:T(8,128)S(1)}, f32[10,8,128]{2,1,0:T(8,128)S(1)}, u32[]{:S(2)}, u32[]{:S(2)}) collective-permute-start(f32[10,8,128]{2,1,0:T(8,128)S(1)} %middle.1), channel_id=1, source_target_pairs={{64,128},{65,129},{66,130},{67,131},{68,132},{69,133},{70,134},{71... | collective-permute-start | bytes 122888 | tf_op jit(solution)/shard_map/ppermute | solution.py:444
  22.8 4.6 %collective-permute-start.4 = (f32[10,8,128]{2,1,0:T(8,128)S(1)}, f32[10,8,128]{2,1,0:T(8,128)S(1)}, u32[]{:S(2)}, u32[]{:S(2)}) collective-permute-start(f32[10,8,128]{2,1,0:T(8,128)S(1)} %get-tuple-element.49), channel_id=1, source_target_pairs={{192,128},{193,129},{194,130},{195,131},{196,132},{197,133},{198,1... | collective-permute-start | bytes 122888 | tf_op jit(solution)/shard_map/ppermute | solution.py:437
  26.7 4.5 %collective-permute-start.10 = (f32[10,8,128]{2,1,0:T(8,128)S(1)}, f32[10,8,128]{2,1,0:T(8,128)S(1)}, u32[]{:S(2)}, u32[]{:S(2)}) collective-permute-start(f32[10,8,128]{2,1,0:T(8,128)S(1)} %get-tuple-element.48.x3_ref), channel_id=1, source_target_pairs={{128,192},{129,193},{130,194},{131,195},{132,196},{133,197},{134,1... | collective-permute-start | bytes 122888 | tf_op jit(solution)/shard_map/ppermute | solution.py:453
  27.9 4.9 %collective-permute-start.6 = (f32[10,8,128]{2,1,0:T(8,128)S(1)}, f32[10,8,128]{2,1,0:T(8,128)S(1)}, u32[]{:S(2)}, u32[]{:S(2)}) collective-permute-start(f32[10,8,128]{2,1,0:T(8,128)S(1)} %get-tuple-element.55), channel_id=1, source_target_pairs={{128,64},{129,65},{130,66},{131,67},{132,68},{133,69},{134,70},{13... | collective-permute-start | bytes 122888 | tf_op jit(solution)/shard_map/ppermute | solution.py:457
  28.6 11.4 %collective-permute-start.7 = (f32[10,8,128]{2,1,0:T(8,128)S(1)}, f32[10,8,128]{2,1,0:T(8,128)S(1)}, u32[]{:S(2)}, u32[]{:S(2)}) collective-permute-start(f32[10,8,128]{2,1,0:T(8,128)S(1)} %get-tuple-element.55), channel_id=1, source_target_pairs={{128,0},{129,1},{130,2},{131,3},{132,4},{133,5},{134,6},{135,7},{1... | collective-permute-start | bytes 122888 | tf_op jit(solution)/shard_map/ppermute | solution.py:456
  29.9 10.1 %collective-permute-start.9 = (f32[10,8,128]{2,1,0:T(8,128)S(1)}, f32[10,8,128]{2,1,0:T(8,128)S(1)}, u32[]{:S(2)}, u32[]{:S(2)}) collective-permute-start(f32[10,8,128]{2,1,0:T(8,128)S(1)} %shift.1), channel_id=1, source_target_pairs={{64,0},{65,1},{66,2},{67,3},{68,4},{69,5},{70,6},{71,7},{72,8},{73... | collective-permute-start | bytes 122888 | tf_op jit(solution)/shard_map/ppermute | solution.py:458
  63.1 5.2 %collective-permute-start.11 = (f32[64,128]{1,0:T(8,128)S(1)}, f32[64,128]{1,0:T(8,128)S(1)}, u32[]{:S(2)}, u32[]{:S(2)}) collective-permute-start(f32[64,128]{1,0:T(8,128)S(1)} %pick.1), channel_id=1, source_target_pairs={{0,64},{64,128},{128,192},{192,0},{1,65},{65,129},{129,193},{193,1... | collective-permute-start | bytes 98312 | tf_op jit(solution)/shard_map/ppermute | solution.py:472
  63.2 5.5 %collective-permute-start.12 = (f32[64,128]{1,0:T(8,128)S(1)}, f32[64,128]{1,0:T(8,128)S(1)}, u32[]{:S(2)}, u32[]{:S(2)}) collective-permute-start(f32[64,128]{1,0:T(8,128)S(1)} %pick.1), channel_id=1, source_target_pairs={{0,128},{64,192},{128,0},{192,64},{1,129},{65,193},{129,1},{193,65... | collective-permute-start | bytes 98312 | tf_op jit(solution)/shard_map/ppermute | solution.py:472
  63.3 6.2 %collective-permute-start.13 = (f32[64,128]{1,0:T(8,128)S(1)}, f32[64,128]{1,0:T(8,128)S(1)}, u32[]{:S(2)}, u32[]{:S(2)}) collective-permute-start(f32[64,128]{1,0:T(8,128)S(1)} %pick.1), channel_id=1, source_target_pairs={{0,192},{64,0},{128,64},{192,128},{1,193},{65,1},{129,65},{193,129... | collective-permute-start | bytes 98312 | tf_op jit(solution)/shard_map/ppermute | solution.py:472

commit v7 on v6

--- a/solution.py
+++ b/solution.py
@@ -287,16 +287,12 @@
                 below_ref[c] = x
 
 
-def rise_kernel(pos_ref, x_ref, r_ref, l_ref, d_ref, x3_ref, s_ref):
+def decide_kernel(pos_ref, x_ref, b_ref, map_ref, r_ref, l_ref, d_ref, u_ref, x3_ref, y2_ref, y1_ref, s_ref):
     @pl.when(pos_ref[0] == 2)
     def _():
-        x3_ref[...] = forward_sweep(l_ref, d_ref, r_ref, s_ref, x_ref[...])
-
-
-def decide_kernel(pos_ref, x3_ref, b_ref, map_ref, s_ref, u_ref, y2_ref, y1_ref):
-    @pl.when(pos_ref[0] == 2)
-    def _():
-        y2 = b_ref[...] + map_dot(map_ref, 0, x3_ref[...])
+        x3 = forward_sweep(l_ref, d_ref, r_ref, s_ref, x_ref[...])
+        x3_ref[...] = x3
+        y2 = b_ref[...] + map_dot(map_ref, 0, x3)
         y2_ref[...] = y2
         y1_ref[...] = backward_sweep(u_ref, s_ref, None, y2)[0]
 
@@ -326,7 +322,7 @@
 
 
 def finish_kernel(
-    pos_ref, y2_ref, y1_ref, y10_ref, below_ref, shift_ref, w_ref, pw_ref, s_ref, u_ref, out_ref, rows_ref, y_ref, prof_ref
+    pos_ref, y2_ref, y10_ref, y1_ref, below_ref, shift_ref, w_ref, pw_ref, s_ref, u_ref, out_ref, rows_ref, y_ref, prof_ref
 ):
     wall = pos_ref[0]
 
@@ -449,10 +445,11 @@
     )
 
     x2, placed = tie((x2, placed))
-    x3, scaled2 = call("rise", rise_kernel, (vec, levels), 5, smem=(0,))(pos, x2, resid, lower, diag)
+    x3, y2, y1, scaled2 = call("decide", decide_kernel, (vec, vec, vec, levels), 8, smem=(0,))(
+        pos, x2, b3, above, resid, lower, diag, upper
+    )
+    y1, shift = tie((y1, shift))
     x33 = lax.ppermute(x3, "wall", [(2, 3)])
-    y2, y1 = call("decide", decide_kernel, (vec, vec), 6, smem=(0,))(pos, x3, b3, above, scaled2, upper)
-    y1, shift = tie((y1, shift))
     y10 = lax.ppermute(y1, "wall", [(2, 0)])
     y11 = lax.ppermute(y1, "wall", [(2, 1)])
     shift = lax.ppermute(shift, "wall", [(1, 0)])
@@ -462,7 +459,7 @@
     adjoint_next, rows = call(
         "finish", finish_kernel, (f32(NV, K, H, S), away(tiles * ROWS_PER_OWNER, S)), 10, smem=(0,),
         scratch=(held(NV, H, S), held(NV * H + SLOTS, S)),
-    )(pos, y2, y11, y10, below, shift, weight, placed, scaled, upper)
+    )(pos, y2, y10, y11, below, shift, weight, placed, scaled, upper)
     got = lax.all_to_all(rows.reshape(tiles, ROWS_PER_OWNER, 1, S), "tile", split_axis=0, concat_axis=0)
     got = got.reshape(tiles * ROWS_PER_OWNER, S)
     part = call("pick", pick_kernel, f32(PATCH_DEV, S), 1)(got)

time: 70.8 us -> 68.9 us (0.973)
  waiting for transfers between devices: 12.3 us -> 9.84 us
  starting transfers between devices: 19.4 us -> 20.2 us
    ppermute x1, waiting for transfers between devices: 7.2 us -> 4.75 us  [on_device(): y10 = lax.ppermute(y1, 'wall', [(2, 0)])]
    ppermute x3, starting transfers between devices: 3.29 us -> 4.06 us  [on_device(): lax.ppermute(part, 'wall', [(w, (w + d) % walls) for w in range(walls)])]
where the time goes in v7:
time: 68.9 us; the launch traced here: 68.5 us
  blocking collectives  21 us (30%)
  starting transfers between devices  20.2 us (29%)
  Pallas kernels  15.3 us (22%)
  waiting for transfers between devices  9.84 us (14%)
  between operations  1.5 us (2%)
  other arithmetic  0.7 us (1%)
    all_to_all x1, blocking collectives, on_device(): lax.all_to_all(rows.reshape(tiles, ROWS_PER_OWNER, 1, S), 'tile', split_a...  21 us
    ppermute x1, starting transfers between devices, on_device(): lax.ppermute(lo, 'tile', [((i + 1) % tiles, i) for i in range(tiles)])  5.64 us
    pallas_call x1, Pallas kernels, on_device(): call('start', start_kernel, (block, block, block, state, cell, f32(NV, NV...  5.09 us
    ppermute x1, waiting for transfers between devices, on_device(): y10 = lax.ppermute(y1, 'wall', [(2, 0)])  4.75 us
    ppermute x3, starting transfers between devices, on_device(): lax.ppermute(part, 'wall', [(w, (w + d) % walls) for w in range(walls)])  4.06 us
    ppermute x1, starting transfers between devices, on_device(): x1 = lax.ppermute(up, 'wall', [(0, 1)])  3.29 us
    ppermute x3, waiting for transfers between devices, on_device(): lax.ppermute(part, 'wall', [(w, (w + d) % walls) for w in range(walls)])  2.65 us
    pallas_call x1, Pallas kernels, on_device(): call('finish', finish_kernel, (f32(NV, K, H, S), away(tiles * ROWS_PER_OW...  2.09 us
  transfers between devices with their start and end apart: 14, of which 6 were waited for; matrix products, arithmetic and copies ran while one was open for 0% of the time, Pallas kernels for 17%

profile of v7, /device:TPU:6, one launch (start us, length us, event | category | flops | bytes accessed | tf_op | source)
XLA Modules:
  0.0 68.5 jit_solution(4877603224570694160)
XLA Ops:
  0.6 1.0 %pack.1 = (f32[176,128]{1,0:T(8,128)S(1)}, f32[176,128]{1,0:T(8,128)S(1)}) custom-call(f32[10,8,8,128]{3,2,1,0:T(8,128)} %a_in.1, f32[8,8,128]{2,1,0:T(8,128)} %rad_ref.3), custom_call_target="tpu_custom_call" | custom-call | bytes 800000 | tf_op jit(solution)/shard_map/pack/pallas_call | solution.py:413
  1.7 5.6 %collective-permute-start.1 = (f32[176,128]{1,0:T(8,128)S(1)}, f32[176,128]{1,0:T(8,128)S(1)}, u32[]{:S(2)}, u32[]{:S(2)}) collective-permute-start(f32[176,128]{1,0:T(8,128)S(1)} %get-tuple-element.32), channel_id=1, source_target_pairs={{1,0},{2,1},{3,2},{4,3},{5,4},{6,5},{7,6},{8,7},{9,8},{10,9},{11,1... | collective-permute-start | bytes 270344 | tf_op jit(solution)/shard_map/ppermute | solution.py:415
  7.4 5.1 %start.1 = (f32[10,10,8,8,128]{4,3,2,1,0:T(8,128)S(1)}, f32[10,10,8,8,128]{4,3,2,1,0:T(8,128)S(1)}, f32[10,10,8,8,128]{4,3,2,1,0:T(8,128)S(1)}, f32[10,8,8,128]{...) custom-call(s32[3]{0:T(128)S(1)} %pad_add_fusion.pos_ref, f32[1,8]{1,0:T(1,128)} %bitcast.15, ...), custom_call_target="tpu_custom_call" | custom-call | flops 30000000 | bytes 11000000 | tf_op jit(solution)/shard_map/start/pallas_call | solution.py:418
  12.5 0.9 %collective-permute-done.left_ref = f32[176,128]{1,0:T(8,128)S(1)} collective-permute-done((f32[176,128]{1,0:T(8,128)S(1)}, f32[176,128]{1,0:T(8,128)S(1)}, u32[]{:S(2)}, u32[]{:S(2)}) %collective-permute-start) | collective-permute-done | bytes 90144 | tf_op jit(solution)/shard_map/ppermute | solution.py:414
  13.4 0.7 collective-permute-start.5
  14.0 1.2 %residual.1 = (f32[10,8,8,128]{3,2,1,0:T(8,128)S(1)}, f32[10,8,128]{2,1,0:T(8,128)S(1)}, f32[10,8,128]{2,1,0:T(8,128)S(1)}) custom-call(s32[3]{0:T(128)S(1)} %pad_add_fusion.pos_ref, f32[10,8,8,128]{3,2,1,0:T(8,128)S(1)} %get-tuple-element.34.r_ref, f32[176,128]{1,0:T(8,128)S(1)} %collective-permute-done.left_ref, ...), custom_call_target="tpu_custom_call" | custom-call | tf_op jit(solution)/shard_map/residual/pallas_call | solution.py:429
  15.3 3.3 %collective-permute-start.2 = (f32[10,8,128]{2,1,0:T(8,128)S(1)}, f32[10,8,128]{2,1,0:T(8,128)S(1)}, u32[]{:S(2)}, u32[]{:S(2)}) collective-permute-start(f32[10,8,128]{2,1,0:T(8,128)S(1)} %get-tuple-element.42), channel_id=1, source_target_pairs={{0,64},{1,65},{2,66},{3,67},{4,68},{5,69},{6,70},{7,71},{8,72},{9,... | collective-permute-start | bytes 122888 | tf_op jit(solution)/shard_map/ppermute | solution.py:432
  18.6 0.6 below.1
  19.2 1.1 %collective-permute-done.2.x_ref.x1_ref = f32[10,8,128]{2,1,0:T(8,128)S(1)} collective-permute-done((f32[10,8,128]{2,1,0:T(8,128)S(1)}, f32[10,8,128]{2,1,0:T(8,128)S(1)}, u32[]{:S(2)}, u32[]{:S(2)}) %collective-permute-start.2) | collective-permute-done | bytes 40992 | tf_op jit(solution)/shard_map/ppermute | solution.py:432
  20.3 1.3 %collective-permute-start.8 = (f32[10,10,8,128]{3,2,1,0:T(8,128)S(1)}, f32[10,10,8,128]{3,2,1,0:T(8,128)S(1)}, u32[]{:S(2)}, u32[]{:S(2)}) collective-permute-start(f32[10,10,8,128]{3,2,1,0:T(8,128)S(1)} %below.1), channel_id=1, source_target_pairs={{64,0},{65,1},{66,2},{67,3},{68,4},{69,5},{70,6},{71,7},{72,8},{73... | collective-permute-start | bytes 1228808 | tf_op jit(solution)/shard_map/ppermute | solution.py:437
  21.6 0.6 middle.1
  22.1 0.7 collective-permute-start.3
  22.8 0.7 collective-permute-start.4
  24.1 1.4 %place.1.pw_ref = f32[576,88]{1,0:T(8,128)S(1)} custom-call(s32[1]{0:T(128)S(6)} %copy.15.count_ref, f32[80,256]{1,0:T(8,128)S(1)} %bitcast.11, s32[1,256]{1,0:T(1,128)S(1)} %bitcast.12, s32[1,256]{1,0:T(1,128)S(1)} %bitcast.13), custom_call_target="tpu_custom_call" | custom-call | tf_op jit(solution)/shard_map/place/pallas_call | solution.py:443
  25.6 0.6 shift.1
  26.1 0.6 decide.1
  26.7 0.7 collective-permute-start.10
  27.4 1.3 %collective-permute-start.6 = (f32[10,8,128]{2,1,0:T(8,128)S(1)}, f32[10,8,128]{2,1,0:T(8,128)S(1)}, u32[]{:S(2)}, u32[]{:S(2)}) collective-permute-start(f32[10,8,128]{2,1,0:T(8,128)S(1)} %get-tuple-element.53), channel_id=1, source_target_pairs={{128,0},{129,1},{130,2},{131,3},{132,4},{133,5},{134,6},{135,7},{1... | collective-permute-start | bytes 122888 | tf_op jit(solution)/shard_map/ppermute | solution.py:453
  28.7 0.7 collective-permute-start.7
  29.3 1.3 %collective-permute-start.9 = (f32[10,8,128]{2,1,0:T(8,128)S(1)}, f32[10,8,128]{2,1,0:T(8,128)S(1)}, u32[]{:S(2)}, u32[]{:S(2)}) collective-permute-start(f32[10,8,128]{2,1,0:T(8,128)S(1)} %shift.1), channel_id=1, source_target_pairs={{64,0},{65,1},{66,2},{67,3},{68,4},{69,5},{70,6},{71,7},{72,8},{73... | collective-permute-start | bytes 122888 | tf_op jit(solution)/shard_map/ppermute | solution.py:455
  30.7 1.6 %scale.1.s_ref = f32[8,10,8,128]{3,2,1,0:T(8,128)S(1)} custom-call(s32[3]{0:T(128)S(1)} %pad_add_fusion.pos_ref, f32[10,8,128]{2,1,0:T(8,128)S(1)} %collective-permute-done.2.x_ref.x1_ref, f32[10,8,128]{2,1,0:T(8,128)S(1)} %collective-permute-done.10.x3_ref, f32[8,10,8,128]{3,2,1,0:T(8,128)S(1)} %get-tuple-element.59.s2_ref, ...), custom_call_target="tpu_custom_call" | custom-call | tf_op jit(solution)/shard_map/scale/pallas_call | solution.py:456
  32.2 4.7 %collective-permute-done.6.y10_ref = f32[10,8,128]{2,1,0:T(8,128)S(1)} collective-permute-done((f32[10,8,128]{2,1,0:T(8,128)S(1)}, f32[10,8,128]{2,1,0:T(8,128)S(1)}, u32[]{:S(2)}, u32[]{:S(2)}) %collective-permute-start.6) | collective-permute-done | bytes 40992 | tf_op jit(solution)/shard_map/ppermute | solution.py:453
  37.0 0.5 collective-permute-done.9.shift_ref
  37.4 2.1 %finish.1 = (f32[10,8,8,128]{3,2,1,0:T(8,128)}, f32[576,128]{1,0:T(8,128)}) custom-call(s32[3]{0:T(128)S(1)} %pad_add_fusion.pos_ref, f32[10,8,128]{2,1,0:T(8,128)S(1)} %get-tuple-element.50.y2_ref, f32[10,8,128]{2,1,0:T(8,128)S(1)} %collective-permute-done.6.y10_ref, f32[10,8,128]{2,1,0:T(8,128)S(1)} %collective-permute-done.7.y1_ref, ...), custom_call_target="tpu_custom_call" | custom-call | tf_op jit(solution)/shard_map/finish/pallas_call | solution.py:459
  39.5 21.0 %all_to_all.5 = f32[64,9,1,128]{3,2,1,0:T(1,128)S(1)} all-to-all(f32[64,9,1,128]{3,2,1,0:T(1,128)} %bitcast.14), channel_id=1, replica_groups=mesh['wall'=4,'tile'=64] {'tile'}, dimensions={0} | all-to-all | bytes 589824 | tf_op jit(solution)/shard_map/all_to_all | solution.py:463
  60.5 0.7 pick.1
  61.2 1.3 %collective-permute-start.11 = (f32[64,128]{1,0:T(8,128)S(1)}, f32[64,128]{1,0:T(8,128)S(1)}, u32[]{:S(2)}, u32[]{:S(2)}) collective-permute-start(f32[64,128]{1,0:T(8,128)S(1)} %pick.1), channel_id=1, source_target_pairs={{0,64},{64,128},{128,192},{192,0},{1,65},{65,129},{129,193},{193,1... | collective-permute-start | bytes 98312 | tf_op jit(solution)/shard_map/ppermute | solution.py:469
  62.5 1.1 %collective-permute-start.12 = (f32[64,128]{1,0:T(8,128)S(1)}, f32[64,128]{1,0:T(8,128)S(1)}, u32[]{:S(2)}, u32[]{:S(2)}) collective-permute-start(f32[64,128]{1,0:T(8,128)S(1)} %pick.1), channel_id=1, source_target_pairs={{0,128},{64,192},{128,0},{192,64},{1,129},{65,193},{129,1},{193,65... | collective-permute-start | bytes 98312 | tf_op jit(solution)/shard_map/ppermute | solution.py:469
  63.6 1.7 %collective-permute-start.13 = (f32[64,128]{1,0:T(8,128)S(1)}, f32[64,128]{1,0:T(8,128)S(1)}, u32[]{:S(2)}, u32[]{:S(2)}) collective-permute-start(f32[64,128]{1,0:T(8,128)S(1)} %pick.1), channel_id=1, source_target_pairs={{0,192},{64,0},{128,64},{192,128},{1,193},{65,1},{129,65},{193,129... | collective-permute-start | bytes 98312 | tf_op jit(solution)/shard_map/ppermute | solution.py:469
  65.3 1.1 %collective-permute-done.11 = f32[64,128]{1,0:T(8,128)S(1)} collective-permute-done((f32[64,128]{1,0:T(8,128)S(1)}, f32[64,128]{1,0:T(8,128)S(1)}, u32[]{:S(2)}, u32[]{:S(2)}) %collective-permute-start.11) | collective-permute-done | bytes 32800 | tf_op jit(solution)/shard_map/ppermute | solution.py:469
  66.4 1.5 %collective-permute-done.12 = f32[64,128]{1,0:T(8,128)S(1)} collective-permute-done((f32[64,128]{1,0:T(8,128)S(1)}, f32[64,128]{1,0:T(8,128)S(1)}, u32[]{:S(2)}, u32[]{:S(2)}) %collective-permute-start.12) | collective-permute-done | bytes 32800 | tf_op jit(solution)/shard_map/ppermute | solution.py:469
  67.9 0.6 add_add_fusion
  (16 shorter events, 0.1 us)
Async XLA Ops:
  1.7 10.8 %collective-permute-start.1 = (f32[176,128]{1,0:T(8,128)S(1)}, f32[176,128]{1,0:T(8,128)S(1)}, u32[]{:S(2)}, u32[]{:S(2)}) collective-permute-start(f32[176,128]{1,0:T(8,128)S(1)} %get-tuple-element.32), channel_id=1, source_target_pairs={{1,0},{2,1},{3,2},{4,3},{5,4},{6,5},{7,6},{8,7},{9,8},{10,9},{11,1... | collective-permute-start | bytes 270344 | tf_op jit(solution)/shard_map/ppermute | solution.py:415
  7.3 6.1 %collective-permute-start = (f32[176,128]{1,0:T(8,128)S(1)}, f32[176,128]{1,0:T(8,128)S(1)}, u32[]{:S(2)}, u32[]{:S(2)}) collective-permute-start(f32[176,128]{1,0:T(8,128)S(1)} %get-tuple-element.36), channel_id=1, source_target_pairs={{0,1},{1,2},{2,3},{3,4},{4,5},{5,6},{6,7},{7,8},{8,9},{9,10},{10,1... | collective-permute-start | bytes 270344 | tf_op jit(solution)/shard_map/ppermute | solution.py:414
  13.4 12.8 %collective-permute-start.5 = (f32[10,10,8,128]{3,2,1,0:T(8,128)S(1)}, f32[10,10,8,128]{3,2,1,0:T(8,128)S(1)}, u32[]{:S(2)}, u32[]{:S(2)}) collective-permute-start(f32[10,10,8,128]{3,2,1,0:T(8,128)S(1)} %get-tuple-element.49), channel_id=1, source_target_pairs={{192,128},{193,129},{194,130},{195,131},{196,132},{197,133},{198,1... | collective-permute-start | bytes 1228808 | tf_op jit(solution)/shard_map/ppermute | solution.py:428
  15.3 8.8 %copy-start = (f32[256,10,8]{0,2,1:T(8,128)S(1)}, f32[256,10,8]{0,2,1:T(8,128)}, u32[]{:S(2)}) copy-start(f32[256,10,8]{0,2,1:T(8,128)} %param.20) | copy-start | bytes 245764
  15.3 8.8 %copy-start.1 = (s32[256,1]{0,1:T(1,128)S(1)}, s32[256,1]{0,1:T(1,128)}, u32[]{:S(2)}) copy-start(s32[256,1]{0,1:T(1,128)} %param.21) | copy-start | bytes 3076
  15.3 8.8 %copy-start.2 = (s32[256]{0:T(256)S(1)}, s32[256]{0:T(256)}, u32[]{:S(2)}) copy-start(s32[256]{0:T(256)} %param.22) | copy-start | bytes 3076
  15.3 5.0 %collective-permute-start.2 = (f32[10,8,128]{2,1,0:T(8,128)S(1)}, f32[10,8,128]{2,1,0:T(8,128)S(1)}, u32[]{:S(2)}, u32[]{:S(2)}) collective-permute-start(f32[10,8,128]{2,1,0:T(8,128)S(1)} %get-tuple-element.42), channel_id=1, source_target_pairs={{0,64},{1,65},{2,66},{3,67},{4,68},{5,69},{6,70},{7,71},{8,72},{9,... | collective-permute-start | bytes 122888 | tf_op jit(solution)/shard_map/ppermute | solution.py:432
  20.3 17.2 %collective-permute-start.8 = (f32[10,10,8,128]{3,2,1,0:T(8,128)S(1)}, f32[10,10,8,128]{3,2,1,0:T(8,128)S(1)}, u32[]{:S(2)}, u32[]{:S(2)}) collective-permute-start(f32[10,10,8,128]{3,2,1,0:T(8,128)S(1)} %below.1), channel_id=1, source_target_pairs={{64,0},{65,1},{66,2},{67,3},{68,4},{69,5},{70,6},{71,7},{72,8},{73... | collective-permute-start | bytes 1228808 | tf_op jit(solution)/shard_map/ppermute | solution.py:437
  22.1 4.0 %collective-permute-start.3 = (f32[10,8,128]{2,1,0:T(8,128)S(1)}, f32[10,8,128]{2,1,0:T(8,128)S(1)}, u32[]{:S(2)}, u32[]{:S(2)}) collective-permute-start(f32[10,8,128]{2,1,0:T(8,128)S(1)} %middle.1), channel_id=1, source_target_pairs={{64,128},{65,129},{66,130},{67,131},{68,132},{69,133},{70,134},{71... | collective-permute-start | bytes 122888 | tf_op jit(solution)/shard_map/ppermute | solution.py:440
  22.8 3.3 %collective-permute-start.4 = (f32[10,8,128]{2,1,0:T(8,128)S(1)}, f32[10,8,128]{2,1,0:T(8,128)S(1)}, u32[]{:S(2)}, u32[]{:S(2)}) collective-permute-start(f32[10,8,128]{2,1,0:T(8,128)S(1)} %get-tuple-element.48), channel_id=1, source_target_pairs={{192,128},{193,129},{194,130},{195,131},{196,132},{197,133},{198,1... | collective-permute-start | bytes 122888 | tf_op jit(solution)/shard_map/ppermute | solution.py:433
  26.7 3.9 %collective-permute-start.10 = (f32[10,8,128]{2,1,0:T(8,128)S(1)}, f32[10,8,128]{2,1,0:T(8,128)S(1)}, u32[]{:S(2)}, u32[]{:S(2)}) collective-permute-start(f32[10,8,128]{2,1,0:T(8,128)S(1)} %get-tuple-element.58), channel_id=1, source_target_pairs={{128,192},{129,193},{130,194},{131,195},{132,196},{133,197},{134,1... | collective-permute-start | bytes 122888 | tf_op jit(solution)/shard_map/ppermute | solution.py:452
  27.4 9.6 %collective-permute-start.6 = (f32[10,8,128]{2,1,0:T(8,128)S(1)}, f32[10,8,128]{2,1,0:T(8,128)S(1)}, u32[]{:S(2)}, u32[]{:S(2)}) collective-permute-start(f32[10,8,128]{2,1,0:T(8,128)S(1)} %get-tuple-element.53), channel_id=1, source_target_pairs={{128,0},{129,1},{130,2},{131,3},{132,4},{133,5},{134,6},{135,7},{1... | collective-permute-start | bytes 122888 | tf_op jit(solution)/shard_map/ppermute | solution.py:453
  28.7 8.3 %collective-permute-start.7 = (f32[10,8,128]{2,1,0:T(8,128)S(1)}, f32[10,8,128]{2,1,0:T(8,128)S(1)}, u32[]{:S(2)}, u32[]{:S(2)}) collective-permute-start(f32[10,8,128]{2,1,0:T(8,128)S(1)} %get-tuple-element.53), channel_id=1, source_target_pairs={{128,64},{129,65},{130,66},{131,67},{132,68},{133,69},{134,70},{13... | collective-permute-start | bytes 122888 | tf_op jit(solution)/shard_map/ppermute | solution.py:454
  29.3 8.1 %collective-permute-start.9 = (f32[10,8,128]{2,1,0:T(8,128)S(1)}, f32[10,8,128]{2,1,0:T(8,128)S(1)}, u32[]{:S(2)}, u32[]{:S(2)}) collective-permute-start(f32[10,8,128]{2,1,0:T(8,128)S(1)} %shift.1), channel_id=1, source_target_pairs={{64,0},{65,1},{66,2},{67,3},{68,4},{69,5},{70,6},{71,7},{72,8},{73... | collective-permute-start | bytes 122888 | tf_op jit(solution)/shard_map/ppermute | solution.py:455
  61.2 5.2 %collective-permute-start.11 = (f32[64,128]{1,0:T(8,128)S(1)}, f32[64,128]{1,0:T(8,128)S(1)}, u32[]{:S(2)}, u32[]{:S(2)}) collective-permute-start(f32[64,128]{1,0:T(8,128)S(1)} %pick.1), channel_id=1, source_target_pairs={{0,64},{64,128},{128,192},{192,0},{1,65},{65,129},{129,193},{193,1... | collective-permute-start | bytes 98312 | tf_op jit(solution)/shard_map/ppermute | solution.py:469
  62.5 5.4 %collective-permute-start.12 = (f32[64,128]{1,0:T(8,128)S(1)}, f32[64,128]{1,0:T(8,128)S(1)}, u32[]{:S(2)}, u32[]{:S(2)}) collective-permute-start(f32[64,128]{1,0:T(8,128)S(1)} %pick.1), channel_id=1, source_target_pairs={{0,128},{64,192},{128,0},{192,64},{1,129},{65,193},{129,1},{193,65... | collective-permute-start | bytes 98312 | tf_op jit(solution)/shard_map/ppermute | solution.py:469
  63.6 4.3 %collective-permute-start.13 = (f32[64,128]{1,0:T(8,128)S(1)}, f32[64,128]{1,0:T(8,128)S(1)}, u32[]{:S(2)}, u32[]{:S(2)}) collective-permute-start(f32[64,128]{1,0:T(8,128)S(1)} %pick.1), channel_id=1, source_target_pairs={{0,192},{64,0},{128,64},{192,128},{1,193},{65,1},{129,65},{193,129... | collective-permute-start | bytes 98312 | tf_op jit(solution)/shard_map/ppermute | solution.py:469

commit v8 on v6

--- a/solution.py
+++ b/solution.py
@@ -186,10 +186,10 @@
         w_ref[k] = jnp.broadcast_to(w_in[:, k : k + 1], (H, S))
     for copy in state:
         copy.wait()
-    interior(a_ref, src_ref, rad_ref, frq_ref, r_ref)
 
     @pl.when(wall != 3)
     def _():
+        interior(a_ref, src_ref, rad_ref, frq_ref, r_ref)
         for k in range(K - 1, -1, -1):
             arrived(k)
 
@@ -226,7 +226,10 @@
                 map_ref[c] = out
 
 
-def residual_kernel(pos_ref, r_ref, left_ref, right_ref, rad_ref, l_ref, d_ref, u_ref, out_ref, up_ref, down_ref, s_ref):
+def residual_kernel(
+    pos_ref, inner_ref, a_ref, src_ref, frq_ref, left_ref, right_ref, rad_ref, l_ref, d_ref, u_ref,
+    out_ref, up_ref, down_ref, s_ref, late_ref,
+):
     wall, tile, last = pos_ref[0], pos_ref[1], pos_ref[2]
     row = lax.broadcasted_iota(jnp.int32, (H, S), 0)
     has_left = tile > 0
@@ -236,20 +239,30 @@
         at = 2 * (v * K + k) + c
         return jnp.broadcast_to(ref[at : at + 1, :], (H, S))
 
-    for k in range(K):
-        rad = rad_ref[k]
-        l0, l1, r0, r1 = (line(ref, NV, k, c) for ref in (left_ref, right_ref) for c in (0, 1))
-        zero = jnp.zeros((H, S), F32)
-        f_l0 = jnp.where((row == 0) & has_left, -0.0625 * (rad + l0), zero)
-        f_l1 = jnp.where(row == 0, 0.25 * (rad + l1), jnp.where(row == 1, -0.0625 * (rad + l1), zero))
-        f_l1 = jnp.where(has_left, f_l1, zero)
-        f_r0 = jnp.where(row == 7, 0.25 * (rad + r0), jnp.where(row == 6, -0.0625 * (rad + r0), zero))
-        f_r0 = jnp.where(has_right, f_r0, zero)
-        f_r1 = jnp.where((row == 7) & has_right, -0.0625 * (rad + r1), zero)
-        for v in range(NV):
-            applied = f_l0 * line(left_ref, v, k, 0) + f_l1 * line(left_ref, v, k, 1)
-            applied = applied + (f_r0 * line(right_ref, v, k, 0) + f_r1 * line(right_ref, v, k, 1))
-            out_ref[v, k] = r_ref[v, k] - applied
+    def add_halo(r_ref):
+        for k in range(K):
+            rad = rad_ref[k]
+            l0, l1, r0, r1 = (line(ref, NV, k, c) for ref in (left_ref, right_ref) for c in (0, 1))
+            zero = jnp.zeros((H, S), F32)
+            f_l0 = jnp.where((row == 0) & has_left, -0.0625 * (rad + l0), zero)
+            f_l1 = jnp.where(row == 0, 0.25 * (rad + l1), jnp.where(row == 1, -0.0625 * (rad + l1), zero))
+            f_l1 = jnp.where(has_left, f_l1, zero)
+            f_r0 = jnp.where(row == 7, 0.25 * (rad + r0), jnp.where(row == 6, -0.0625 * (rad + r0), zero))
+            f_r0 = jnp.where(has_right, f_r0, zero)
+            f_r1 = jnp.where((row == 7) & has_right, -0.0625 * (rad + r1), zero)
+            for v in range(NV):
+                applied = f_l0 * line(left_ref, v, k, 0) + f_l1 * line(left_ref, v, k, 1)
+                applied = applied + (f_r0 * line(right_ref, v, k, 0) + f_r1 * line(right_ref, v, k, 1))
+                out_ref[v, k] = r_ref[v, k] - applied
+
+    @pl.when(wall == 3)
+    def _():
+        interior(a_ref, src_ref, rad_ref, frq_ref, late_ref)
+        add_halo(late_ref)
+
+    @pl.when(wall != 3)
+    def _():
+        add_halo(inner_ref)
 
     @pl.when(wall == 0)
     def _():
@@ -326,7 +339,7 @@
 
 
 def finish_kernel(
-    pos_ref, y2_ref, y1_ref, y10_ref, below_ref, shift_ref, w_ref, pw_ref, s_ref, u_ref, out_ref, rows_ref, y_ref, prof_ref
+    pos_ref, y2_ref, y10_ref, y1_ref, below_ref, shift_ref, w_ref, pw_ref, s_ref, u_ref, out_ref, rows_ref, y_ref, prof_ref
 ):
     wall = pos_ref[0]
 
@@ -419,11 +432,11 @@
     right = lax.ppermute(lo, "tile", [((i + 1) % tiles, i) for i in range(tiles)])
 
     lo, pos1 = tie((lo, pos))
-    lower, diag, upper, inner, weight, maps = call(
-        "start", start_kernel, (block, block, block, state, cell, f32(NV, NV, H, S)), 9, smem=(0,),
+    lower, diag, upper, inner, weight, maps, adjoint, source, radius, frequency = call(
+        "start", start_kernel, (block, block, block, state, cell, f32(NV, NV, H, S), state, state, cell, cell), 9, smem=(0,),
         far=(2, 3, 4, 5, 6, 7, 8),
         scratch=(
-            state, state, cell, cell, held(NV, NV, H, S), held(NV, NV, H, S), pltpu.SemaphoreType.DMA((4,)), pltpu.SemaphoreType.DMA((K, 3)),
+            held(NV, NV, H, S), held(NV, NV, H, S), pltpu.SemaphoreType.DMA((4,)), pltpu.SemaphoreType.DMA((K, 3)),
         ),
         flops=30_000_000, nbytes=11_000_000,
     )(pos1, wall_weight, adjoint, source, radius, frequency, lower, diag, upper)
@@ -431,8 +444,8 @@
     maps, left, right = tie((maps, left, right))
     above = lax.ppermute(maps, "wall", [(3, 2)])
     resid, up, down = call(
-        "residual", residual_kernel, (state, vec, vec), 8, smem=(0,), scratch=(levels,)
-    )(pos, inner, left, right, radius, lower, diag, upper)
+        "residual", residual_kernel, (state, vec, vec), 11, smem=(0,), scratch=(levels, state)
+    )(pos, inner, adjoint, source, frequency, left, right, radius, lower, diag, upper)
     x1 = lax.ppermute(up, "wall", [(0, 1)])
     b3 = lax.ppermute(down, "wall", [(3, 2)])
     up, pos1 = tie((up, pos))
@@ -450,9 +463,10 @@
 
     x2, placed = tie((x2, placed))
     x3, scaled2 = call("rise", rise_kernel, (vec, levels), 5, smem=(0,))(pos, x2, resid, lower, diag)
+    y2, y1 = call("decide", decide_kernel, (vec, vec), 6, smem=(0,))(pos, x3, b3, above, scaled2, upper)
+    x3, y1 = tie((x3, y1))
+    y1, shift = tie((y1, shift))
     x33 = lax.ppermute(x3, "wall", [(2, 3)])
-    y2, y1 = call("decide", decide_kernel, (vec, vec), 6, smem=(0,))(pos, x3, b3, above, scaled2, upper)
-    y1, shift = tie((y1, shift))
     y10 = lax.ppermute(y1, "wall", [(2, 0)])
     y11 = lax.ppermute(y1, "wall", [(2, 1)])
     shift = lax.ppermute(shift, "wall", [(1, 0)])
@@ -462,7 +476,7 @@
     adjoint_next, rows = call(
         "finish", finish_kernel, (f32(NV, K, H, S), away(tiles * ROWS_PER_OWNER, S)), 10, smem=(0,),
         scratch=(held(NV, H, S), held(NV * H + SLOTS, S)),
-    )(pos, y2, y11, y10, below, shift, weight, placed, scaled, upper)
+    )(pos, y2, y10, y11, below, shift, weight, placed, scaled, upper)
     got = lax.all_to_all(rows.reshape(tiles, ROWS_PER_OWNER, 1, S), "tile", split_axis=0, concat_axis=0)
     got = got.reshape(tiles * ROWS_PER_OWNER, S)
     part = call("pick", pick_kernel, f32(PATCH_DEV, S), 1)(got)

time: 70.8 us -> 68.6 us (0.969)
  waiting for transfers between devices: 12.3 us -> 9.95 us
  starting transfers between devices: 19.4 us -> 20.3 us
    ppermute x1, waiting for transfers between devices: 7.2 us -> 4.72 us  [on_device(): y10 = lax.ppermute(y1, 'wall', [(2, 0)])]
    ppermute x3, starting transfers between devices: 3.29 us -> 4.02 us  [on_device(): lax.ppermute(part, 'wall', [(w, (w + d) % walls) for w in range(walls)])]
where the time goes in v8:
time: 68.6 us; the launch traced here: 68.3 us
  starting transfers between devices  20.3 us (30%)
  blocking collectives  20.3 us (30%)
  Pallas kernels  15.5 us (23%)
  waiting for transfers between devices  9.95 us (15%)
  between operations  1.51 us (2%)
  other arithmetic  0.7 us (1%)
    all_to_all x1, blocking collectives, on_device(): lax.all_to_all(rows.reshape(tiles, ROWS_PER_OWNER, 1, S), 'tile', split_a...  20.3 us
    ppermute x1, starting transfers between devices, on_device(): lax.ppermute(lo, 'tile', [((i + 1) % tiles, i) for i in range(tiles)])  5.64 us
    pallas_call x1, Pallas kernels, on_device(): call('start', start_kernel, (block, block, block, state, cell, f32(NV, NV...  5.1 us
    ppermute x1, waiting for transfers between devices, on_device(): y10 = lax.ppermute(y1, 'wall', [(2, 0)])  4.72 us
    ppermute x3, starting transfers between devices, on_device(): lax.ppermute(part, 'wall', [(w, (w + d) % walls) for w in range(walls)])  4.02 us
    ppermute x1, starting transfers between devices, on_device(): x1 = lax.ppermute(up, 'wall', [(0, 1)])  3.29 us
    ppermute x3, waiting for transfers between devices, on_device(): lax.ppermute(part, 'wall', [(w, (w + d) % walls) for w in range(walls)])  2.59 us
    pallas_call x1, Pallas kernels, on_device(): call('finish', finish_kernel, (f32(NV, K, H, S), away(tiles * ROWS_PER_OW...  2.11 us
  transfers between devices with their start and end apart: 14, of which 6 were waited for; matrix products, arithmetic and copies ran while one was open for 0% of the time, Pallas kernels for 17%

profile of v8, /device:TPU:6, one launch (start us, length us, event | category | flops | bytes accessed | tf_op | source)
XLA Modules:
  0.0 68.3 jit_solution(16479775430056728800)
XLA Ops:
  0.6 1.0 %pack.1 = (f32[176,128]{1,0:T(8,128)S(1)}, f32[176,128]{1,0:T(8,128)S(1)}) custom-call(f32[10,8,8,128]{3,2,1,0:T(8,128)} %a_in.1, f32[8,8,128]{2,1,0:T(8,128)} %rad_in.1), custom_call_target="tpu_custom_call" | custom-call | bytes 800000 | tf_op jit(solution)/shard_map/pack/pallas_call | solution.py:430
  1.7 5.6 %collective-permute-start.1 = (f32[176,128]{1,0:T(8,128)S(1)}, f32[176,128]{1,0:T(8,128)S(1)}, u32[]{:S(2)}, u32[]{:S(2)}) collective-permute-start(f32[176,128]{1,0:T(8,128)S(1)} %get-tuple-element.38), channel_id=1, source_target_pairs={{1,0},{2,1},{3,2},{4,3},{5,4},{6,5},{7,6},{8,7},{9,8},{10,9},{11,1... | collective-permute-start | bytes 270344 | tf_op jit(solution)/shard_map/ppermute | solution.py:432
  7.4 5.1 %start.1 = (f32[10,10,8,8,128]{4,3,2,1,0:T(8,128)S(1)}, f32[10,10,8,8,128]{4,3,2,1,0:T(8,128)S(1)}, f32[10,10,8,8,128]{4,3,2,1,0:T(8,128)S(1)}, f32[10,8,8,128]{...) custom-call(s32[3]{0:T(128)S(1)} %pad_add_fusion.pos_ref, ...), custom_call_target="tpu_custom_call" | custom-call | flops 30000000 | bytes 11000000 | tf_op jit(solution)/shard_map/start/pallas_call | solution.py:435
  12.5 0.9 %collective-permute-done.left_ref = f32[176,128]{1,0:T(8,128)S(1)} collective-permute-done((f32[176,128]{1,0:T(8,128)S(1)}, f32[176,128]{1,0:T(8,128)S(1)}, u32[]{:S(2)}, u32[]{:S(2)}) %collective-permute-start) | collective-permute-done | bytes 90144 | tf_op jit(solution)/shard_map/ppermute | solution.py:431
  13.4 0.7 collective-permute-start.5
  14.0 1.0 %residual.1 = (f32[10,8,8,128]{3,2,1,0:T(8,128)S(1)}, f32[10,8,128]{2,1,0:T(8,128)S(1)}, f32[10,8,128]{2,1,0:T(8,128)S(1)}) custom-call(s32[3]{0:T(128)S(1)} %pad_add_fusion.pos_ref, f32[10,8,8,128]{3,2,1,0:T(8,128)S(1)} %get-tuple-element.40.inner_ref, f32[10,8,8,128]{3,2,1,0:T(8,128)S(1)} %get-tuple-element.41.a_ref, ...), custom_call_target="tpu_custom_call" | custom-call | tf_op jit(solution)/shard_map/residual/pallas_call | solution.py:446
  15.1 3.3 %collective-permute-start.2 = (f32[10,8,128]{2,1,0:T(8,128)S(1)}, f32[10,8,128]{2,1,0:T(8,128)S(1)}, u32[]{:S(2)}, u32[]{:S(2)}) collective-permute-start(f32[10,8,128]{2,1,0:T(8,128)S(1)} %get-tuple-element.52), channel_id=1, source_target_pairs={{0,64},{1,65},{2,66},{3,67},{4,68},{5,69},{6,70},{7,71},{8,72},{9,... | collective-permute-start | bytes 122888 | tf_op jit(solution)/shard_map/ppermute | solution.py:449
  18.4 0.6 below.1
  19.0 1.1 %collective-permute-done.2.x_ref.x1_ref = f32[10,8,128]{2,1,0:T(8,128)S(1)} collective-permute-done((f32[10,8,128]{2,1,0:T(8,128)S(1)}, f32[10,8,128]{2,1,0:T(8,128)S(1)}, u32[]{:S(2)}, u32[]{:S(2)}) %collective-permute-start.2) | collective-permute-done | bytes 40992 | tf_op jit(solution)/shard_map/ppermute | solution.py:449
  20.1 1.3 %collective-permute-start.8 = (f32[10,10,8,128]{3,2,1,0:T(8,128)S(1)}, f32[10,10,8,128]{3,2,1,0:T(8,128)S(1)}, u32[]{:S(2)}, u32[]{:S(2)}) collective-permute-start(f32[10,10,8,128]{3,2,1,0:T(8,128)S(1)} %below.1), channel_id=1, source_target_pairs={{64,0},{65,1},{66,2},{67,3},{68,4},{69,5},{70,6},{71,7},{72,8},{73... | collective-permute-start | bytes 1228808 | tf_op jit(solution)/shard_map/ppermute | solution.py:454
  21.9 0.7 collective-permute-start.3
  22.6 0.7 collective-permute-start.4
  23.9 1.4 %place.1.pw_ref = f32[576,88]{1,0:T(8,128)S(1)} custom-call(s32[1]{0:T(128)S(6)} %copy.15.count_ref, f32[80,256]{1,0:T(8,128)S(1)} %bitcast.11, s32[1,256]{1,0:T(1,128)S(1)} %bitcast.12, s32[1,256]{1,0:T(1,128)S(1)} %bitcast.13), custom_call_target="tpu_custom_call" | custom-call | tf_op jit(solution)/shard_map/place/pallas_call | solution.py:460
  25.3 0.6 shift.1
  25.9 0.6 rise.1
  26.5 0.6 decide.1
  27.0 0.7 collective-permute-start.10
  27.7 1.3 %collective-permute-start.6 = (f32[10,8,128]{2,1,0:T(8,128)S(1)}, f32[10,8,128]{2,1,0:T(8,128)S(1)}, u32[]{:S(2)}, u32[]{:S(2)}) collective-permute-start(f32[10,8,128]{2,1,0:T(8,128)S(1)} %get-tuple-element.66), channel_id=1, source_target_pairs={{128,0},{129,1},{130,2},{131,3},{132,4},{133,5},{134,6},{135,7},{1... | collective-permute-start | bytes 122888 | tf_op jit(solution)/shard_map/ppermute | solution.py:470
  29.0 0.8 %collective-permute-start.7 = (f32[10,8,128]{2,1,0:T(8,128)S(1)}, f32[10,8,128]{2,1,0:T(8,128)S(1)}, u32[]{:S(2)}, u32[]{:S(2)}) collective-permute-start(f32[10,8,128]{2,1,0:T(8,128)S(1)} %get-tuple-element.66), channel_id=1, source_target_pairs={{128,64},{129,65},{130,66},{131,67},{132,68},{133,69},{134,70},{13... | collective-permute-start | bytes 122888 | tf_op jit(solution)/shard_map/ppermute | solution.py:471
  29.9 1.3 %collective-permute-start.9 = (f32[10,8,128]{2,1,0:T(8,128)S(1)}, f32[10,8,128]{2,1,0:T(8,128)S(1)}, u32[]{:S(2)}, u32[]{:S(2)}) collective-permute-start(f32[10,8,128]{2,1,0:T(8,128)S(1)} %shift.1), channel_id=1, source_target_pairs={{64,0},{65,1},{66,2},{67,3},{68,4},{69,5},{70,6},{71,7},{72,8},{73... | collective-permute-start | bytes 122888 | tf_op jit(solution)/shard_map/ppermute | solution.py:472
  31.2 1.4 %scale.1.s_ref = f32[8,10,8,128]{3,2,1,0:T(8,128)S(1)} custom-call(s32[3]{0:T(128)S(1)} %pad_add_fusion.pos_ref, f32[10,8,128]{2,1,0:T(8,128)S(1)} %collective-permute-done.2.x_ref.x1_ref, f32[10,8,128]{2,1,0:T(8,128)S(1)} %collective-permute-done.10.x3_ref, f32[8,10,8,128]{3,2,1,0:T(8,128)S(1)} %get-tuple-element.61.s_ref.s2_ref, ...), custom_call_target="tpu_custom_call" | custom-call | tf_op jit(solution)/shard_map/scale/pallas_call | solution.py:473
  32.6 4.7 %collective-permute-done.6.y10_ref = f32[10,8,128]{2,1,0:T(8,128)S(1)} collective-permute-done((f32[10,8,128]{2,1,0:T(8,128)S(1)}, f32[10,8,128]{2,1,0:T(8,128)S(1)}, u32[]{:S(2)}, u32[]{:S(2)}) %collective-permute-start.6) | collective-permute-done | bytes 40992 | tf_op jit(solution)/shard_map/ppermute | solution.py:470
  37.3 0.7 collective-permute-done.9.shift_ref
  38.0 2.1 %finish.1 = (f32[10,8,8,128]{3,2,1,0:T(8,128)}, f32[576,128]{1,0:T(8,128)}) custom-call(s32[3]{0:T(128)S(1)} %pad_add_fusion.pos_ref, f32[10,8,128]{2,1,0:T(8,128)S(1)} %get-tuple-element.62.y2_ref, f32[10,8,128]{2,1,0:T(8,128)S(1)} %collective-permute-done.6.y10_ref, f32[10,8,128]{2,1,0:T(8,128)S(1)} %collective-permute-done.7.y1_ref, ...), custom_call_target="tpu_custom_call" | custom-call | tf_op jit(solution)/shard_map/finish/pallas_call | solution.py:476
  40.1 20.3 %all_to_all.5 = f32[64,9,1,128]{3,2,1,0:T(1,128)S(1)} all-to-all(f32[64,9,1,128]{3,2,1,0:T(1,128)} %bitcast.14), channel_id=1, replica_groups=mesh['wall'=4,'tile'=64] {'tile'}, dimensions={0} | all-to-all | bytes 589824 | tf_op jit(solution)/shard_map/all_to_all | solution.py:480
  60.4 0.7 pick.1
  61.0 1.2 %collective-permute-start.11 = (f32[64,128]{1,0:T(8,128)S(1)}, f32[64,128]{1,0:T(8,128)S(1)}, u32[]{:S(2)}, u32[]{:S(2)}) collective-permute-start(f32[64,128]{1,0:T(8,128)S(1)} %pick.1), channel_id=1, source_target_pairs={{0,64},{64,128},{128,192},{192,0},{1,65},{65,129},{129,193},{193,1... | collective-permute-start | bytes 98312 | tf_op jit(solution)/shard_map/ppermute | solution.py:486
  62.2 0.6 collective-permute-start.12
  62.9 2.2 %collective-permute-start.13 = (f32[64,128]{1,0:T(8,128)S(1)}, f32[64,128]{1,0:T(8,128)S(1)}, u32[]{:S(2)}, u32[]{:S(2)}) collective-permute-start(f32[64,128]{1,0:T(8,128)S(1)} %pick.1), channel_id=1, source_target_pairs={{0,192},{64,0},{128,64},{192,128},{1,193},{65,1},{129,65},{193,129... | collective-permute-start | bytes 98312 | tf_op jit(solution)/shard_map/ppermute | solution.py:486
  65.1 1.2 %collective-permute-done.11 = f32[64,128]{1,0:T(8,128)S(1)} collective-permute-done((f32[64,128]{1,0:T(8,128)S(1)}, f32[64,128]{1,0:T(8,128)S(1)}, u32[]{:S(2)}, u32[]{:S(2)}) %collective-permute-start.11) | collective-permute-done | bytes 32800 | tf_op jit(solution)/shard_map/ppermute | solution.py:486
  66.2 1.4 %collective-permute-done.12 = f32[64,128]{1,0:T(8,128)S(1)} collective-permute-done((f32[64,128]{1,0:T(8,128)S(1)}, f32[64,128]{1,0:T(8,128)S(1)}, u32[]{:S(2)}, u32[]{:S(2)}) %collective-permute-start.12) | collective-permute-done | bytes 32800 | tf_op jit(solution)/shard_map/ppermute | solution.py:486
  67.7 0.6 add_add_fusion
  (17 shorter events, 0.7 us)
Async XLA Ops:
  1.7 10.8 %collective-permute-start.1 = (f32[176,128]{1,0:T(8,128)S(1)}, f32[176,128]{1,0:T(8,128)S(1)}, u32[]{:S(2)}, u32[]{:S(2)}) collective-permute-start(f32[176,128]{1,0:T(8,128)S(1)} %get-tuple-element.38), channel_id=1, source_target_pairs={{1,0},{2,1},{3,2},{4,3},{5,4},{6,5},{7,6},{8,7},{9,8},{10,9},{11,1... | collective-permute-start | bytes 270344 | tf_op jit(solution)/shard_map/ppermute | solution.py:432
  7.3 6.1 %collective-permute-start = (f32[176,128]{1,0:T(8,128)S(1)}, f32[176,128]{1,0:T(8,128)S(1)}, u32[]{:S(2)}, u32[]{:S(2)}) collective-permute-start(f32[176,128]{1,0:T(8,128)S(1)} %get-tuple-element.45), channel_id=1, source_target_pairs={{0,1},{1,2},{2,3},{3,4},{4,5},{5,6},{6,7},{7,8},{8,9},{9,10},{10,1... | collective-permute-start | bytes 270344 | tf_op jit(solution)/shard_map/ppermute | solution.py:431
  13.4 13.1 %collective-permute-start.5 = (f32[10,10,8,128]{3,2,1,0:T(8,128)S(1)}, f32[10,10,8,128]{3,2,1,0:T(8,128)S(1)}, u32[]{:S(2)}, u32[]{:S(2)}) collective-permute-start(f32[10,10,8,128]{3,2,1,0:T(8,128)S(1)} %get-tuple-element.60), channel_id=1, source_target_pairs={{192,128},{193,129},{194,130},{195,131},{196,132},{197,133},{198,1... | collective-permute-start | bytes 1228808 | tf_op jit(solution)/shard_map/ppermute | solution.py:445
  15.1 8.8 %copy-start = (f32[256,10,8]{0,2,1:T(8,128)S(1)}, f32[256,10,8]{0,2,1:T(8,128)}, u32[]{:S(2)}) copy-start(f32[256,10,8]{0,2,1:T(8,128)} %param.20) | copy-start | bytes 245764
  15.1 8.8 %copy-start.1 = (s32[256,1]{0,1:T(1,128)S(1)}, s32[256,1]{0,1:T(1,128)}, u32[]{:S(2)}) copy-start(s32[256,1]{0,1:T(1,128)} %param.21) | copy-start | bytes 3076
  15.1 8.8 %copy-start.2 = (s32[256]{0:T(256)S(1)}, s32[256]{0:T(256)}, u32[]{:S(2)}) copy-start(s32[256]{0:T(256)} %param.22) | copy-start | bytes 3076
  15.1 4.9 %collective-permute-start.2 = (f32[10,8,128]{2,1,0:T(8,128)S(1)}, f32[10,8,128]{2,1,0:T(8,128)S(1)}, u32[]{:S(2)}, u32[]{:S(2)}) collective-permute-start(f32[10,8,128]{2,1,0:T(8,128)S(1)} %get-tuple-element.52), channel_id=1, source_target_pairs={{0,64},{1,65},{2,66},{3,67},{4,68},{5,69},{6,70},{7,71},{8,72},{9,... | collective-permute-start | bytes 122888 | tf_op jit(solution)/shard_map/ppermute | solution.py:449
  20.1 17.9 %collective-permute-start.8 = (f32[10,10,8,128]{3,2,1,0:T(8,128)S(1)}, f32[10,10,8,128]{3,2,1,0:T(8,128)S(1)}, u32[]{:S(2)}, u32[]{:S(2)}) collective-permute-start(f32[10,10,8,128]{3,2,1,0:T(8,128)S(1)} %below.1), channel_id=1, source_target_pairs={{64,0},{65,1},{66,2},{67,3},{68,4},{69,5},{70,6},{71,7},{72,8},{73... | collective-permute-start | bytes 1228808 | tf_op jit(solution)/shard_map/ppermute | solution.py:454
  21.9 4.0 %collective-permute-start.3 = (f32[10,8,128]{2,1,0:T(8,128)S(1)}, f32[10,8,128]{2,1,0:T(8,128)S(1)}, u32[]{:S(2)}, u32[]{:S(2)}) collective-permute-start(f32[10,8,128]{2,1,0:T(8,128)S(1)} %middle.1), channel_id=1, source_target_pairs={{64,128},{65,129},{66,130},{67,131},{68,132},{69,133},{70,134},{71... | collective-permute-start | bytes 122888 | tf_op jit(solution)/shard_map/ppermute | solution.py:457
  22.6 3.9 %collective-permute-start.4 = (f32[10,8,128]{2,1,0:T(8,128)S(1)}, f32[10,8,128]{2,1,0:T(8,128)S(1)}, u32[]{:S(2)}, u32[]{:S(2)}) collective-permute-start(f32[10,8,128]{2,1,0:T(8,128)S(1)} %get-tuple-element.59), channel_id=1, source_target_pairs={{192,128},{193,129},{194,130},{195,131},{196,132},{197,133},{198,1... | collective-permute-start | bytes 122888 | tf_op jit(solution)/shard_map/ppermute | solution.py:450
  27.0 4.1 %collective-permute-start.10 = (f32[10,8,128]{2,1,0:T(8,128)S(1)}, f32[10,8,128]{2,1,0:T(8,128)S(1)}, u32[]{:S(2)}, u32[]{:S(2)}) collective-permute-start(f32[10,8,128]{2,1,0:T(8,128)S(1)} %get-tuple-element.71.x3_ref), channel_id=1, source_target_pairs={{128,192},{129,193},{130,194},{131,195},{132,196},{133,197},{134,1... | collective-permute-start | bytes 122888 | tf_op jit(solution)/shard_map/ppermute | solution.py:469
  27.7 9.6 %collective-permute-start.6 = (f32[10,8,128]{2,1,0:T(8,128)S(1)}, f32[10,8,128]{2,1,0:T(8,128)S(1)}, u32[]{:S(2)}, u32[]{:S(2)}) collective-permute-start(f32[10,8,128]{2,1,0:T(8,128)S(1)} %get-tuple-element.66), channel_id=1, source_target_pairs={{128,0},{129,1},{130,2},{131,3},{132,4},{133,5},{134,6},{135,7},{1... | collective-permute-start | bytes 122888 | tf_op jit(solution)/shard_map/ppermute | solution.py:470
  29.0 8.3 %collective-permute-start.7 = (f32[10,8,128]{2,1,0:T(8,128)S(1)}, f32[10,8,128]{2,1,0:T(8,128)S(1)}, u32[]{:S(2)}, u32[]{:S(2)}) collective-permute-start(f32[10,8,128]{2,1,0:T(8,128)S(1)} %get-tuple-element.66), channel_id=1, source_target_pairs={{128,64},{129,65},{130,66},{131,67},{132,68},{133,69},{134,70},{13... | collective-permute-start | bytes 122888 | tf_op jit(solution)/shard_map/ppermute | solution.py:471
  29.9 8.1 %collective-permute-start.9 = (f32[10,8,128]{2,1,0:T(8,128)S(1)}, f32[10,8,128]{2,1,0:T(8,128)S(1)}, u32[]{:S(2)}, u32[]{:S(2)}) collective-permute-start(f32[10,8,128]{2,1,0:T(8,128)S(1)} %shift.1), channel_id=1, source_target_pairs={{64,0},{65,1},{66,2},{67,3},{68,4},{69,5},{70,6},{71,7},{72,8},{73... | collective-permute-start | bytes 122888 | tf_op jit(solution)/shard_map/ppermute | solution.py:472
  61.0 5.2 %collective-permute-start.11 = (f32[64,128]{1,0:T(8,128)S(1)}, f32[64,128]{1,0:T(8,128)S(1)}, u32[]{:S(2)}, u32[]{:S(2)}) collective-permute-start(f32[64,128]{1,0:T(8,128)S(1)} %pick.1), channel_id=1, source_target_pairs={{0,64},{64,128},{128,192},{192,0},{1,65},{65,129},{129,193},{193,1... | collective-permute-start | bytes 98312 | tf_op jit(solution)/shard_map/ppermute | solution.py:486
  62.2 5.4 %collective-permute-start.12 = (f32[64,128]{1,0:T(8,128)S(1)}, f32[64,128]{1,0:T(8,128)S(1)}, u32[]{:S(2)}, u32[]{:S(2)}) collective-permute-start(f32[64,128]{1,0:T(8,128)S(1)} %pick.1), channel_id=1, source_target_pairs={{0,128},{64,192},{128,0},{192,64},{1,129},{65,193},{129,1},{193,65... | collective-permute-start | bytes 98312 | tf_op jit(solution)/shard_map/ppermute | solution.py:486
  62.9 4.8 %collective-permute-start.13 = (f32[64,128]{1,0:T(8,128)S(1)}, f32[64,128]{1,0:T(8,128)S(1)}, u32[]{:S(2)}, u32[]{:S(2)}) collective-permute-start(f32[64,128]{1,0:T(8,128)S(1)} %pick.1), channel_id=1, source_target_pairs={{0,192},{64,0},{128,64},{192,128},{1,193},{65,1},{129,65},{193,129... | collective-permute-start | bytes 98312 | tf_op jit(solution)/shard_map/ppermute | solution.py:486

commit v9 on v8

--- a/solution.py
+++ b/solution.py
@@ -85,6 +85,18 @@
         if emit is not None:
             emit(k, b)
     return b, p
+
+
+def split(x):
+    high = x.astype(jnp.bfloat16).astype(F32)
+    return high, x - high
+
+
+def dot_passes(a, b):
+    a_high, a_low = split(a)
+    b_high, b_low = split(b)
+    one = lambda p, q: jnp.dot(p, q, preferred_element_type=F32)
+    return one(a_high, b_high) + (one(a_high, b_low) + one(a_low, b_high))
 
 
 def map_dot(m_ref, base, x):
@@ -368,7 +380,7 @@
     row = lax.broadcasted_iota(jnp.int32, (SLOTS, S), 0)
     lane = lax.broadcasted_iota(jnp.int32, (SLOTS, S), 1)
     prof_ref[NV * H :, :] = (row == lane).astype(F32)
-    rows_ref[...] = jnp.dot(pw_ref[...], prof_ref[...], precision=highest, preferred_element_type=F32)
+    rows_ref[...] = dot_passes(pw_ref[...], prof_ref[...])
 
 
 def place_kernel(count_ref, w_ref, owner_ref, tag_ref, out_ref):
@@ -410,7 +422,10 @@
     tag = jnp.sum(jnp.where(mine, wide, 0.0), axis=0, keepdims=True)
     target = (lax.broadcasted_iota(jnp.int32, (PATCH_DEV, rows), 0) + 1).astype(F32)
     picker = (tag == target).astype(F32)
-    out_ref[...] = jnp.dot(picker, got_ref[...], precision=highest, preferred_element_type=F32)
+    high, rest = split(got_ref[...])
+    middle, low = split(rest)
+    one = lambda q: jnp.dot(picker, q, preferred_element_type=F32)
+    out_ref[...] = one(high) + (one(middle) + one(low))
 
 
 def on_device(

time: 68.6 us -> 68.5 us (level)
  no operation moved by 1% of the time
where the time goes in v9:
time: 68.5 us; the launch traced here: 68.1 us
  starting transfers between devices  20.3 us (30%)
  blocking collectives  20.3 us (30%)
  Pallas kernels  15.3 us (22%)
  waiting for transfers between devices  9.96 us (15%)
  between operations  1.51 us (2%)
  other arithmetic  0.7 us (1%)
    all_to_all x1, blocking collectives, on_device(): lax.all_to_all(rows.reshape(tiles, ROWS_PER_OWNER, 1, S), 'tile', split_a...  20.3 us
    ppermute x1, starting transfers between devices, on_device(): lax.ppermute(lo, 'tile', [((i + 1) % tiles, i) for i in range(tiles)])  5.64 us
    pallas_call x1, Pallas kernels, on_device(): call('start', start_kernel, (block, block, block, state, cell, f32(NV, NV...  5.1 us
    ppermute x1, waiting for transfers between devices, on_device(): y10 = lax.ppermute(y1, 'wall', [(2, 0)])  4.72 us
    ppermute x3, starting transfers between devices, on_device(): lax.ppermute(part, 'wall', [(w, (w + d) % walls) for w in range(walls)])  4.03 us
    ppermute x1, starting transfers between devices, on_device(): x1 = lax.ppermute(up, 'wall', [(0, 1)])  3.29 us
    ppermute x3, waiting for transfers between devices, on_device(): lax.ppermute(part, 'wall', [(w, (w + d) % walls) for w in range(walls)])  2.6 us
    pallas_call x1, Pallas kernels, on_device(): call('finish', finish_kernel, (f32(NV, K, H, S), away(tiles * ROWS_PER_OW...  1.98 us
  transfers between devices with their start and end apart: 14, of which 6 were waited for; matrix products, arithmetic and copies ran while one was open for 0% of the time, Pallas kernels for 17%

profile of v9, /device:TPU:6, one launch (start us, length us, event | category | flops | bytes accessed | tf_op | source)
XLA Modules:
  0.0 68.1 jit_solution(15807606553984096295)
XLA Ops:
  0.6 1.0 %pack.1 = (f32[176,128]{1,0:T(8,128)S(1)}, f32[176,128]{1,0:T(8,128)S(1)}) custom-call(f32[10,8,8,128]{3,2,1,0:T(8,128)} %a_in.1, f32[8,8,128]{2,1,0:T(8,128)} %rad_in.1), custom_call_target="tpu_custom_call" | custom-call | bytes 800000 | tf_op jit(solution)/shard_map/pack/pallas_call | solution.py:445
  1.7 5.6 %collective-permute-start.1 = (f32[176,128]{1,0:T(8,128)S(1)}, f32[176,128]{1,0:T(8,128)S(1)}, u32[]{:S(2)}, u32[]{:S(2)}) collective-permute-start(f32[176,128]{1,0:T(8,128)S(1)} %get-tuple-element.38), channel_id=1, source_target_pairs={{1,0},{2,1},{3,2},{4,3},{5,4},{6,5},{7,6},{8,7},{9,8},{10,9},{11,1... | collective-permute-start | bytes 270344 | tf_op jit(solution)/shard_map/ppermute | solution.py:447
  7.4 5.1 %start.1 = (f32[10,10,8,8,128]{4,3,2,1,0:T(8,128)S(1)}, f32[10,10,8,8,128]{4,3,2,1,0:T(8,128)S(1)}, f32[10,10,8,8,128]{4,3,2,1,0:T(8,128)S(1)}, f32[10,8,8,128]{...) custom-call(s32[3]{0:T(128)S(1)} %pad_add_fusion.pos_ref, ...), custom_call_target="tpu_custom_call" | custom-call | flops 30000000 | bytes 11000000 | tf_op jit(solution)/shard_map/start/pallas_call | solution.py:450
  12.5 0.9 %collective-permute-done.left_ref = f32[176,128]{1,0:T(8,128)S(1)} collective-permute-done((f32[176,128]{1,0:T(8,128)S(1)}, f32[176,128]{1,0:T(8,128)S(1)}, u32[]{:S(2)}, u32[]{:S(2)}) %collective-permute-start) | collective-permute-done | bytes 90144 | tf_op jit(solution)/shard_map/ppermute | solution.py:446
  13.4 0.7 collective-permute-start.5
  14.0 1.0 %residual.1 = (f32[10,8,8,128]{3,2,1,0:T(8,128)S(1)}, f32[10,8,128]{2,1,0:T(8,128)S(1)}, f32[10,8,128]{2,1,0:T(8,128)S(1)}) custom-call(s32[3]{0:T(128)S(1)} %pad_add_fusion.pos_ref, f32[10,8,8,128]{3,2,1,0:T(8,128)S(1)} %get-tuple-element.40.inner_ref, f32[10,8,8,128]{3,2,1,0:T(8,128)S(1)} %get-tuple-element.41.a_ref, ...), custom_call_target="tpu_custom_call" | custom-call | tf_op jit(solution)/shard_map/residual/pallas_call | solution.py:461
  15.1 3.3 %collective-permute-start.2 = (f32[10,8,128]{2,1,0:T(8,128)S(1)}, f32[10,8,128]{2,1,0:T(8,128)S(1)}, u32[]{:S(2)}, u32[]{:S(2)}) collective-permute-start(f32[10,8,128]{2,1,0:T(8,128)S(1)} %get-tuple-element.52), channel_id=1, source_target_pairs={{0,64},{1,65},{2,66},{3,67},{4,68},{5,69},{6,70},{7,71},{8,72},{9,... | collective-permute-start | bytes 122888 | tf_op jit(solution)/shard_map/ppermute | solution.py:464
  18.4 0.6 below.1
  19.0 1.1 %collective-permute-done.2.x_ref.x1_ref = f32[10,8,128]{2,1,0:T(8,128)S(1)} collective-permute-done((f32[10,8,128]{2,1,0:T(8,128)S(1)}, f32[10,8,128]{2,1,0:T(8,128)S(1)}, u32[]{:S(2)}, u32[]{:S(2)}) %collective-permute-start.2) | collective-permute-done | bytes 40992 | tf_op jit(solution)/shard_map/ppermute | solution.py:464
  20.1 1.3 %collective-permute-start.8 = (f32[10,10,8,128]{3,2,1,0:T(8,128)S(1)}, f32[10,10,8,128]{3,2,1,0:T(8,128)S(1)}, u32[]{:S(2)}, u32[]{:S(2)}) collective-permute-start(f32[10,10,8,128]{3,2,1,0:T(8,128)S(1)} %below.1), channel_id=1, source_target_pairs={{64,0},{65,1},{66,2},{67,3},{68,4},{69,5},{70,6},{71,7},{72,8},{73... | collective-permute-start | bytes 1228808 | tf_op jit(solution)/shard_map/ppermute | solution.py:469
  21.9 0.7 collective-permute-start.3
  22.6 0.7 collective-permute-start.4
  23.9 1.4 %place.1.pw_ref = f32[576,88]{1,0:T(8,128)S(1)} custom-call(s32[1]{0:T(128)S(6)} %copy.15.count_ref, f32[80,256]{1,0:T(8,128)S(1)} %bitcast.11, s32[1,256]{1,0:T(1,128)S(1)} %bitcast.12, s32[1,256]{1,0:T(1,128)S(1)} %bitcast.13), custom_call_target="tpu_custom_call" | custom-call | tf_op jit(solution)/shard_map/place/pallas_call | solution.py:475
  25.3 0.6 shift.1
  25.9 0.6 rise.1
  26.5 0.6 decide.1
  27.0 0.7 collective-permute-start.10
  27.7 1.3 %collective-permute-start.6 = (f32[10,8,128]{2,1,0:T(8,128)S(1)}, f32[10,8,128]{2,1,0:T(8,128)S(1)}, u32[]{:S(2)}, u32[]{:S(2)}) collective-permute-start(f32[10,8,128]{2,1,0:T(8,128)S(1)} %get-tuple-element.66), channel_id=1, source_target_pairs={{128,0},{129,1},{130,2},{131,3},{132,4},{133,5},{134,6},{135,7},{1... | collective-permute-start | bytes 122888 | tf_op jit(solution)/shard_map/ppermute | solution.py:485
  29.0 0.8 %collective-permute-start.7 = (f32[10,8,128]{2,1,0:T(8,128)S(1)}, f32[10,8,128]{2,1,0:T(8,128)S(1)}, u32[]{:S(2)}, u32[]{:S(2)}) collective-permute-start(f32[10,8,128]{2,1,0:T(8,128)S(1)} %get-tuple-element.66), channel_id=1, source_target_pairs={{128,64},{129,65},{130,66},{131,67},{132,68},{133,69},{134,70},{13... | collective-permute-start | bytes 122888 | tf_op jit(solution)/shard_map/ppermute | solution.py:486
  29.9 1.3 %collective-permute-start.9 = (f32[10,8,128]{2,1,0:T(8,128)S(1)}, f32[10,8,128]{2,1,0:T(8,128)S(1)}, u32[]{:S(2)}, u32[]{:S(2)}) collective-permute-start(f32[10,8,128]{2,1,0:T(8,128)S(1)} %shift.1), channel_id=1, source_target_pairs={{64,0},{65,1},{66,2},{67,3},{68,4},{69,5},{70,6},{71,7},{72,8},{73... | collective-permute-start | bytes 122888 | tf_op jit(solution)/shard_map/ppermute | solution.py:487
  31.2 1.4 %scale.1.s_ref = f32[8,10,8,128]{3,2,1,0:T(8,128)S(1)} custom-call(s32[3]{0:T(128)S(1)} %pad_add_fusion.pos_ref, f32[10,8,128]{2,1,0:T(8,128)S(1)} %collective-permute-done.2.x_ref.x1_ref, f32[10,8,128]{2,1,0:T(8,128)S(1)} %collective-permute-done.10.x3_ref, f32[8,10,8,128]{3,2,1,0:T(8,128)S(1)} %get-tuple-element.61.s_ref.s2_ref, ...), custom_call_target="tpu_custom_call" | custom-call | tf_op jit(solution)/shard_map/scale/pallas_call | solution.py:488
  32.6 4.7 %collective-permute-done.6.y10_ref = f32[10,8,128]{2,1,0:T(8,128)S(1)} collective-permute-done((f32[10,8,128]{2,1,0:T(8,128)S(1)}, f32[10,8,128]{2,1,0:T(8,128)S(1)}, u32[]{:S(2)}, u32[]{:S(2)}) %collective-permute-start.6) | collective-permute-done | bytes 40992 | tf_op jit(solution)/shard_map/ppermute | solution.py:485
  37.3 0.7 collective-permute-done.9.shift_ref
  38.0 2.0 %finish.1 = (f32[10,8,8,128]{3,2,1,0:T(8,128)}, f32[576,128]{1,0:T(8,128)}) custom-call(s32[3]{0:T(128)S(1)} %pad_add_fusion.pos_ref, f32[10,8,128]{2,1,0:T(8,128)S(1)} %get-tuple-element.62.y2_ref, f32[10,8,128]{2,1,0:T(8,128)S(1)} %collective-permute-done.6.y10_ref, f32[10,8,128]{2,1,0:T(8,128)S(1)} %collective-permute-done.7.y1_ref, ...), custom_call_target="tpu_custom_call" | custom-call | tf_op jit(solution)/shard_map/finish/pallas_call | solution.py:491
  39.9 20.3 %all_to_all.5 = f32[64,9,1,128]{3,2,1,0:T(1,128)S(1)} all-to-all(f32[64,9,1,128]{3,2,1,0:T(1,128)} %bitcast.14), channel_id=1, replica_groups=mesh['wall'=4,'tile'=64] {'tile'}, dimensions={0} | all-to-all | bytes 589824 | tf_op jit(solution)/shard_map/all_to_all | solution.py:495
  60.2 0.6 pick.1
  60.9 1.2 %collective-permute-start.11 = (f32[64,128]{1,0:T(8,128)S(1)}, f32[64,128]{1,0:T(8,128)S(1)}, u32[]{:S(2)}, u32[]{:S(2)}) collective-permute-start(f32[64,128]{1,0:T(8,128)S(1)} %pick.1), channel_id=1, source_target_pairs={{0,64},{64,128},{128,192},{192,0},{1,65},{65,129},{129,193},{193,1... | collective-permute-start | bytes 98312 | tf_op jit(solution)/shard_map/ppermute | solution.py:501
  62.1 0.6 collective-permute-start.12
  62.7 2.2 %collective-permute-start.13 = (f32[64,128]{1,0:T(8,128)S(1)}, f32[64,128]{1,0:T(8,128)S(1)}, u32[]{:S(2)}, u32[]{:S(2)}) collective-permute-start(f32[64,128]{1,0:T(8,128)S(1)} %pick.1), channel_id=1, source_target_pairs={{0,192},{64,0},{128,64},{192,128},{1,193},{65,1},{129,65},{193,129... | collective-permute-start | bytes 98312 | tf_op jit(solution)/shard_map/ppermute | solution.py:501
  64.9 1.2 %collective-permute-done.11 = f32[64,128]{1,0:T(8,128)S(1)} collective-permute-done((f32[64,128]{1,0:T(8,128)S(1)}, f32[64,128]{1,0:T(8,128)S(1)}, u32[]{:S(2)}, u32[]{:S(2)}) %collective-permute-start.11) | collective-permute-done | bytes 32800 | tf_op jit(solution)/shard_map/ppermute | solution.py:501
  66.1 1.4 %collective-permute-done.12 = f32[64,128]{1,0:T(8,128)S(1)} collective-permute-done((f32[64,128]{1,0:T(8,128)S(1)}, f32[64,128]{1,0:T(8,128)S(1)}, u32[]{:S(2)}, u32[]{:S(2)}) %collective-permute-start.12) | collective-permute-done | bytes 32800 | tf_op jit(solution)/shard_map/ppermute | solution.py:501
  67.5 0.6 add_add_fusion
  (17 shorter events, 0.7 us)
Async XLA Ops:
  1.7 10.8 %collective-permute-start.1 = (f32[176,128]{1,0:T(8,128)S(1)}, f32[176,128]{1,0:T(8,128)S(1)}, u32[]{:S(2)}, u32[]{:S(2)}) collective-permute-start(f32[176,128]{1,0:T(8,128)S(1)} %get-tuple-element.38), channel_id=1, source_target_pairs={{1,0},{2,1},{3,2},{4,3},{5,4},{6,5},{7,6},{8,7},{9,8},{10,9},{11,1... | collective-permute-start | bytes 270344 | tf_op jit(solution)/shard_map/ppermute | solution.py:447
  7.3 6.1 %collective-permute-start = (f32[176,128]{1,0:T(8,128)S(1)}, f32[176,128]{1,0:T(8,128)S(1)}, u32[]{:S(2)}, u32[]{:S(2)}) collective-permute-start(f32[176,128]{1,0:T(8,128)S(1)} %get-tuple-element.45), channel_id=1, source_target_pairs={{0,1},{1,2},{2,3},{3,4},{4,5},{5,6},{6,7},{7,8},{8,9},{9,10},{10,1... | collective-permute-start | bytes 270344 | tf_op jit(solution)/shard_map/ppermute | solution.py:446
  13.4 13.1 %collective-permute-start.5 = (f32[10,10,8,128]{3,2,1,0:T(8,128)S(1)}, f32[10,10,8,128]{3,2,1,0:T(8,128)S(1)}, u32[]{:S(2)}, u32[]{:S(2)}) collective-permute-start(f32[10,10,8,128]{3,2,1,0:T(8,128)S(1)} %get-tuple-element.60), channel_id=1, source_target_pairs={{192,128},{193,129},{194,130},{195,131},{196,132},{197,133},{198,1... | collective-permute-start | bytes 1228808 | tf_op jit(solution)/shard_map/ppermute | solution.py:460
  15.1 8.8 %copy-start = (f32[256,10,8]{0,2,1:T(8,128)S(1)}, f32[256,10,8]{0,2,1:T(8,128)}, u32[]{:S(2)}) copy-start(f32[256,10,8]{0,2,1:T(8,128)} %param.20) | copy-start | bytes 245764
  15.1 8.8 %copy-start.1 = (s32[256,1]{0,1:T(1,128)S(1)}, s32[256,1]{0,1:T(1,128)}, u32[]{:S(2)}) copy-start(s32[256,1]{0,1:T(1,128)} %param.21) | copy-start | bytes 3076
  15.1 8.8 %copy-start.2 = (s32[256]{0:T(256)S(1)}, s32[256]{0:T(256)}, u32[]{:S(2)}) copy-start(s32[256]{0:T(256)} %param.22) | copy-start | bytes 3076
  15.1 4.9 %collective-permute-start.2 = (f32[10,8,128]{2,1,0:T(8,128)S(1)}, f32[10,8,128]{2,1,0:T(8,128)S(1)}, u32[]{:S(2)}, u32[]{:S(2)}) collective-permute-start(f32[10,8,128]{2,1,0:T(8,128)S(1)} %get-tuple-element.52), channel_id=1, source_target_pairs={{0,64},{1,65},{2,66},{3,67},{4,68},{5,69},{6,70},{7,71},{8,72},{9,... | collective-permute-start | bytes 122888 | tf_op jit(solution)/shard_map/ppermute | solution.py:464
  20.1 17.9 %collective-permute-start.8 = (f32[10,10,8,128]{3,2,1,0:T(8,128)S(1)}, f32[10,10,8,128]{3,2,1,0:T(8,128)S(1)}, u32[]{:S(2)}, u32[]{:S(2)}) collective-permute-start(f32[10,10,8,128]{3,2,1,0:T(8,128)S(1)} %below.1), channel_id=1, source_target_pairs={{64,0},{65,1},{66,2},{67,3},{68,4},{69,5},{70,6},{71,7},{72,8},{73... | collective-permute-start | bytes 1228808 | tf_op jit(solution)/shard_map/ppermute | solution.py:469
  21.9 4.0 %collective-permute-start.3 = (f32[10,8,128]{2,1,0:T(8,128)S(1)}, f32[10,8,128]{2,1,0:T(8,128)S(1)}, u32[]{:S(2)}, u32[]{:S(2)}) collective-permute-start(f32[10,8,128]{2,1,0:T(8,128)S(1)} %middle.1), channel_id=1, source_target_pairs={{64,128},{65,129},{66,130},{67,131},{68,132},{69,133},{70,134},{71... | collective-permute-start | bytes 122888 | tf_op jit(solution)/shard_map/ppermute | solution.py:472
  22.6 3.9 %collective-permute-start.4 = (f32[10,8,128]{2,1,0:T(8,128)S(1)}, f32[10,8,128]{2,1,0:T(8,128)S(1)}, u32[]{:S(2)}, u32[]{:S(2)}) collective-permute-start(f32[10,8,128]{2,1,0:T(8,128)S(1)} %get-tuple-element.59), channel_id=1, source_target_pairs={{192,128},{193,129},{194,130},{195,131},{196,132},{197,133},{198,1... | collective-permute-start | bytes 122888 | tf_op jit(solution)/shard_map/ppermute | solution.py:465
  27.0 4.1 %collective-permute-start.10 = (f32[10,8,128]{2,1,0:T(8,128)S(1)}, f32[10,8,128]{2,1,0:T(8,128)S(1)}, u32[]{:S(2)}, u32[]{:S(2)}) collective-permute-start(f32[10,8,128]{2,1,0:T(8,128)S(1)} %get-tuple-element.71.x3_ref), channel_id=1, source_target_pairs={{128,192},{129,193},{130,194},{131,195},{132,196},{133,197},{134,1... | collective-permute-start | bytes 122888 | tf_op jit(solution)/shard_map/ppermute | solution.py:484
  27.7 9.6 %collective-permute-start.6 = (f32[10,8,128]{2,1,0:T(8,128)S(1)}, f32[10,8,128]{2,1,0:T(8,128)S(1)}, u32[]{:S(2)}, u32[]{:S(2)}) collective-permute-start(f32[10,8,128]{2,1,0:T(8,128)S(1)} %get-tuple-element.66), channel_id=1, source_target_pairs={{128,0},{129,1},{130,2},{131,3},{132,4},{133,5},{134,6},{135,7},{1... | collective-permute-start | bytes 122888 | tf_op jit(solution)/shard_map/ppermute | solution.py:485
  29.0 8.3 %collective-permute-start.7 = (f32[10,8,128]{2,1,0:T(8,128)S(1)}, f32[10,8,128]{2,1,0:T(8,128)S(1)}, u32[]{:S(2)}, u32[]{:S(2)}) collective-permute-start(f32[10,8,128]{2,1,0:T(8,128)S(1)} %get-tuple-element.66), channel_id=1, source_target_pairs={{128,64},{129,65},{130,66},{131,67},{132,68},{133,69},{134,70},{13... | collective-permute-start | bytes 122888 | tf_op jit(solution)/shard_map/ppermute | solution.py:486
  29.9 8.1 %collective-permute-start.9 = (f32[10,8,128]{2,1,0:T(8,128)S(1)}, f32[10,8,128]{2,1,0:T(8,128)S(1)}, u32[]{:S(2)}, u32[]{:S(2)}) collective-permute-start(f32[10,8,128]{2,1,0:T(8,128)S(1)} %shift.1), channel_id=1, source_target_pairs={{64,0},{65,1},{66,2},{67,3},{68,4},{69,5},{70,6},{71,7},{72,8},{73... | collective-permute-start | bytes 122888 | tf_op jit(solution)/shard_map/ppermute | solution.py:487
  60.9 5.2 %collective-permute-start.11 = (f32[64,128]{1,0:T(8,128)S(1)}, f32[64,128]{1,0:T(8,128)S(1)}, u32[]{:S(2)}, u32[]{:S(2)}) collective-permute-start(f32[64,128]{1,0:T(8,128)S(1)} %pick.1), channel_id=1, source_target_pairs={{0,64},{64,128},{128,192},{192,0},{1,65},{65,129},{129,193},{193,1... | collective-permute-start | bytes 98312 | tf_op jit(solution)/shard_map/ppermute | solution.py:501
  62.1 5.4 %collective-permute-start.12 = (f32[64,128]{1,0:T(8,128)S(1)}, f32[64,128]{1,0:T(8,128)S(1)}, u32[]{:S(2)}, u32[]{:S(2)}) collective-permute-start(f32[64,128]{1,0:T(8,128)S(1)} %pick.1), channel_id=1, source_target_pairs={{0,128},{64,192},{128,0},{192,64},{1,129},{65,193},{129,1},{193,65... | collective-permute-start | bytes 98312 | tf_op jit(solution)/shard_map/ppermute | solution.py:501
  62.7 4.8 %collective-permute-start.13 = (f32[64,128]{1,0:T(8,128)S(1)}, f32[64,128]{1,0:T(8,128)S(1)}, u32[]{:S(2)}, u32[]{:S(2)}) collective-permute-start(f32[64,128]{1,0:T(8,128)S(1)} %pick.1), channel_id=1, source_target_pairs={{0,192},{64,0},{128,64},{192,128},{1,193},{65,1},{129,65},{193,129... | collective-permute-start | bytes 98312 | tf_op jit(solution)/shard_map/ppermute | solution.py:501
